TPU v7x, 32 devices: a whole 2x2x4 slice. The times are simulated.
32 devices in a mesh: lat: 1, lon: 32 (over z, y, x, core).
Axes of the slice: x: 2, y: 2, z: 4, core: 2. Of those that a mesh axis runs over, the one named last changes fastest.
Arguments:
- fields: bfloat16 [2, 24, 768, 256], P(None, 'lat', 'lon'), may hold values from -6 to 6
- legendre: float32 [24, 192, 8], P('lat', 'lon'), may hold values from -1.25 to 1.25
- mixing: bfloat16 [8, 256, 256], P('lat'), may hold values from -0.375 to 0.375
- cotangent: bfloat16 [8, 192, 2, 2, 256], P('lat', 'lon'), may hold values from -0.3046875 to 0.3046875
Outputs:
- mixed: bfloat16 [8, 192, 2, 2, 256], P('lat', 'lon')
- weight_grad: float32 [256, 8, 256], P('lon', 'lat')
All inputs are finite; a program needn't handle non-finite values.
Results may differ from a plain program's by a relative error of at most 0.015.
Values may be sent and summed in bfloat16 or wider, within the bound.
No kernel may reach another device: no remote copies, remote signals or barrier semaphores. Data moves between devices by JAX's collectives and lax.ppermute only.
A program may use at most 64 MiB of HBM per device.

v0:
```python
import math

import jax
import jax.numpy as jnp
from jax import lax
from jax.sharding import PartitionSpec as P


def shards(fields, legendre, mixing, cotangent):
    samples = fields.shape[0]
    lat_rows = fields.shape[1]
    lon_cells = fields.shape[2]
    channels = fields.shape[3]
    lon_count = lax.axis_size("lon")
    lat_count = lax.axis_size("lat")
    nlon_total = lon_cells * lon_count
    wave_dev = legendre.shape[1]
    wave_total = wave_dev * lon_count
    degrees = legendre.shape[2]
    degree_dev = degrees // lat_count
    column_rows = 2 * wave_dev * samples
    column_width = 2 * samples * channels
    positions = jnp.arange(nlon_total, dtype=jnp.int32)
    wavenums = jnp.arange(wave_total, dtype=jnp.int32)
    phase = (positions[:, None] * wavenums[None, :] % nlon_total).astype(jnp.float32) * (
        2.0 * math.pi / nlon_total
    )
    fourier = jnp.stack([jnp.cos(phase), -jnp.sin(phase)], axis=2).reshape(
        nlon_total, 2 * wave_total
    )
    fourier = fourier * (1.0 / nlon_total**0.5)
    fourier_hi = fourier.astype(jnp.bfloat16)
    fourier_lo = (fourier - fourier_hi.astype(jnp.float32)).astype(jnp.bfloat16)
    portion = lax.all_to_all(fields, "lon", split_axis=3, concat_axis=2, tiled=True)
    spectrum = jnp.einsum("bjkc,kf->jfbc", portion, fourier_hi, preferred_element_type=jnp.float32)
    spectrum = spectrum + jnp.einsum(
        "bjkc,kf->jfbc", portion, fourier_lo, preferred_element_type=jnp.float32
    )
    owned = lax.all_to_all(spectrum, "lon", split_axis=1, concat_axis=3, tiled=True)
    spectral = owned.reshape(owned.shape[0], column_rows, channels)
    wave_global = lax.axis_index("lon") * wave_dev + jnp.arange(wave_dev, dtype=jnp.int32)
    degree_ids = jnp.arange(degrees, dtype=jnp.int32)
    keep = degree_ids[None, None, :] >= wave_global[None, :, None]
    basis = jnp.where(keep, legendre, jnp.float32(0.0))
    spectral_waves = spectral.reshape(lat_rows, wave_dev, column_width)
    summed = lax.psum_scatter(
        jnp.einsum("jml,jmq->lmq", basis, spectral_waves, precision=lax.Precision.HIGHEST),
        "lat",
        scatter_dimension=0,
        tiled=True,
    )
    coef = summed.reshape(degree_dev, column_rows, channels)
    coef_bf = coef.astype(jnp.bfloat16)
    mixed = jnp.einsum("lrc,lcd->lrd", coef_bf, mixing, preferred_element_type=jnp.float32)
    mixed = mixed.astype(jnp.bfloat16).reshape(degree_dev, wave_dev, 2, samples, channels)
    cot_rows = cotangent.reshape(degree_dev, column_rows, channels)
    weight_grad = lax.psum_scatter(
        jnp.einsum("lrc,lrd->cld", coef_bf, cot_rows, preferred_element_type=jnp.float32),
        "lon",
        scatter_dimension=0,
        tiled=True,
    )
    return (mixed, weight_grad)


def solution(mesh):
    placed = (
        P(None, "lat", "lon", None),
        P("lat", "lon", None),
        P("lat", None, None),
        P("lat", "lon", None, None, None),
    )
    return jax.shard_map(
        shards,
        mesh=mesh,
        in_specs=placed,
        out_specs=(P("lat", "lon", None, None, None), P("lon", "lat", None)),
        check_vma=False,
    )
```

profile of v0, /device:TPU:0, one launch (start us, length us, event | category | flops | bytes accessed | tf_op | source)
XLA Modules:
  0.0 244.5 jit_solution(11056926571188096367)
XLA Ops:
  7.2 5.0 %copy.32 = bf16[2,24,24,256]{2,1,0,3:T(8,128)(2,1)} copy(bf16[2,24,24,256]{3,2,1,0:T(8,128)(2,1)} %param.4) | data formatting | bytes 1179648 | tf_op args[0]
  12.1 6.4 %reshape.116 = bf16[32,2,4608]{2,1,0:T(2,128)(2,1)} reshape(bf16[256,2,24,24]{3,2,1,0:T(8,128)(2,1)} %bitcast.42) | data formatting | bytes 1179648
  18.5 7.5 %all-to-all-start = ((bf16[32,2,4608]{2,1,0:T(2,128)(2,1)}), bf16[32,2,4608]{2,1,0:T(2,128)(2,1)S(1)}, u32[]{:S(2)}, u32[]{:S(2)}) async-start(bf16[32,2,4608]{2,1,0:T(2,128)(2,1)} %reshape.116), calls=%async_computation | async-start | bytes 1179648 | tf_op jit(solution)/shard_map/all_to_all | solution.py:34
  26.0 2.4 sine_negate_fusion
  28.4 0.2 subtract_convert_fusion
  28.6 0.6 copy.31
  29.2 0.2 convert_element_type.71
  29.4 0.6 copy.37
  30.1 0.2 convert_element_type.74
  30.3 12.3 %all-to-all-done = bf16[32,2,4608]{2,1,0:T(2,128)(2,1)S(1)} async-done(((bf16[32,2,4608]{2,1,0:T(2,128)(2,1)}), bf16[32,2,4608]{2,1,0:T(2,128)(2,1)S(1)}, u32[]{:S(2)}, u32[]{:S(2)}) %all-to-all-start) | async-done | bytes 589856 | tf_op jit(solution)/shard_map/all_to_all | solution.py:34
  42.6 5.7 %reshape.117 = bf16[256,2,24,24]{3,2,1,0:T(8,128)(2,1)} reshape(bf16[32,2,4608]{2,1,0:T(2,128)(2,1)S(1)} %all-to-all-done) | data formatting | bytes 1179648
  48.2 5.6 %copy.51 = bf16[2,24,32,24,8]{3,2,1,4,0:T(8,128)(2,1)} copy(bf16[2,24,32,24,8]{3,1,0,4,2:T(8,128)(2,1)} %bitcast.39) | data formatting | bytes 1179648 | tf_op jit(solution)/shard_map/all_to_all | solution.py:34
  53.8 5.3 %reshape.115 = bf16[2,24,768,8]{2,1,3,0:T(8,128)(2,1)S(1)} reshape(bf16[2,24,32,24,8]{3,2,1,4,0:T(8,128)(2,1)} %copy.51) | data formatting | bytes 1179648 | tf_op jit(solution)/shard_map/all_to_all | solution.py:34
  59.1 0.5 fusion.6
  59.6 0.5 fusion
  60.1 2.2 copy.40
  62.3 4.6 %reshape.118 = f32[32,1,4608]{2,1,0:T(1,128)} reshape(f32[384,2,8,24]{3,2,1,0:T(8,128)} %bitcast.40) | data formatting | bytes 1179648
  66.9 3.3 %all-to-all-start.1 = ((f32[32,1,4608]{2,1,0:T(1,128)}), f32[32,1,4608]{2,1,0:T(1,128)S(1)}, u32[]{:S(2)}, u32[]{:S(2)}) async-start(f32[32,1,4608]{2,1,0:T(1,128)} %reshape.118), calls=%async_computation.1 | async-start | bytes 1179648 | tf_op jit(solution)/shard_map/all_to_all | solution.py:39
  70.4 0.1 iota_compare_fusion
  70.4 16.5 %all-to-all-done.1 = f32[32,1,4608]{2,1,0:T(1,128)S(1)} async-done(((f32[32,1,4608]{2,1,0:T(1,128)}), f32[32,1,4608]{2,1,0:T(1,128)S(1)}, u32[]{:S(2)}, u32[]{:S(2)}) %all-to-all-start.1) | async-done | bytes 589856 | tf_op jit(solution)/shard_map/all_to_all | solution.py:39
  87.0 0.5 broadcast.99
  87.5 2.0 reduce
  89.5 3.9 %reshape.119 = f32[384,2,8,24]{3,2,1,0:T(8,128)} reshape(f32[32,4608]{1,0:T(8,128)S(1)} %reduce) | data formatting | bytes 1179648
  93.4 2.2 copy.41
  95.7 2.8 %fusion.1 = bf16[8,6,1024]{2,0,1:T(8,128)(2,1)S(1)} fusion(f32[24,6,1024]{0,2,1:T(8,128)S(1)} %bitcast.38, f32[24,6,8]{0,2,1:T(8,128)S(1)} %copy-done.2, pred[6,8]{1,0:T(8,128)(4,1)S(1)} %iota_compare_fusion), kind=kOutput, calls=%fused_computation.7 | convolution fusion | flops 14206080 | bytes 692784 | tf_op jit(solution)/shard_map/jml,jmq->lmq/dot_general | solution.py:47
  98.5 0.1 copy.43
  98.6 0.1 convert_element_type.77
  98.7 1.8 convolution_bitcast_fusion
  100.6 0.2 convolution_convert_fusion
  100.8 0.7 reshape.111
  101.5 134.6 %reduce-scatter.2.cloned.1.call-done = f32[8,8,256]{2,0,1:T(8,128)} async-done(((f32[256,8,256]{2,0,1:T(8,128)}), f32[8,8,256]{2,0,1:T(8,128)}) %reduce-scatter.2.cloned.1.call-update) | async-done | bytes 65552 | tf_op jit(solution)/shard_map/reduce_scatter | solution.py:57
  236.1 1.5 copy.44
  (10 shorter events, 0.1 us)
Async XLA Ops:
  7.2 93.4 %copy-start = (bf16[8,256,256]{2,1,0:T(8,128)(2,1)S(1)}, bf16[8,256,256]{2,1,0:T(8,128)(2,1)}, u32[]{:S(2)}) copy-start(bf16[8,256,256]{2,1,0:T(8,128)(2,1)} %param.6) | copy-start | bytes 3145732
  18.5 24.0 %all-to-all-start = ((bf16[32,2,4608]{2,1,0:T(2,128)(2,1)}), bf16[32,2,4608]{2,1,0:T(2,128)(2,1)S(1)}, u32[]{:S(2)}, u32[]{:S(2)}) async-start(bf16[32,2,4608]{2,1,0:T(2,128)(2,1)} %reshape.116), calls=%async_computation | async-start | bytes 1179648 | tf_op jit(solution)/shard_map/all_to_all | solution.py:34
  62.3 8.0 %copy-start.1 = (bf16[8,6,2,2,256]{4,3,2,1,0:T(2,128)(2,1)S(1)}, bf16[8,6,2,2,256]{4,3,2,1,0:T(2,128)(2,1)}, u32[]{:S(2)}) copy-start(bf16[8,6,2,2,256]{4,3,2,1,0:T(2,128)(2,1)} %param.7) | copy-start | bytes 294916
  66.9 20.0 %all-to-all-start.1 = ((f32[32,1,4608]{2,1,0:T(1,128)}), f32[32,1,4608]{2,1,0:T(1,128)S(1)}, u32[]{:S(2)}, u32[]{:S(2)}) async-start(f32[32,1,4608]{2,1,0:T(1,128)} %reshape.118), calls=%async_computation.1 | async-start | bytes 1179648 | tf_op jit(solution)/shard_map/all_to_all | solution.py:39
  70.2 165.9 %reduce-scatter.2.cloned.1.call-start = ((), (), s32[]{:S(2)}) async-start(), calls=%async_computation.3 | async-start | bytes 2162688 | tf_op jit(solution)/shard_map/reduce_scatter | solution.py:57
  93.4 2.3 copy-start.2
Sparse Core Ops, SparseCore 0:
  100.7 135.3 reduce-scatter.1
where the time goes:
time: 245 us; the launch traced here: 244 us
  waiting for transfers between devices  163 us (67%)
  local copies, waits for them, and re-layouts  45.4 us (19%)
  between operations  14.2 us (6%)
  starting transfers between devices  10.8 us (4%)
  matrix products  5.92 us (2%)
  other arithmetic  4.67 us (2%)
    reduce_scatter x1, waiting for transfers between devices, shards(): lax.psum_scatter(jnp.einsum('lrc,lrd->cld', coef_bf, cot_rows, preferred_...  135 us
    unnamed x12, local copies, waits for them, and re-layouts  27 us
    all_to_all x1, waiting for transfers between devices, shards(): lax.all_to_all(spectrum, 'lon', split_axis=1, concat_axis=3, tiled=True)  16.5 us
    all_to_all x1, waiting for transfers between devices, shards(): lax.all_to_all(fields, 'lon', split_axis=3, concat_axis=2, tiled=True)  12.3 us
    all_to_all x2, local copies, waits for them, and re-layouts, shards(): lax.all_to_all(fields, 'lon', split_axis=3, concat_axis=2, tiled=True)  10.9 us
    all_to_all x1, starting transfers between devices, shards(): lax.all_to_all(fields, 'lon', split_axis=3, concat_axis=2, tiled=True)  7.48 us
  transfers between devices with their start and end apart: 3, of which 3 were waited for; matrix products, arithmetic and copies ran while one was open for 2% of the time, Pallas kernels for 0%

commit v1 on v0

--- a/solution.py
+++ b/solution.py
@@ -1,12 +1,21 @@
+import functools
 import math
 
 import jax
 import jax.numpy as jnp
 from jax import lax
+from jax.experimental import pallas as pl
+from jax.experimental.pallas import tpu as pltpu
 from jax.sharding import PartitionSpec as P
 
-
-def shards(fields, legendre, mixing, cotangent):
+F32 = jnp.float32
+BF16 = jnp.bfloat16
+TILE = 8
+LANES = 128
+VMEM_BYTES = 32 * 1024 * 1024
+
+
+def dense_shards(fields, legendre, mixing, cotangent):
     samples = fields.shape[0]
     lat_rows = fields.shape[1]
     lon_cells = fields.shape[2]
@@ -63,6 +72,257 @@
     return (mixed, weight_grad)
 
 
+def put_rows(ref, first, stride, block):
+    for lane in range(ref.shape[0]):
+        piece = block[:, lane * LANES : (lane + 1) * LANES]
+        ref[lane, pl.ds(first, block.shape[0], stride=stride), :] = piece
+
+
+def take_rows(ref, first, count):
+    return jnp.concatenate([ref[lane, pl.ds(first, count), :] for lane in range(ref.shape[0])], axis=1)
+
+
+def fourier_kernel(nlon_total, where_ref, fields_ref, keep_ref, send_ref, total_ref):
+    rows, cells, _ = fields_ref.shape[1:]
+    parts = keep_ref.shape[0] // rows
+    index = where_ref[0]
+    width = TILE * cells
+    column = lax.broadcasted_iota(jnp.int32, (parts, width), 1)
+    part = lax.broadcasted_iota(jnp.int32, (parts, width), 0)
+    cell = index * cells + lax.rem(column, cells)
+    turn = lax.rem(cell * (part // 2) + lax.rem(part, 2) * (nlon_total // 4), nlon_total)
+    wave = jnp.cos(turn.astype(F32) * (2.0 * math.pi / nlon_total)) * (1.0 / nlon_total**0.5)
+    spread = (parts, TILE, width)
+    own_row = (
+        lax.broadcasted_iota(jnp.int32, spread, 2) // cells
+        == lax.broadcasted_iota(jnp.int32, spread, 1)
+    )
+    wave = jnp.where(own_row, jnp.broadcast_to(wave[:, None, :], spread), 0.0)
+    wave = wave.reshape(parts * TILE, width)
+    wave_hi = wave.astype(BF16)
+    wave_lo = (wave - wave_hi.astype(F32)).astype(BF16)
+    core = lax.rem(index, 2)
+    for out_ref, sample in ((send_ref, 1 - core), (keep_ref, core)):
+        for first in range(0, rows, TILE):
+            grid = fields_ref[sample, pl.ds(first, TILE)]
+            grid = grid.astype(F32).reshape(width, grid.shape[2]).astype(BF16)
+            sums = jnp.dot(wave_hi, grid, preferred_element_type=F32)
+            sums = sums + jnp.dot(wave_lo, grid, preferred_element_type=F32)
+            total_ref[:, pl.ds(first, TILE), :] = sums.reshape(parts, TILE, sums.shape[1])
+        whole = total_ref[...].reshape(out_ref.shape)
+        out_ref[...] = whole.astype(out_ref.dtype)
+
+
+def legendre_kernel(rows, degrees, acc_ref, got_ref, out_ref, coef_ref):
+    parts = 2 * degrees
+    spec_rows = parts * rows
+    cot_rows = out_ref.shape[0] - parts * degrees
+    table_at = spec_rows + cot_rows
+    table = acc_ref[pl.ds(table_at, acc_ref.shape[0] - table_at), :]
+    table = table + got_ref[pl.ds(table_at, acc_ref.shape[0] - table_at), :].astype(F32)
+    half = degrees // 2
+    degree = lax.broadcasted_iota(jnp.int32, (degrees, rows), 0)
+    for wave in range(degrees):
+        at, lane = (wave % half) * degrees, (wave // half) * LANES
+        block = table[at : at + degrees, lane : lane + LANES]
+        basis = block[:, :rows] + block[:, rows : 2 * rows] + block[:, 2 * rows : 3 * rows]
+        basis = jnp.where(degree >= wave, basis, 0.0)
+        for part in (2 * wave, 2 * wave + 1):
+            here = pl.ds(part * rows, rows)
+            spec = acc_ref[here, :] + got_ref[here, :].astype(F32)
+            sums = jnp.dot(
+                basis, spec, preferred_element_type=F32, precision=lax.Precision.HIGHEST
+            )
+            put_rows(coef_ref, part, parts, sums)
+    out_ref[pl.ds(0, parts * degrees), :] = take_rows(coef_ref, 0, parts * degrees).astype(BF16)
+    here = pl.ds(spec_rows, cot_rows)
+    there = pl.ds(parts * degrees, cot_rows)
+    out_ref[there, :] = (acc_ref[here, :] + got_ref[here, :].astype(F32)).astype(BF16)
+
+
+def mixing_kernel(
+    wave_dev, samples, where_ref, mine_ref, other_ref, mixing_ref, mixed_ref, grad_ref, coef_ref, cot_ref
+):
+    degrees, channels = mixing_ref.shape[:2]
+    parts = 2 * degrees
+    coef_rows = parts * degrees
+    per_degree = parts * samples
+    index = where_ref[0]
+    core = lax.rem(index, 2)
+    terms = coef_rows * samples
+    spare = coef_ref.shape[1] - terms
+    put_rows(coef_ref, terms, 1, jnp.zeros((spare, channels), F32))
+    mine, other = mine_ref[...].astype(F32), other_ref[...].astype(F32)
+    for sample in range(samples):
+        held = jnp.where(core == sample, mine, other)
+        put_rows(coef_ref, sample, samples, held[:coef_rows])
+        for group in range(degrees // 2 + 1):
+            for part in range(2):
+                at = coef_rows + (2 * group + part) * degrees
+                block = held[at : at + degrees]
+                row = (2 * group + part) * samples + sample
+                put_rows(cot_ref, row, per_degree, block)
+                if 0 < group < degrees - group:
+                    row = (2 * (degrees - group) + part) * samples + sample
+                    turned = pltpu.roll(block, degrees - group, 0)
+                    put_rows(cot_ref, row, per_degree, turned)
+
+    block_rows = 2 * wave_dev * samples
+    offset = index * block_rows
+    last = (per_degree - 1) // block_rows * block_rows
+    start = jnp.minimum(offset, last)
+    inside = lax.broadcasted_iota(jnp.int32, (block_rows, channels), 0) + offset < per_degree
+    for degree in range(degrees):
+        first = pl.multiple_of(degree * per_degree + start, TILE)
+        block = jnp.where(inside, take_rows(coef_ref, first, block_rows), 0.0).astype(BF16)
+        mixed = jnp.dot(block, mixing_ref[degree], preferred_element_type=F32)
+        mixed_ref[degree] = mixed.astype(BF16)
+
+    own = grad_ref.shape[0]
+    channel = lax.broadcasted_iota(jnp.int32, (own, channels), 1)
+    row = lax.broadcasted_iota(jnp.int32, (own, channels), 0)
+    pick = jnp.where(channel == index * own + row, 1.0, 0.0).astype(BF16)
+    coef = take_rows(coef_ref, 0, terms).astype(BF16)
+    turned = lax.dot_general(
+        pick, coef, (((1,), (1,)), ((), ())), preferred_element_type=F32
+    )
+    spread = (own, degrees, terms)
+    of_degree = (
+        lax.broadcasted_iota(jnp.int32, spread, 2) // per_degree
+        == lax.broadcasted_iota(jnp.int32, spread, 1)
+    )
+    turned = jnp.where(of_degree, jnp.broadcast_to(turned[:, None, :], spread), 0.0)
+    turned = turned.reshape(own * degrees, terms).astype(BF16)
+    grad = jnp.dot(turned, take_rows(cot_ref, 0, terms).astype(BF16), preferred_element_type=F32)
+    grad_ref[...] = grad.reshape(own, degrees, channels)
+
+
+def pack_rows(legendre, cotangent, index, core):
+    wave_dev, degrees = legendre.shape[1:]
+    rows = legendre.shape[0]
+    channels = cotangent.shape[4]
+
+    def of_wave(array, wave):
+        return jnp.where(index == wave // wave_dev, array[:, wave % wave_dev], 0)
+
+    half = degrees // 2
+    table = jnp.stack([of_wave(legendre, wave) for wave in range(degrees)], axis=0)
+    table = table.transpose(0, 2, 1).reshape(2, half * degrees, rows)
+    high = lax.reduce_precision(table, 8, 7)
+    middle = lax.reduce_precision(table - high, 8, 7)
+    low = table - high - middle
+    pieces = jnp.concatenate([high, middle, low], axis=2)
+    pieces = jnp.pad(pieces, ((0, 0), (0, 0), (0, channels // 2 - 3 * rows)))
+    pieces = jnp.concatenate([pieces[0], pieces[1]], axis=1).astype(BF16)
+
+    groups = []
+    for group in range(half + 1):
+        block = of_wave(cotangent, group)
+        if 0 < group < degrees - group:
+            rest = of_wave(cotangent, degrees - group)
+            block = jnp.concatenate([rest[degrees - group :], block[group:]], axis=0)
+        groups.append(block)
+    packed = jnp.stack(groups, axis=0).transpose(3, 0, 2, 1, 4)
+    packed = packed.reshape(packed.shape[0], (half + 1) * 2 * degrees, channels)
+    mine = jnp.where(core == 0, packed[0], packed[1])
+    other = jnp.where(core == 0, packed[1], packed[0])
+    return jnp.concatenate([mine, pieces], axis=0), jnp.concatenate([other, pieces], axis=0)
+
+
+def sparse_shards(fields, legendre, mixing, cotangent):
+    samples, rows, cells, channels = fields.shape
+    lon_count = lax.axis_size("lon")
+    wave_dev, degrees = legendre.shape[1:]
+    parts = 2 * degrees
+    spec_rows = parts * rows
+    index = lax.axis_index("lon")
+    core = lax.rem(index, 2)
+    where = index.reshape(1).astype(jnp.int32)
+    whole = pl.BlockSpec(memory_space=pltpu.VMEM)
+    scalar = pl.BlockSpec(memory_space=pltpu.SMEM)
+    params = pltpu.CompilerParams(vmem_limit_bytes=VMEM_BYTES)
+
+    keep, send = pl.pallas_call(
+        functools.partial(fourier_kernel, cells * lon_count),
+        out_shape=(
+            jax.ShapeDtypeStruct((spec_rows, channels), F32),
+            jax.ShapeDtypeStruct((spec_rows, channels), BF16),
+        ),
+        in_specs=[scalar, whole],
+        out_specs=(whole, whole),
+        scratch_shapes=[pltpu.VMEM((parts, rows, channels), F32)],
+        compiler_params=params,
+    )(where, fields)
+
+    def exchange(array, bits):
+        pairs = [(i, i ^ bits[i % 2]) for i in range(lon_count)]
+        return lax.ppermute(array, "lon", pairs)
+
+    mine, other = pack_rows(legendre, cotangent, index, core)
+    got = exchange(send, (1, 1))
+    extra = exchange(other, (1, 1))
+    acc = jnp.concatenate(
+        [keep + got.astype(F32), mine.astype(F32) + extra.astype(F32)], axis=0
+    )
+    bits = [1 << k for k in range(1, lon_count.bit_length() - 1)]
+    shift = len(bits) // 2
+    orders = list(zip(bits, bits[shift:] + bits[:shift]))
+    for step, order in enumerate(orders):
+        got = exchange(acc.astype(BF16), order)
+        if step < len(orders) - 1:
+            acc = acc + got.astype(F32)
+
+    cot_rows = (degrees // 2 + 1) * parts
+    pay_rows = parts * degrees + cot_rows
+    pay = pl.pallas_call(
+        functools.partial(legendre_kernel, rows, degrees),
+        out_shape=jax.ShapeDtypeStruct((pay_rows, channels), BF16),
+        in_specs=[whole, whole],
+        out_specs=whole,
+        scratch_shapes=[pltpu.VMEM((channels // LANES, parts * degrees, LANES), F32)],
+        compiler_params=params,
+    )(acc, got)
+    paid = exchange(pay, (1, 1))
+
+    block_rows = 2 * wave_dev * samples
+    terms = parts * degrees * samples
+    mixed, grad = pl.pallas_call(
+        functools.partial(mixing_kernel, wave_dev, samples),
+        out_shape=(
+            jax.ShapeDtypeStruct((degrees, block_rows, channels), BF16),
+            jax.ShapeDtypeStruct((channels // lon_count, degrees, channels), F32),
+        ),
+        in_specs=[scalar, whole, whole, whole],
+        out_specs=(whole, whole),
+        scratch_shapes=[
+            pltpu.VMEM((channels // LANES, terms + block_rows, LANES), F32),
+            pltpu.VMEM((channels // LANES, terms, LANES), F32),
+        ],
+        compiler_params=params,
+    )(where, pay, paid, mixing)
+    return mixed.reshape(degrees, wave_dev, 2, samples, channels), grad
+
+
+def few_waves(mesh, fields, legendre):
+    samples, rows, longitudes, channels = fields.shape
+    waves, degrees = legendre.shape[1:]
+    count = mesh.shape["lon"]
+    return (
+        mesh.shape["lat"] == 1
+        and samples == 2
+        and count >= 4
+        and count & (count - 1) == 0
+        and degrees == TILE
+        and degrees <= waves
+        and rows % TILE == 0
+        and 3 * rows <= LANES
+        and channels == 2 * LANES
+        and channels // count == TILE
+        and longitudes % 4 == 0
+        and (4 * waves // count) % TILE == 0
+    )
+
+
 def solution(mesh):
     placed = (
         P(None, "lat", "lon", None),
@@ -70,10 +330,15 @@
         P("lat", None, None),
         P("lat", "lon", None, None, None),
     )
-    return jax.shard_map(
-        shards,
-        mesh=mesh,
-        in_specs=placed,
-        out_specs=(P("lat", "lon", None, None, None), P("lon", "lat", None)),
-        check_vma=False,
-    )
+
+    def program(fields, legendre, mixing, cotangent):
+        body = sparse_shards if few_waves(mesh, fields, legendre) else dense_shards
+        return jax.shard_map(
+            body,
+            mesh=mesh,
+            in_specs=placed,
+            out_specs=(P("lat", "lon", None, None, None), P("lon", "lat", None)),
+            check_vma=False,
+        )(fields, legendre, mixing, cotangent)
+
+    return program

time: 245 us -> 40.4 us (0.16)
  waiting for transfers between devices: 163 us -> 22.4 us
  local copies, waits for them, and re-layouts: 45.4 us -> 1.6 us
  between operations: 14.2 us -> 0.91 us
  matrix products: 5.92 us -> 0 us
    reduce_scatter x1 -> x0, waiting for transfers between devices: 135 us -> none  [shards(): lax.psum_scatter(jnp.einsum('lrc,lrd->cld', coef_bf, cot_rows, preferred_...]
    all_to_all x2 -> x0, waiting for transfers between devices: 28.8 us -> none  [the longest x1 16.5 us: shards(): lax.all_to_all(spectrum, 'lon', split_axis=1, concat_axis=3, tiled=True)]
    unnamed x12 -> x6, local copies, waits for them, and re-layouts: 27 us -> 0.02 us
    ppermute x0 -> x7, waiting for transfers between devices: none -> 22.4 us  [exchange(): return lax.ppermute(array, 'lon', pairs)]
    all_to_all x4 -> x0, local copies, waits for them, and re-layouts: 13.6 us -> none  [the longest x2 10.9 us: shards(): lax.all_to_all(fields, 'lon', split_axis=3, concat_axis=2, tiled=True)]
    all_to_all x2 -> x0, starting transfers between devices: 10.8 us -> none  [the longest x1 7.48 us: shards(): lax.all_to_all(fields, 'lon', split_axis=3, concat_axis=2, tiled=True)]
    ppermute x0 -> x7, starting transfers between devices: none -> 10.7 us  [exchange(): return lax.ppermute(array, 'lon', pairs)]
    dot_general x5 -> x0, matrix products: 5.92 us -> none  [the longest x1 2.84 us: shards(): jnp.einsum('jml,jmq->lmq', basis, spectral_waves, precision=lax.Precision...]
  transfers between devices with their start and end apart: 3 -> 7, of which waited for: 3 -> 7; matrix products, arithmetic and copies ran while one was open for 2% -> 0% of each run, Pallas kernels for 0% -> 1%
where the time goes in v1:
time: 40.4 us; the launch traced here: 40.2 us
  waiting for transfers between devices  22.4 us (55%)
  starting transfers between devices  10.7 us (26%)
  other arithmetic  2.35 us (6%)
  Pallas kernels  2.14 us (5%)
  local copies, waits for them, and re-layouts  1.6 us (4%)
  between operations  0.91 us (2%)
    ppermute x7, waiting for transfers between devices, exchange(): return lax.ppermute(array, 'lon', pairs)  22.4 us
    ppermute x7, starting transfers between devices, exchange(): return lax.ppermute(array, 'lon', pairs)  10.7 us
    pallas_call x1, Pallas kernels, sparse_shards(): pl.pallas_call(functools.partial(mixing_kernel, wave_dev, samples), out_s...  1.22 us
    slice x1, local copies, waits for them, and re-layouts, of_wave(): return jnp.where(index == wave // wave_dev, array[:, wave % wave_dev], 0)  0.85 us
    unnamed x11, other arithmetic  0.85 us
  transfers between devices with their start and end apart: 7, of which 7 were waited for; matrix products, arithmetic and copies ran while one was open for 0% of the time, Pallas kernels for 1%

profile of v1, /device:TPU:0, one launch (start us, length us, event | category | flops | bytes accessed | tf_op | source)
XLA Modules:
  0.0 40.2 jit_solution(2073877820906414791)
XLA Ops:
  0.7 0.7 %constant_dynamic-update-slice_fusion.4 = bf16[5,8,2,2,256]{4,3,2,1,0:T(2,128)(2,1)S(1)} fusion(pred[]{:T(512)S(6)} %eq.7, bf16[8,6,2,2,256]{4,3,2,1,0:T(2,128)(2,1)} %param.7), kind=kLoop, calls=%fused_computation.23 | loop fusion | flops 8191 | bytes 32769
  1.4 0.0 copy-start.2
  1.4 0.9 %fusion.14 = (bf16[8,1,2,2,256]{4,3,2,1,0:T(2,128)(2,1)S(1)}, bf16[8,1,2,2,256]{4,3,2,0,1:T(2,128)(2,1)S(1)}, bf16[8,1,2,2,256]{4,3,2,0,1:T(2,128)(2,1)S(1)}, bf...) fusion(bf16[8,6,2,2,256]{4,3,2,1,0:T(2,128)(2,1)} %param.7), kind=kLoop, calls=%fused_computation.60 | loop fusion | bytes 163840 | tf_op jit(solution)/shard_map/slice | solution.py:206
  2.3 0.0 copy-start.1
  2.3 0.0 copy-done.2
  2.5 0.1 fusion.3
  2.8 0.7 %constant_dynamic-update-slice_fusion = bf16[5,8,2,2,256]{4,3,2,1,0:T(2,128)(2,1)S(1)} fusion(bf16[5,8,2,2,256]{4,3,2,1,0:T(2,128)(2,1)S(1)} %constant_dynamic-update-slice_fusion.1, pred[]{:T(512)S(6)} %eq.7, bf16[8,6,2,2,256]{4,3,2,1,0:T(2,128)(2,1)} %param.7), kind=kLoop, calls=%fused_computation.19 | loop fusion | flops 8192 | bytes 32769 | tf_op jit(solution)/shard_map/stack | solution.py:225
  3.5 0.2 broadcast_select_fusion.1
  3.8 0.5 %collective-permute-start.1 = (bf16[112,256]{1,0:T(8,128)(2,1)S(1)}, bf16[112,256]{1,0:T(8,128)(2,1)S(1)}, u32[]{:S(2)}, u32[]{:S(2)}) collective-permute-start(bf16[112,256]{1,0:T(8,128)(2,1)S(1)} %fusion.2), channel_id=1, source_target_pairs={{0,1},{1,0},{2,3},{3,2},{4,5},{5,4},{6,7},{7,6},{8,9},{9,8},{10,11... | collective-permute-start | bytes 172040 | tf_op jit(solution)/shard_map/ppermute | solution.py:259
  4.3 0.0 copy-done.1
  4.3 0.4 %shard_map.59 = (f32[384,256]{1,0:T(8,128)S(1)}, bf16[384,256]{1,0:T(8,128)(2,1)S(1)}) custom-call(s32[1]{0:T(128)} %bitcast.where_ref, bf16[2,24,24,256]{3,2,1,0:T(8,128)(2,1)S(1)} %copy-done.1), custom_call_target="tpu_custom_call" | custom-call | tf_op jit(solution)/shard_map/pallas_call | solution.py:245
  4.7 0.1 collective-permute-start
  4.9 0.3 collective-permute-done.1
  5.2 1.1 %collective-permute-done = bf16[384,256]{1,0:T(8,128)(2,1)S(1)} collective-permute-done((bf16[384,256]{1,0:T(8,128)(2,1)S(1)}, bf16[384,256]{1,0:T(8,128)(2,1)S(1)}, u32[]{:S(2)}, u32[]{:S(2)}) %collective-permute-start) | collective-permute-done | bytes 196640 | tf_op jit(solution)/shard_map/ppermute | solution.py:259
  6.3 2.7 %collective-permute-start.2 = (bf16[496,256]{1,0:T(8,128)(2,1)S(1)}, bf16[496,256]{1,0:T(8,128)(2,1)S(1)}, u32[]{:S(2)}, u32[]{:S(2)}) collective-permute-start(bf16[496,256]{1,0:T(8,128)(2,1)S(1)} %fusion), channel_id=1, source_target_pairs={{0,2},{1,9},{2,0},{3,11},{4,6},{5,13},{6,4},{7,15},{8,10},{9,1},{1... | collective-permute-start | bytes 761864 | tf_op jit(solution)/shard_map/ppermute | solution.py:259
  9.0 4.3 %collective-permute-done.2 = bf16[496,256]{1,0:T(8,128)(2,1)S(1)} collective-permute-done((bf16[496,256]{1,0:T(8,128)(2,1)S(1)}, bf16[496,256]{1,0:T(8,128)(2,1)S(1)}, u32[]{:S(2)}, u32[]{:S(2)}) %collective-permute-start.2) | collective-permute-done | bytes 253984 | tf_op jit(solution)/shard_map/ppermute | solution.py:259
  13.3 0.1 fusion.7
  13.3 2.1 %collective-permute-start.3 = (bf16[496,256]{1,0:T(8,128)(2,1)S(1)}, bf16[496,256]{1,0:T(8,128)(2,1)S(1)}, u32[]{:S(2)}, u32[]{:S(2)}) collective-permute-start(bf16[496,256]{1,0:T(8,128)(2,1)S(1)} %fusion.7), channel_id=1, source_target_pairs={{0,4},{1,17},{2,6},{3,19},{4,0},{5,21},{6,2},{7,23},{8,12},{9,25},... | collective-permute-start | bytes 761864 | tf_op jit(solution)/shard_map/ppermute | solution.py:259
  15.4 4.3 %collective-permute-done.3 = bf16[496,256]{1,0:T(8,128)(2,1)S(1)} collective-permute-done((bf16[496,256]{1,0:T(8,128)(2,1)S(1)}, bf16[496,256]{1,0:T(8,128)(2,1)S(1)}, u32[]{:S(2)}, u32[]{:S(2)}) %collective-permute-start.3) | collective-permute-done | bytes 253984 | tf_op jit(solution)/shard_map/ppermute | solution.py:259
  19.7 0.1 fusion.1
  19.8 0.0 copy-start
  19.8 2.1 %collective-permute-start.4 = (bf16[496,256]{1,0:T(8,128)(2,1)S(1)}, bf16[496,256]{1,0:T(8,128)(2,1)S(1)}, u32[]{:S(2)}, u32[]{:S(2)}) collective-permute-start(bf16[496,256]{1,0:T(8,128)(2,1)S(1)} %fusion.1), channel_id=1, source_target_pairs={{0,8},{1,3},{2,10},{3,1},{4,12},{5,7},{6,14},{7,5},{8,0},{9,11},{1... | collective-permute-start | bytes 761864 | tf_op jit(solution)/shard_map/ppermute | solution.py:259
  21.9 4.3 %collective-permute-done.4 = bf16[496,256]{1,0:T(8,128)(2,1)S(1)} collective-permute-done((bf16[496,256]{1,0:T(8,128)(2,1)S(1)}, bf16[496,256]{1,0:T(8,128)(2,1)S(1)}, u32[]{:S(2)}, u32[]{:S(2)}) %collective-permute-start.4) | collective-permute-done | bytes 253984 | tf_op jit(solution)/shard_map/ppermute | solution.py:259
  26.2 0.1 fusion.13
  26.3 3.1 %collective-permute-start.5 = (bf16[496,256]{1,0:T(8,128)(2,1)S(1)}, bf16[496,256]{1,0:T(8,128)(2,1)S(1)}, u32[]{:S(2)}, u32[]{:S(2)}) collective-permute-start(bf16[496,256]{1,0:T(8,128)(2,1)S(1)} %get-tuple-element.10), channel_id=1, source_target_pairs={{0,16},{1,5},{2,18},{3,7},{4,20},{5,1},{6,22},{7,3},{8,24},{9,13},... | collective-permute-start | bytes 761864 | tf_op jit(solution)/shard_map/ppermute | solution.py:259
  29.4 7.0 %collective-permute-done.5.got_ref = bf16[496,256]{1,0:T(8,128)(2,1)S(1)} collective-permute-done((bf16[496,256]{1,0:T(8,128)(2,1)S(1)}, bf16[496,256]{1,0:T(8,128)(2,1)S(1)}, u32[]{:S(2)}, u32[]{:S(2)}) %collective-permute-start.5) | collective-permute-done | bytes 253984 | tf_op jit(solution)/shard_map/ppermute | solution.py:259
  36.4 0.5 %shard_map.60.mine_ref = bf16[208,256]{1,0:T(8,128)(2,1)S(1)} custom-call(f32[496,256]{1,0:T(8,128)S(1)} %get-tuple-element.11.acc_ref, bf16[496,256]{1,0:T(8,128)(2,1)S(1)} %collective-permute-done.5.got_ref), custom_call_target="tpu_custom_call" | custom-call | tf_op jit(solution)/shard_map/pallas_call | solution.py:277
  36.9 0.1 collective-permute-start.6
  37.0 1.3 %collective-permute-done.6.other_ref = bf16[208,256]{1,0:T(8,128)(2,1)S(1)} collective-permute-done((bf16[208,256]{1,0:T(8,128)(2,1)S(1)}, bf16[208,256]{1,0:T(8,128)(2,1)S(1)}, u32[]{:S(2)}, u32[]{:S(2)}) %collective-permute-start.6) | collective-permute-done | bytes 106528 | tf_op jit(solution)/shard_map/ppermute | solution.py:259
  38.3 0.0 copy-done
  38.3 1.2 %shard_map.61 = (bf16[8,24,256]{2,1,0:T(8,128)(2,1)S(1)}, f32[8,8,256]{2,1,0:T(8,128)}) custom-call(s32[1]{0:T(128)} %bitcast.where_ref, bf16[208,256]{1,0:T(8,128)(2,1)S(1)} %shard_map.60.mine_ref, bf16[208,256]{1,0:T(8,128)(2,1)S(1)} %collective-permute-done.6.other_ref, bf16[8,256,256]{2,1,0:T(8,128)(2,1)S(1)} %copy-done), custom_call_target="tpu_custom_call" | custom-call | tf_op jit(solution)/shard_map/pallas_call | solution.py:289
  39.5 0.7 %reshape.178 = bf16[8,6,2,2,256]{4,3,2,1,0:T(2,128)(2,1)} reshape(bf16[8,24,256]{2,1,0:T(8,128)(2,1)S(1)} %get-tuple-element.8) | data formatting | bytes 196608 | tf_op jit(solution)/shard_map/reshape | solution.py:303
  (27 shorter events, 0.4 us)
Async XLA Ops:
  1.4 0.9 %copy-start.2 = (f32[24,6,8]{0,2,1:T(8,128)S(1)}, f32[24,6,8]{0,2,1:T(8,128)}, u32[]{:S(2)}) copy-start(f32[24,6,8]{0,2,1:T(8,128)} %param.5) | copy-start | bytes 13828
  2.3 2.0 %copy-start.1 = (bf16[2,24,24,256]{3,2,1,0:T(8,128)(2,1)S(1)}, bf16[2,24,24,256]{3,2,1,0:T(8,128)(2,1)}, u32[]{:S(2)}) copy-start(bf16[2,24,24,256]{3,2,1,0:T(8,128)(2,1)} %fields_ref.1) | copy-start | bytes 1769476
  3.8 1.4 %collective-permute-start.1 = (bf16[112,256]{1,0:T(8,128)(2,1)S(1)}, bf16[112,256]{1,0:T(8,128)(2,1)S(1)}, u32[]{:S(2)}, u32[]{:S(2)}) collective-permute-start(bf16[112,256]{1,0:T(8,128)(2,1)S(1)} %fusion.2), channel_id=1, source_target_pairs={{0,1},{1,0},{2,3},{3,2},{4,5},{5,4},{6,7},{7,6},{8,9},{9,8},{10,11... | collective-permute-start | bytes 172040 | tf_op jit(solution)/shard_map/ppermute | solution.py:259
  4.7 1.5 %collective-permute-start = (bf16[384,256]{1,0:T(8,128)(2,1)S(1)}, bf16[384,256]{1,0:T(8,128)(2,1)S(1)}, u32[]{:S(2)}, u32[]{:S(2)}) collective-permute-start(bf16[384,256]{1,0:T(8,128)(2,1)S(1)} %get-tuple-element.7), channel_id=1, source_target_pairs={{0,1},{1,0},{2,3},{3,2},{4,5},{5,4},{6,7},{7,6},{8,9},{9,8},{10,11... | collective-permute-start | bytes 589832 | tf_op jit(solution)/shard_map/ppermute | solution.py:259
  6.3 7.0 %collective-permute-start.2 = (bf16[496,256]{1,0:T(8,128)(2,1)S(1)}, bf16[496,256]{1,0:T(8,128)(2,1)S(1)}, u32[]{:S(2)}, u32[]{:S(2)}) collective-permute-start(bf16[496,256]{1,0:T(8,128)(2,1)S(1)} %fusion), channel_id=1, source_target_pairs={{0,2},{1,9},{2,0},{3,11},{4,6},{5,13},{6,4},{7,15},{8,10},{9,1},{1... | collective-permute-start | bytes 761864 | tf_op jit(solution)/shard_map/ppermute | solution.py:259
  13.3 6.4 %collective-permute-start.3 = (bf16[496,256]{1,0:T(8,128)(2,1)S(1)}, bf16[496,256]{1,0:T(8,128)(2,1)S(1)}, u32[]{:S(2)}, u32[]{:S(2)}) collective-permute-start(bf16[496,256]{1,0:T(8,128)(2,1)S(1)} %fusion.7), channel_id=1, source_target_pairs={{0,4},{1,17},{2,6},{3,19},{4,0},{5,21},{6,2},{7,23},{8,12},{9,25},... | collective-permute-start | bytes 761864 | tf_op jit(solution)/shard_map/ppermute | solution.py:259
  19.8 18.5 %copy-start = (bf16[8,256,256]{2,1,0:T(8,128)(2,1)S(1)}, bf16[8,256,256]{2,1,0:T(8,128)(2,1)}, u32[]{:S(2)}) copy-start(bf16[8,256,256]{2,1,0:T(8,128)(2,1)} %mixing_ref.1) | copy-start | bytes 3145732
  19.8 6.4 %collective-permute-start.4 = (bf16[496,256]{1,0:T(8,128)(2,1)S(1)}, bf16[496,256]{1,0:T(8,128)(2,1)S(1)}, u32[]{:S(2)}, u32[]{:S(2)}) collective-permute-start(bf16[496,256]{1,0:T(8,128)(2,1)S(1)} %fusion.1), channel_id=1, source_target_pairs={{0,8},{1,3},{2,10},{3,1},{4,12},{5,7},{6,14},{7,5},{8,0},{9,11},{1... | collective-permute-start | bytes 761864 | tf_op jit(solution)/shard_map/ppermute | solution.py:259
  26.3 10.1 %collective-permute-start.5 = (bf16[496,256]{1,0:T(8,128)(2,1)S(1)}, bf16[496,256]{1,0:T(8,128)(2,1)S(1)}, u32[]{:S(2)}, u32[]{:S(2)}) collective-permute-start(bf16[496,256]{1,0:T(8,128)(2,1)S(1)} %get-tuple-element.10), channel_id=1, source_target_pairs={{0,16},{1,5},{2,18},{3,7},{4,20},{5,1},{6,22},{7,3},{8,24},{9,13},... | collective-permute-start | bytes 761864 | tf_op jit(solution)/shard_map/ppermute | solution.py:259
  36.9 1.4 %collective-permute-start.6 = (bf16[208,256]{1,0:T(8,128)(2,1)S(1)}, bf16[208,256]{1,0:T(8,128)(2,1)S(1)}, u32[]{:S(2)}, u32[]{:S(2)}) collective-permute-start(bf16[208,256]{1,0:T(8,128)(2,1)S(1)} %shard_map.60.mine_ref), channel_id=1, source_target_pairs={{0,1},{1,0},{2,3},{3,2},{4,5},{5,4},{6,7},{7,6},{8,9},{9,8},{10,11... | collective-permute-start | bytes 319496 | tf_op jit(solution)/shard_map/ppermute | solution.py:259

commit v2 on v1

v2 whole, which is shorter than its diff:
```python
import functools
import math

import jax
import jax.numpy as jnp
from jax import lax
from jax.experimental import pallas as pl
from jax.experimental.pallas import tpu as pltpu
from jax.sharding import PartitionSpec as P

F32 = jnp.float32
BF16 = jnp.bfloat16
TILE = 8
LANES = 128
VMEM_BYTES = 32 * 1024 * 1024


def dense_shards(fields, legendre, mixing, cotangent):
    samples = fields.shape[0]
    lat_rows = fields.shape[1]
    lon_cells = fields.shape[2]
    channels = fields.shape[3]
    lon_count = lax.axis_size("lon")
    lat_count = lax.axis_size("lat")
    nlon_total = lon_cells * lon_count
    wave_dev = legendre.shape[1]
    wave_total = wave_dev * lon_count
    degrees = legendre.shape[2]
    degree_dev = degrees // lat_count
    column_rows = 2 * wave_dev * samples
    column_width = 2 * samples * channels
    positions = jnp.arange(nlon_total, dtype=jnp.int32)
    wavenums = jnp.arange(wave_total, dtype=jnp.int32)
    phase = (positions[:, None] * wavenums[None, :] % nlon_total).astype(jnp.float32) * (
        2.0 * math.pi / nlon_total
    )
    fourier = jnp.stack([jnp.cos(phase), -jnp.sin(phase)], axis=2).reshape(
        nlon_total, 2 * wave_total
    )
    fourier = fourier * (1.0 / nlon_total**0.5)
    fourier_hi = fourier.astype(jnp.bfloat16)
    fourier_lo = (fourier - fourier_hi.astype(jnp.float32)).astype(jnp.bfloat16)
    portion = lax.all_to_all(fields, "lon", split_axis=3, concat_axis=2, tiled=True)
    spectrum = jnp.einsum("bjkc,kf->jfbc", portion, fourier_hi, preferred_element_type=jnp.float32)
    spectrum = spectrum + jnp.einsum(
        "bjkc,kf->jfbc", portion, fourier_lo, preferred_element_type=jnp.float32
    )
    owned = lax.all_to_all(spectrum, "lon", split_axis=1, concat_axis=3, tiled=True)
    spectral = owned.reshape(owned.shape[0], column_rows, channels)
    wave_global = lax.axis_index("lon") * wave_dev + jnp.arange(wave_dev, dtype=jnp.int32)
    degree_ids = jnp.arange(degrees, dtype=jnp.int32)
    keep = degree_ids[None, None, :] >= wave_global[None, :, None]
    basis = jnp.where(keep, legendre, jnp.float32(0.0))
    spectral_waves = spectral.reshape(lat_rows, wave_dev, column_width)
    summed = lax.psum_scatter(
        jnp.einsum("jml,jmq->lmq", basis, spectral_waves, precision=lax.Precision.HIGHEST),
        "lat",
        scatter_dimension=0,
        tiled=True,
    )
    coef = summed.reshape(degree_dev, column_rows, channels)
    coef_bf = coef.astype(jnp.bfloat16)
    mixed = jnp.einsum("lrc,lcd->lrd", coef_bf, mixing, preferred_element_type=jnp.float32)
    mixed = mixed.astype(jnp.bfloat16).reshape(degree_dev, wave_dev, 2, samples, channels)
    cot_rows = cotangent.reshape(degree_dev, column_rows, channels)
    weight_grad = lax.psum_scatter(
        jnp.einsum("lrc,lrd->cld", coef_bf, cot_rows, preferred_element_type=jnp.float32),
        "lon",
        scatter_dimension=0,
        tiled=True,
    )
    return (mixed, weight_grad)


def put_rows(ref, first, stride, block):
    for lane in range(ref.shape[0]):
        piece = block[:, lane * LANES : (lane + 1) * LANES]
        ref[lane, pl.ds(first, block.shape[0], stride=stride), :] = piece


def take_rows(ref, first, count):
    return jnp.concatenate([ref[lane, pl.ds(first, count), :] for lane in range(ref.shape[0])], axis=1)


def fourier_kernel(nlon_total, where_ref, fields_ref, first_ref, second_ref, send_ref, total_ref):
    rows, cells, _ = fields_ref.shape[1:]
    parts = send_ref.shape[0] // rows
    index = where_ref[0]
    width = TILE * cells
    column = lax.broadcasted_iota(jnp.int32, (parts, width), 1)
    part = lax.broadcasted_iota(jnp.int32, (parts, width), 0)
    cell = index * cells + lax.rem(column, cells)
    turn = lax.rem(cell * (part // 2) + lax.rem(part, 2) * (nlon_total // 4), nlon_total)
    wave = jnp.cos(turn.astype(F32) * (2.0 * math.pi / nlon_total)) * (1.0 / nlon_total**0.5)
    spread = (parts, TILE, width)
    own_row = (
        lax.broadcasted_iota(jnp.int32, spread, 2) // cells
        == lax.broadcasted_iota(jnp.int32, spread, 1)
    )
    wave = jnp.where(own_row, jnp.broadcast_to(wave[:, None, :], spread), 0.0)
    wave = wave.reshape(parts * TILE, width)
    wave_hi = wave.astype(BF16)
    wave_lo = (wave - wave_hi.astype(F32)).astype(BF16)
    core = lax.rem(index, 2)
    for sample in (1 - core, core):
        for first in range(0, rows, TILE):
            grid = fields_ref[sample, pl.ds(first, TILE)]
            grid = grid.astype(F32).reshape(width, grid.shape[2]).astype(BF16)
            sums = jnp.dot(wave_hi, grid, preferred_element_type=F32)
            sums = sums + jnp.dot(wave_lo, grid, preferred_element_type=F32)
            total_ref[:, pl.ds(first, TILE), :] = sums.reshape(parts, TILE, sums.shape[1])
        if sample is not core:
            send_ref[...] = total_ref[...].reshape(send_ref.shape).astype(BF16)
    cut = first_ref.shape[0] // rows
    first_ref[...] = total_ref[pl.ds(0, cut)].reshape(first_ref.shape)
    second_ref[...] = total_ref[pl.ds(cut, parts - cut)].reshape(second_ref.shape)


def legendre_kernel(
    rows, first_ref, first_got_ref, second_ref, second_got_ref, out_ref
):
    degrees = TILE
    groups = degrees // 2 + 1
    first = first_ref[...] + first_got_ref[...].astype(F32)
    second = second_ref[...] + second_got_ref[...].astype(F32)
    spec_rows = 2 * degrees * rows
    spec = jnp.concatenate([first, second], axis=0)
    packed = groups * 2 * degrees
    table = spec[spec_rows + packed :]
    coefs = []
    for part in range(2):
        for group in range(groups):
            at, lane = group // 2 * degrees, group % 2 * LANES
            basis = table[at : at + degrees, lane : lane + LANES]
            basis = basis[:, : 2 * rows] + basis[:, 2 * rows : 4 * rows]
            partner = degrees - group if 0 < group < degrees - group else group
            low = (2 * group + part) * rows
            high = (2 * partner + part) * rows
            block = jnp.concatenate([spec[low : low + rows], spec[high : high + rows]], axis=0)
            coefs.append(
                jnp.dot(basis, block, preferred_element_type=F32, precision=lax.Precision.HIGHEST)
            )
    coefs.append(spec[spec_rows : spec_rows + packed])
    out_ref[...] = jnp.concatenate(coefs, axis=0).astype(BF16)


def mixing_kernel(
    wave_dev, samples, where_ref, mine_ref, other_ref, mixing_ref, mixed_ref, grad_ref, coef_ref
):
    degrees, channels = mixing_ref.shape[:2]
    groups = degrees // 2 + 1
    slots = 2 * groups * degrees
    terms = slots * samples
    index = where_ref[0]
    core = lax.rem(index, 2)
    mine, other = mine_ref[...].astype(F32), other_ref[...].astype(F32)
    held = [jnp.where(core == k, mine, other) for k in range(2)]
    for sample in range(samples):
        put_rows(coef_ref, sample, samples, held[sample][:slots])
    coef = take_rows(coef_ref, 0, terms).astype(BF16)
    cot = jnp.concatenate([held[0][slots:], held[1][slots:]], axis=0).astype(BF16)

    block_rows = 2 * wave_dev * samples
    shape = (degrees * block_rows, terms)
    row = lax.broadcasted_iota(jnp.int32, shape, 0)
    degree = row // block_rows
    wave = index * wave_dev + row % block_rows // (2 * samples)
    group = jnp.where(wave < groups, wave, degrees - wave)
    place = jnp.where(wave < groups, degree, degree - wave)
    term = ((row // samples % 2 * groups + group) * degrees + place) * samples + row % samples
    term = jnp.where(degree >= wave, term, -1)
    chosen = jnp.where(lax.broadcasted_iota(jnp.int32, shape, 1) == term, 1.0, 0.0).astype(BF16)
    lhs = jnp.dot(chosen, coef, preferred_element_type=F32)
    for degree in range(degrees):
        block = lhs[degree * block_rows : (degree + 1) * block_rows].astype(BF16)
        mixed = jnp.dot(block, mixing_ref[degree], preferred_element_type=F32)
        mixed_ref[degree] = mixed.astype(BF16)

    own = grad_ref.shape[0]
    channel = lax.broadcasted_iota(jnp.int32, (own, channels), 1)
    row = lax.broadcasted_iota(jnp.int32, (own, channels), 0)
    pick = jnp.where(channel == index * own + row, 1.0, 0.0).astype(BF16)
    turned = lax.dot_general(
        pick, coef, (((1,), (1,)), ((), ())), preferred_element_type=F32
    )
    spread = (own, degrees, terms)
    slot = lax.broadcasted_iota(jnp.int32, spread, 2) // samples
    place, group = slot % degrees, slot // degrees % groups
    degree = jnp.where(place >= group, place, place + degrees - group)
    of_degree = degree == lax.broadcasted_iota(jnp.int32, spread, 1)
    turned = jnp.where(of_degree, jnp.broadcast_to(turned[:, None, :], spread), 0.0)
    turned = turned.reshape(own * degrees, terms).astype(BF16)
    grad = jnp.dot(turned, cot, preferred_element_type=F32)
    grad_ref[...] = grad.reshape(own, degrees, channels)


def pack_rows(legendre, cotangent, index, core):
    wave_dev, degrees = legendre.shape[1:]
    rows = legendre.shape[0]
    channels = cotangent.shape[4]
    half = degrees // 2

    def of_wave(array, wave):
        return jnp.where(index == wave // wave_dev, array[:, wave % wave_dev], 0)

    tables = []
    degree = jnp.arange(degrees, dtype=jnp.int32)[:, None]
    for group in range(half + 1):
        block = jnp.where(degree >= group, of_wave(legendre, group).T, 0)
        rest = jnp.zeros_like(block)
        if 0 < group < degrees - group:
            rest = jnp.roll(of_wave(legendre, degrees - group).T, group, axis=0)
            rest = jnp.where(degree < group, rest, 0)
        tables.append(jnp.concatenate([block, rest], axis=1))
    if len(tables) % 2:
        tables.append(jnp.zeros_like(tables[0]))
    table = jnp.stack(tables, axis=0).reshape(len(tables) // 2, 2, degrees, 2 * rows)
    table = table.transpose(0, 2, 1, 3)
    high = lax.reduce_precision(table, 8, 7)
    table = jnp.concatenate([high, table - high], axis=3)
    table = jnp.pad(table, ((0, 0), (0, 0), (0, 0), (0, LANES - 4 * rows)))
    table = table.reshape(-1, channels).astype(BF16)

    groups = []
    for group in range(half + 1):
        block = of_wave(cotangent, group)
        if 0 < group < degrees - group:
            rest = of_wave(cotangent, degrees - group)
            block = jnp.concatenate([rest[degrees - group :], block[group:]], axis=0)
        groups.append(block)
    packed = jnp.stack(groups, axis=0)
    mine = jnp.where(core == 0, packed[:, :, 0], packed[:, :, 1]).reshape(-1, channels)
    other = jnp.where(core == 0, packed[:, :, 1], packed[:, :, 0]).reshape(-1, channels)
    return jnp.concatenate([mine, table], axis=0), jnp.concatenate([other, table], axis=0)


def sparse_shards(fields, legendre, mixing, cotangent):
    samples, rows, cells, channels = fields.shape
    lon_count = lax.axis_size("lon")
    wave_dev, degrees = legendre.shape[1:]
    parts = 2 * degrees
    spec_rows = parts * rows
    packed_rows = (degrees // 2 + 1) * parts
    index = lax.axis_index("lon")
    core = lax.rem(index, 2)
    where = index.reshape(1).astype(jnp.int32)
    whole = pl.BlockSpec(memory_space=pltpu.VMEM)
    scalar = pl.BlockSpec(memory_space=pltpu.SMEM)
    params = pltpu.CompilerParams(vmem_limit_bytes=VMEM_BYTES)

    def exchange(array, even, odd):
        pairs = [(i, i ^ (odd if i % 2 else even)) for i in range(lon_count)]
        return lax.ppermute(array, "lon", pairs)

    cut = (parts // 2 + 2) * rows
    keep_a, keep_b, send = pl.pallas_call(
        functools.partial(fourier_kernel, cells * lon_count),
        out_shape=(
            jax.ShapeDtypeStruct((cut, channels), F32),
            jax.ShapeDtypeStruct((spec_rows - cut, channels), F32),
            jax.ShapeDtypeStruct((spec_rows, channels), BF16),
        ),
        in_specs=[scalar, whole],
        out_specs=(whole, whole, whole),
        scratch_shapes=[pltpu.VMEM((parts, rows, channels), F32)],
        compiler_params=params,
    )(where, fields)

    got = exchange(send, 1, 1)
    extra, other = pack_rows(legendre, cotangent, index, core)
    extra = extra + exchange(other, 1, 1)
    acc_a = keep_a + got[:cut].astype(F32)
    acc_b = jnp.concatenate([keep_b + got[cut:].astype(F32), extra.astype(F32)], axis=0)
    orders_a, orders_b = hop_orders(lon_count)
    for step, (hops_a, hops_b) in enumerate(zip(orders_a, orders_b)):
        got_a = exchange(acc_a.astype(BF16), *hops_a)
        got_b = exchange(acc_b.astype(BF16), *hops_b)
        if step < len(orders_a) - 1:
            acc_a = acc_a + got_a.astype(F32)
            acc_b = acc_b + got_b.astype(F32)

    mine = pl.pallas_call(
        functools.partial(legendre_kernel, rows),
        out_shape=jax.ShapeDtypeStruct((2 * packed_rows, channels), BF16),
        in_specs=[whole] * 4,
        out_specs=whole,
        compiler_params=params,
    )(acc_a, got_a, acc_b, got_b)
    other = exchange(mine, 1, 1)

    block_rows = 2 * wave_dev * samples
    mixed, grad = pl.pallas_call(
        functools.partial(mixing_kernel, wave_dev, samples),
        out_shape=(
            jax.ShapeDtypeStruct((degrees, block_rows, channels), BF16),
            jax.ShapeDtypeStruct((channels // lon_count, degrees, channels), F32),
        ),
        in_specs=[scalar] + [whole] * 3,
        out_specs=(whole, whole),
        scratch_shapes=[pltpu.VMEM((channels // LANES, packed_rows * samples, LANES), F32)],
        compiler_params=params,
    )(where, mine, other, mixing)
    return mixed.reshape(degrees, wave_dev, 2, samples, channels), grad


def hop_orders(lon_count):
    bits = [1 << k for k in range(1, lon_count.bit_length() - 1)]
    bits[-1] += bits[-2]
    half = len(bits) // 2
    near, far = bits[:half], bits[half:]
    chain_a = list(zip(near + far, far + near))
    chain_b = list(zip(near[::-1] + far[::-1], far[::-1] + near[::-1]))
    return chain_a, chain_b


def few_waves(mesh, fields, legendre):
    samples, rows, longitudes, channels = fields.shape
    waves, degrees = legendre.shape[1:]
    count = mesh.shape["lon"]
    return (
        mesh.shape["lat"] == 1
        and samples == 2
        and count >= 8
        and count & (count - 1) == 0
        and degrees == TILE
        and degrees <= waves
        and rows % TILE == 0
        and 4 * rows <= LANES
        and channels == 2 * LANES
        and channels // count == TILE
        and longitudes % 4 == 0
        and (4 * waves // count) % TILE == 0
    )


def solution(mesh):
    placed = (
        P(None, "lat", "lon", None),
        P("lat", "lon", None),
        P("lat", None, None),
        P("lat", "lon", None, None, None),
    )

    def program(fields, legendre, mixing, cotangent):
        body = sparse_shards if few_waves(mesh, fields, legendre) else dense_shards
        return jax.shard_map(
            body,
            mesh=mesh,
            in_specs=placed,
            out_specs=(P("lat", "lon", None, None, None), P("lon", "lat", None)),
            check_vma=False,
        )(fields, legendre, mixing, cotangent)

    return program
```

time: 40.4 us -> 37.4 us (0.926)
  waiting for transfers between devices: 22.4 us -> 12.7 us
  starting transfers between devices: 10.7 us -> 17 us
  other arithmetic: 2.35 us -> 2.82 us
    ppermute x7 -> x11, waiting for transfers between devices: 22.4 us -> 12.7 us  [exchange(): return lax.ppermute(array, 'lon', pairs)]
    ppermute x7 -> x11, starting transfers between devices: 10.7 us -> 17 us  [exchange(): return lax.ppermute(array, 'lon', pairs)]
    unnamed x11 -> x7, other arithmetic: 0.85 us -> 1.04 us
  transfers between devices with their start and end apart: 7 -> 11, of which waited for: 7 -> 8; matrix products, arithmetic and copies ran while one was open for 0% -> 1% of each run, Pallas kernels for 1% -> 1%
where the time goes in v2:
time: 37.4 us; the launch traced here: 37.2 us
  starting transfers between devices  17 us (45%)
  waiting for transfers between devices  12.7 us (34%)
  other arithmetic  2.82 us (8%)
  Pallas kernels  2.06 us (6%)
  local copies, waits for them, and re-layouts  1.7 us (5%)
  between operations  0.92 us (2%)
    ppermute x11, starting transfers between devices, exchange(): return lax.ppermute(array, 'lon', pairs)  17 us
    ppermute x11, waiting for transfers between devices, exchange(): return lax.ppermute(array, 'lon', pairs)  12.7 us
    pallas_call x1, Pallas kernels, sparse_shards(): pl.pallas_call(functools.partial(mixing_kernel, wave_dev, samples), out_s...  1.21 us
    unnamed x7, other arithmetic  1.04 us
    slice x1, local copies, waits for them, and re-layouts, of_wave(): return jnp.where(index == wave // wave_dev, array[:, wave % wave_dev], 0)  0.91 us
    another operation x1, other arithmetic, pack_rows(): packed = jnp.stack(groups, axis=0)  0.75 us
  transfers between devices with their start and end apart: 11, of which 8 were waited for; matrix products, arithmetic and copies ran while one was open for 1% of the time, Pallas kernels for 1%

profile of v2, /device:TPU:0, one launch (start us, length us, event | category | flops | bytes accessed | tf_op | source)
XLA Modules:
  0.0 37.2 jit_solution(15235442532899718631)
XLA Ops:
  0.7 0.9 %fusion.27 = (bf16[8,1,2,2,256]{4,3,2,1,0:T(2,128)(2,1)S(1)}, bf16[8,1,2,2,256]{4,3,2,0,1:T(2,128)(2,1)S(1)}, bf16[8,1,2,2,256]{4,3,2,0,1:T(2,128)(2,1)S(1)}, bf...) fusion(bf16[8,6,2,2,256]{4,3,2,1,0:T(2,128)(2,1)} %param.7), kind=kLoop, calls=%fused_computation.92 | loop fusion | bytes 163840 | tf_op jit(solution)/shard_map/slice | solution.py:204
  1.6 0.7 %constant_dynamic-update-slice_fusion.4 = bf16[5,8,2,2,256]{4,3,2,1,0:T(2,128)(2,1)S(1)} fusion(pred[]{:T(512)S(6)} %eq.7, bf16[8,6,2,2,256]{4,3,2,1,0:T(2,128)(2,1)} %param.7), kind=kLoop, calls=%fused_computation.35 | loop fusion | flops 8191 | bytes 32769
  2.6 0.1 fusion.19
  2.7 0.1 constant_dynamic-update-slice_fusion.9
  2.8 0.1 constant_dynamic-update-slice_fusion.8
  3.0 0.1 constant_dynamic-update-slice_fusion.7
  3.3 0.7 %constant_dynamic-update-slice_fusion = bf16[5,8,2,2,256]{4,3,2,1,0:T(2,128)(2,1)S(1)} fusion(bf16[5,8,2,2,256]{4,3,2,1,0:T(2,128)(2,1)S(1)} %constant_dynamic-update-slice_fusion.1, pred[]{:T(512)S(6)} %eq.7, bf16[8,6,2,2,256]{4,3,2,1,0:T(2,128)(2,1)} %param.7), kind=kLoop, calls=%fused_computation.31 | loop fusion | flops 8192 | bytes 32769 | tf_op jit(solution)/shard_map/stack | solution.py:231
  4.0 0.1 broadcast_select_fusion.1
  4.1 0.1 fusion.14
  4.2 0.5 %collective-permute-start.5 = (bf16[104,256]{1,0:T(8,128)(2,1)S(1)}, bf16[104,256]{1,0:T(8,128)(2,1)S(1)}, u32[]{:S(2)}, u32[]{:S(2)}) collective-permute-start(bf16[104,256]{1,0:T(8,128)(2,1)S(1)} %pad_maximum_fusion.1), channel_id=1, source_target_pairs={{0,1},{1,0},{2,3},{3,2},{4,5},{5,4},{6,7},{7,6},{8,9},{9,8},{10,11... | collective-permute-start | bytes 159752 | tf_op jit(solution)/shard_map/ppermute | solution.py:253
  4.7 0.4 %shard_map.59 = (f32[240,256]{1,0:T(8,128)S(1)}, f32[144,256]{1,0:T(8,128)S(1)}, bf16[384,256]{1,0:T(8,128)(2,1)S(1)}) custom-call(s32[1]{0:T(128)} %bitcast.where_ref, bf16[2,24,24,256]{3,2,1,0:T(8,128)(2,1)S(1)} %copy-done.1), custom_call_target="tpu_custom_call" | custom-call | tf_op jit(solution)/shard_map/pallas_call | solution.py:256
  5.2 0.1 collective-permute-start
  5.3 0.3 collective-permute-done.5
  5.6 1.1 %collective-permute-done = bf16[384,256]{1,0:T(8,128)(2,1)S(1)} collective-permute-done((bf16[384,256]{1,0:T(8,128)(2,1)S(1)}, bf16[384,256]{1,0:T(8,128)(2,1)S(1)}, u32[]{:S(2)}, u32[]{:S(2)}) %collective-permute-start) | collective-permute-done | bytes 196640 | tf_op jit(solution)/shard_map/ppermute | solution.py:253
  6.7 2.7 %collective-permute-start.6 = (bf16[248,256]{1,0:T(8,128)(2,1)S(1)}, bf16[248,256]{1,0:T(8,128)(2,1)S(1)}, u32[]{:S(2)}, u32[]{:S(2)}) collective-permute-start(bf16[248,256]{1,0:T(8,128)(2,1)S(1)} %fusion), channel_id=1, source_target_pairs={{0,4},{1,25},{2,6},{3,27},{4,0},{5,29},{6,2},{7,31},{8,12},{9,17},... | collective-permute-start | bytes 380936 | tf_op jit(solution)/shard_map/ppermute | solution.py:253
  9.5 1.6 %collective-permute-start.1 = (bf16[240,256]{1,0:T(8,128)(2,1)S(1)}, bf16[240,256]{1,0:T(8,128)(2,1)S(1)}, u32[]{:S(2)}, u32[]{:S(2)}) collective-permute-start(bf16[240,256]{1,0:T(8,128)(2,1)S(1)} %fusion.2), channel_id=1, source_target_pairs={{0,2},{1,9},{2,0},{3,11},{4,6},{5,13},{6,4},{7,15},{8,10},{9,1},{1... | collective-permute-start | bytes 368648 | tf_op jit(solution)/shard_map/ppermute | solution.py:253
  11.0 1.3 %collective-permute-done.6 = bf16[248,256]{1,0:T(8,128)(2,1)S(1)} collective-permute-done((bf16[248,256]{1,0:T(8,128)(2,1)S(1)}, bf16[248,256]{1,0:T(8,128)(2,1)S(1)}, u32[]{:S(2)}, u32[]{:S(2)}) %collective-permute-start.6) | collective-permute-done | bytes 127008 | tf_op jit(solution)/shard_map/ppermute | solution.py:253
  12.4 2.1 %collective-permute-start.7 = (bf16[248,256]{1,0:T(8,128)(2,1)S(1)}, bf16[248,256]{1,0:T(8,128)(2,1)S(1)}, u32[]{:S(2)}, u32[]{:S(2)}) collective-permute-start(bf16[248,256]{1,0:T(8,128)(2,1)S(1)} %fusion.16), channel_id=1, source_target_pairs={{0,2},{1,9},{2,0},{3,11},{4,6},{5,13},{6,4},{7,15},{8,10},{9,1},{1... | collective-permute-start | bytes 380936 | tf_op jit(solution)/shard_map/ppermute | solution.py:253
  14.5 1.6 %collective-permute-start.2 = (bf16[240,256]{1,0:T(8,128)(2,1)S(1)}, bf16[240,256]{1,0:T(8,128)(2,1)S(1)}, u32[]{:S(2)}, u32[]{:S(2)}) collective-permute-start(bf16[240,256]{1,0:T(8,128)(2,1)S(1)} %fusion.24), channel_id=1, source_target_pairs={{0,4},{1,25},{2,6},{3,27},{4,0},{5,29},{6,2},{7,31},{8,12},{9,17},... | collective-permute-start | bytes 368648 | tf_op jit(solution)/shard_map/ppermute | solution.py:253
  16.1 1.3 %collective-permute-done.7 = bf16[248,256]{1,0:T(8,128)(2,1)S(1)} collective-permute-done((bf16[248,256]{1,0:T(8,128)(2,1)S(1)}, bf16[248,256]{1,0:T(8,128)(2,1)S(1)}, u32[]{:S(2)}, u32[]{:S(2)}) %collective-permute-start.7) | collective-permute-done | bytes 127008 | tf_op jit(solution)/shard_map/ppermute | solution.py:253
  17.4 4.2 %collective-permute-start.8 = (bf16[248,256]{1,0:T(8,128)(2,1)S(1)}, bf16[248,256]{1,0:T(8,128)(2,1)S(1)}, u32[]{:S(2)}, u32[]{:S(2)}) collective-permute-start(bf16[248,256]{1,0:T(8,128)(2,1)S(1)} %fusion.1), channel_id=1, source_target_pairs={{0,24},{1,5},{2,26},{3,7},{4,28},{5,1},{6,30},{7,3},{8,16},{9,13},... | collective-permute-start | bytes 380936 | tf_op jit(solution)/shard_map/ppermute | solution.py:253
  21.8 2.9 %collective-permute-done.8 = bf16[248,256]{1,0:T(8,128)(2,1)S(1)} collective-permute-done((bf16[248,256]{1,0:T(8,128)(2,1)S(1)}, bf16[248,256]{1,0:T(8,128)(2,1)S(1)}, u32[]{:S(2)}, u32[]{:S(2)}) %collective-permute-start.8) | collective-permute-done | bytes 127008 | tf_op jit(solution)/shard_map/ppermute | solution.py:253
  24.6 0.1 fusion.25
  24.7 1.3 %collective-permute-start.9 = (bf16[248,256]{1,0:T(8,128)(2,1)S(1)}, bf16[248,256]{1,0:T(8,128)(2,1)S(1)}, u32[]{:S(2)}, u32[]{:S(2)}) collective-permute-start(bf16[248,256]{1,0:T(8,128)(2,1)S(1)} %get-tuple-element.12), channel_id=1, source_target_pairs={{0,8},{1,3},{2,10},{3,1},{4,12},{5,7},{6,14},{7,5},{8,0},{9,11},{1... | collective-permute-start | bytes 380936 | tf_op jit(solution)/shard_map/ppermute | solution.py:253
  26.0 0.6 %collective-permute-done.3 = bf16[240,256]{1,0:T(8,128)(2,1)S(1)} collective-permute-done((bf16[240,256]{1,0:T(8,128)(2,1)S(1)}, bf16[240,256]{1,0:T(8,128)(2,1)S(1)}, u32[]{:S(2)}, u32[]{:S(2)}) %collective-permute-start.3) | collective-permute-done | bytes 122912 | tf_op jit(solution)/shard_map/ppermute | solution.py:253
  26.6 0.1 fusion.26
  26.7 2.9 %collective-permute-start.4 = (bf16[240,256]{1,0:T(8,128)(2,1)S(1)}, bf16[240,256]{1,0:T(8,128)(2,1)S(1)}, u32[]{:S(2)}, u32[]{:S(2)}) collective-permute-start(bf16[240,256]{1,0:T(8,128)(2,1)S(1)} %get-tuple-element.14), channel_id=1, source_target_pairs={{0,24},{1,5},{2,26},{3,7},{4,28},{5,1},{6,30},{7,3},{8,16},{9,13},... | collective-permute-start | bytes 368648 | tf_op jit(solution)/shard_map/ppermute | solution.py:253
  29.6 4.0 %collective-permute-done.4.first_got_ref = bf16[240,256]{1,0:T(8,128)(2,1)S(1)} collective-permute-done((bf16[240,256]{1,0:T(8,128)(2,1)S(1)}, bf16[240,256]{1,0:T(8,128)(2,1)S(1)}, u32[]{:S(2)}, u32[]{:S(2)}) %collective-permute-start.4) | collective-permute-done | bytes 122912 | tf_op jit(solution)/shard_map/ppermute | solution.py:253
  33.6 0.4 %shard_map.60.mine_ref = bf16[160,256]{1,0:T(8,128)(2,1)S(1)} custom-call(f32[240,256]{1,0:T(8,128)S(1)} %get-tuple-element.15.first_ref, bf16[240,256]{1,0:T(8,128)(2,1)S(1)} %collective-permute-done.4.first_got_ref, f32[248,256]{1,0:T(8,128)S(1)} %get-tuple-element.13.second_ref, bf16[248,256]{1,0:T(8,128)(2,1)S(1)} %collective-permute-done.9.second_got_ref), custom_call_target="tpu_custom_call" | custom-call | tf_op jit(solution)/shard_map/pallas_call | solution.py:282
  34.0 1.3 %collective-permute-done.10.other_ref = bf16[160,256]{1,0:T(8,128)(2,1)S(1)} collective-permute-done((bf16[160,256]{1,0:T(8,128)(2,1)S(1)}, bf16[160,256]{1,0:T(8,128)(2,1)S(1)}, u32[]{:S(2)}, u32[]{:S(2)}) %collective-permute-start.10) | collective-permute-done | bytes 81952 | tf_op jit(solution)/shard_map/ppermute | solution.py:253
  35.3 1.2 %shard_map.61 = (bf16[8,24,256]{2,1,0:T(8,128)(2,1)S(1)}, f32[8,8,256]{2,1,0:T(8,128)}) custom-call(s32[1]{0:T(128)} %bitcast.where_ref, bf16[160,256]{1,0:T(8,128)(2,1)S(1)} %shard_map.60.mine_ref, bf16[160,256]{1,0:T(8,128)(2,1)S(1)} %collective-permute-done.10.other_ref, bf16[8,256,256]{2,1,0:T(8,128)(2,1)S(1)} %copy-done), custom_call_target="tpu_custom_call" | custom-call | tf_op jit(solution)/shard_map/pallas_call | solution.py:292
  36.5 0.7 %reshape.136 = bf16[8,6,2,2,256]{4,3,2,1,0:T(2,128)(2,1)} reshape(bf16[8,24,256]{2,1,0:T(8,128)(2,1)S(1)} %get-tuple-element.10) | data formatting | bytes 196608 | tf_op jit(solution)/shard_map/reshape | solution.py:303
  (49 shorter events, 0.9 us)
Async XLA Ops:
  0.7 1.8 %copy-start.2 = (f32[24,6,8]{0,2,1:T(8,128)S(1)}, f32[24,6,8]{0,2,1:T(8,128)}, u32[]{:S(2)}) copy-start(f32[24,6,8]{0,2,1:T(8,128)} %param.5) | copy-start | bytes 13828
  0.7 4.0 %copy-start.1 = (bf16[2,24,24,256]{3,2,1,0:T(8,128)(2,1)S(1)}, bf16[2,24,24,256]{3,2,1,0:T(8,128)(2,1)}, u32[]{:S(2)}) copy-start(bf16[2,24,24,256]{3,2,1,0:T(8,128)(2,1)} %fields_ref.1) | copy-start | bytes 1769476
  4.2 1.4 %collective-permute-start.5 = (bf16[104,256]{1,0:T(8,128)(2,1)S(1)}, bf16[104,256]{1,0:T(8,128)(2,1)S(1)}, u32[]{:S(2)}, u32[]{:S(2)}) collective-permute-start(bf16[104,256]{1,0:T(8,128)(2,1)S(1)} %pad_maximum_fusion.1), channel_id=1, source_target_pairs={{0,1},{1,0},{2,3},{3,2},{4,5},{5,4},{6,7},{7,6},{8,9},{9,8},{10,11... | collective-permute-start | bytes 159752 | tf_op jit(solution)/shard_map/ppermute | solution.py:253
  5.2 1.5 %collective-permute-start = (bf16[384,256]{1,0:T(8,128)(2,1)S(1)}, bf16[384,256]{1,0:T(8,128)(2,1)S(1)}, u32[]{:S(2)}, u32[]{:S(2)}) collective-permute-start(bf16[384,256]{1,0:T(8,128)(2,1)S(1)} %get-tuple-element.8), channel_id=1, source_target_pairs={{0,1},{1,0},{2,3},{3,2},{4,5},{5,4},{6,7},{7,6},{8,9},{9,8},{10,11... | collective-permute-start | bytes 589832 | tf_op jit(solution)/shard_map/ppermute | solution.py:253
  6.7 5.6 %collective-permute-start.6 = (bf16[248,256]{1,0:T(8,128)(2,1)S(1)}, bf16[248,256]{1,0:T(8,128)(2,1)S(1)}, u32[]{:S(2)}, u32[]{:S(2)}) collective-permute-start(bf16[248,256]{1,0:T(8,128)(2,1)S(1)} %fusion), channel_id=1, source_target_pairs={{0,4},{1,25},{2,6},{3,27},{4,0},{5,29},{6,2},{7,31},{8,12},{9,17},... | collective-permute-start | bytes 380936 | tf_op jit(solution)/shard_map/ppermute | solution.py:253
  9.5 5.0 %collective-permute-start.1 = (bf16[240,256]{1,0:T(8,128)(2,1)S(1)}, bf16[240,256]{1,0:T(8,128)(2,1)S(1)}, u32[]{:S(2)}, u32[]{:S(2)}) collective-permute-start(bf16[240,256]{1,0:T(8,128)(2,1)S(1)} %fusion.2), channel_id=1, source_target_pairs={{0,2},{1,9},{2,0},{3,11},{4,6},{5,13},{6,4},{7,15},{8,10},{9,1},{1... | collective-permute-start | bytes 368648 | tf_op jit(solution)/shard_map/ppermute | solution.py:253
  12.4 5.0 %collective-permute-start.7 = (bf16[248,256]{1,0:T(8,128)(2,1)S(1)}, bf16[248,256]{1,0:T(8,128)(2,1)S(1)}, u32[]{:S(2)}, u32[]{:S(2)}) collective-permute-start(bf16[248,256]{1,0:T(8,128)(2,1)S(1)} %fusion.16), channel_id=1, source_target_pairs={{0,2},{1,9},{2,0},{3,11},{4,6},{5,13},{6,4},{7,15},{8,10},{9,1},{1... | collective-permute-start | bytes 380936 | tf_op jit(solution)/shard_map/ppermute | solution.py:253
  14.5 7.1 %collective-permute-start.2 = (bf16[240,256]{1,0:T(8,128)(2,1)S(1)}, bf16[240,256]{1,0:T(8,128)(2,1)S(1)}, u32[]{:S(2)}, u32[]{:S(2)}) collective-permute-start(bf16[240,256]{1,0:T(8,128)(2,1)S(1)} %fusion.24), channel_id=1, source_target_pairs={{0,4},{1,25},{2,6},{3,27},{4,0},{5,29},{6,2},{7,31},{8,12},{9,17},... | collective-permute-start | bytes 368648 | tf_op jit(solution)/shard_map/ppermute | solution.py:253
  17.4 7.2 %collective-permute-start.8 = (bf16[248,256]{1,0:T(8,128)(2,1)S(1)}, bf16[248,256]{1,0:T(8,128)(2,1)S(1)}, u32[]{:S(2)}, u32[]{:S(2)}) collective-permute-start(bf16[248,256]{1,0:T(8,128)(2,1)S(1)} %fusion.1), channel_id=1, source_target_pairs={{0,24},{1,5},{2,26},{3,7},{4,28},{5,1},{6,30},{7,3},{8,16},{9,13},... | collective-permute-start | bytes 380936 | tf_op jit(solution)/shard_map/ppermute | solution.py:253
  21.7 4.9 %collective-permute-start.3 = (bf16[240,256]{1,0:T(8,128)(2,1)S(1)}, bf16[240,256]{1,0:T(8,128)(2,1)S(1)}, u32[]{:S(2)}, u32[]{:S(2)}) collective-permute-start(bf16[240,256]{1,0:T(8,128)(2,1)S(1)} %fusion.3), channel_id=1, source_target_pairs={{0,8},{1,3},{2,10},{3,1},{4,12},{5,7},{6,14},{7,5},{8,0},{9,11},{1... | collective-permute-start | bytes 368648 | tf_op jit(solution)/shard_map/ppermute | solution.py:253
  24.7 10.6 %copy-start = (bf16[8,256,256]{2,1,0:T(8,128)(2,1)S(1)}, bf16[8,256,256]{2,1,0:T(8,128)(2,1)}, u32[]{:S(2)}) copy-start(bf16[8,256,256]{2,1,0:T(8,128)(2,1)} %mixing_ref.1) | copy-start | bytes 3145732
  24.7 8.9 %collective-permute-start.9 = (bf16[248,256]{1,0:T(8,128)(2,1)S(1)}, bf16[248,256]{1,0:T(8,128)(2,1)S(1)}, u32[]{:S(2)}, u32[]{:S(2)}) collective-permute-start(bf16[248,256]{1,0:T(8,128)(2,1)S(1)} %get-tuple-element.12), channel_id=1, source_target_pairs={{0,8},{1,3},{2,10},{3,1},{4,12},{5,7},{6,14},{7,5},{8,0},{9,11},{1... | collective-permute-start | bytes 380936 | tf_op jit(solution)/shard_map/ppermute | solution.py:253
  26.7 6.8 %collective-permute-start.4 = (bf16[240,256]{1,0:T(8,128)(2,1)S(1)}, bf16[240,256]{1,0:T(8,128)(2,1)S(1)}, u32[]{:S(2)}, u32[]{:S(2)}) collective-permute-start(bf16[240,256]{1,0:T(8,128)(2,1)S(1)} %get-tuple-element.14), channel_id=1, source_target_pairs={{0,24},{1,5},{2,26},{3,7},{4,28},{5,1},{6,30},{7,3},{8,16},{9,13},... | collective-permute-start | bytes 368648 | tf_op jit(solution)/shard_map/ppermute | solution.py:253
  34.0 1.3 %collective-permute-start.10 = (bf16[160,256]{1,0:T(8,128)(2,1)S(1)}, bf16[160,256]{1,0:T(8,128)(2,1)S(1)}, u32[]{:S(2)}, u32[]{:S(2)}) collective-permute-start(bf16[160,256]{1,0:T(8,128)(2,1)S(1)} %shard_map.60.mine_ref), channel_id=1, source_target_pairs={{0,1},{1,0},{2,3},{3,2},{4,5},{5,4},{6,7},{7,6},{8,9},{9,8},{10,11... | collective-permute-start | bytes 245768 | tf_op jit(solution)/shard_map/ppermute | solution.py:253

commit v3 on v2

--- a/solution.py
+++ b/solution.py
@@ -72,20 +72,101 @@
     return (mixed, weight_grad)
 
 
-def put_rows(ref, first, stride, block):
-    for lane in range(ref.shape[0]):
-        piece = block[:, lane * LANES : (lane + 1) * LANES]
-        ref[lane, pl.ds(first, block.shape[0], stride=stride), :] = piece
-
-
-def take_rows(ref, first, count):
-    return jnp.concatenate([ref[lane, pl.ds(first, count), :] for lane in range(ref.shape[0])], axis=1)
-
-
-def fourier_kernel(nlon_total, where_ref, fields_ref, first_ref, second_ref, send_ref, total_ref):
-    rows, cells, _ = fields_ref.shape[1:]
-    parts = send_ref.shape[0] // rows
+def tile_slots(degrees):
+    slots = []
+    for group in range(degrees // 2 + 1):
+        for place in range(degrees):
+            if place >= group:
+                slots.append((group, place))
+            elif group < degrees - group:
+                slots.append((degrees - group, place + degrees - group))
+            else:
+                slots.append(None)
+    return slots
+
+
+def packed_tiles(wave_dev, index, cots, legendre_ref, table_ref):
+    degrees, rows = legendre_ref.shape[1:]
+    slots = tile_slots(degrees)
+    row = lax.broadcasted_iota(jnp.int32, (TILE, LANES), 0)
+    zeros = jnp.zeros((TILE, LANES), F32)
+    owned = [index == owner for owner in range((degrees - 1) // wave_dev + 1)]
+
+    def cotangent(slot):
+        if slot is None:
+            return zeros
+        wave, degree = slot
+        at = (degree * wave_dev + wave % wave_dev) * TILE
+        return jnp.where(owned[wave // wave_dev], cots[at : at + TILE], 0.0)
+
+    upper = row < TILE // 2
+    parts = ([], [])
+    for pair in range(len(slots) // 2):
+        one, two = cotangent(slots[2 * pair]), cotangent(slots[2 * pair + 1])
+        parts[0].append(jnp.where(upper, one, pltpu.roll(two, TILE // 2, 0)))
+        parts[1].append(jnp.where(upper, pltpu.roll(one, TILE // 2, 0), two))
+
+    table_ref[...] = jnp.zeros(table_ref.shape, F32)
+    table_ref[:, :, pl.ds(0, rows)] = legendre_ref[...]
+
+    def basis(wave):
+        block = jnp.where(owned[wave // wave_dev], table_ref[wave % wave_dev], 0.0)
+        return jnp.where(row >= wave, block, 0.0)
+
+    groups = degrees // 2 + 1
+    tables = []
+    for group in range(groups):
+        block = basis(group)
+        if 0 < group < degrees - group:
+            rest = pltpu.roll(basis(degrees - group), group, 0)
+            block = block + pltpu.roll(rest, rows, 1)
+        high = block.astype(BF16).astype(F32)
+        tables.append(high + pltpu.roll(block - high, 2 * rows, 1))
+    tables += [zeros] * (groups % 2)
+
+    half = len(slots) // 4
+    whole = []
+    for tiles in parts:
+        lanes = [tiles[lane * half : (lane + 1) * half] + tables[lane::2] for lane in range(2)]
+        whole.append(jnp.concatenate([jnp.concatenate(lane, axis=0) for lane in lanes], axis=1))
+    return whole
+
+
+def fourier_kernel(
+    nlon_total,
+    where_ref,
+    fields_ref,
+    legendre_ref,
+    cot_ref,
+    first_ref,
+    second_ref,
+    send_ref,
+    grid_ref,
+    values_ref,
+    cots_ref,
+    total_ref,
+    table_ref,
+    sems,
+):
+    rows, cells, channels = fields_ref.shape[1:]
+    wave_dev, degrees = legendre_ref.shape[:2]
+    parts = 2 * degrees
+    spec_rows = parts * rows
     index = where_ref[0]
+    core = lax.rem(index, 2)
+    chunks = [(k, first) for k in range(2) for first in range(0, rows, TILE)]
+    copies = []
+    for slot, (k, first) in enumerate(chunks):
+        sample = 1 - core if k == 0 else core
+        copies.append(
+            pltpu.make_async_copy(
+                fields_ref.at[sample, pl.ds(first, TILE)], grid_ref.at[slot], sems.at[slot]
+            )
+        )
+    copies.append(pltpu.make_async_copy(legendre_ref, values_ref, sems.at[len(chunks)]))
+    copies.append(pltpu.make_async_copy(cot_ref, cots_ref, sems.at[len(chunks) + 1]))
+    for copy in copies:
+        copy.start()
     width = TILE * cells
     column = lax.broadcasted_iota(jnp.int32, (parts, width), 1)
     part = lax.broadcasted_iota(jnp.int32, (parts, width), 0)
@@ -101,19 +182,26 @@
     wave = wave.reshape(parts * TILE, width)
     wave_hi = wave.astype(BF16)
     wave_lo = (wave - wave_hi.astype(F32)).astype(BF16)
-    core = lax.rem(index, 2)
-    for sample in (1 - core, core):
-        for first in range(0, rows, TILE):
-            grid = fields_ref[sample, pl.ds(first, TILE)]
-            grid = grid.astype(F32).reshape(width, grid.shape[2]).astype(BF16)
-            sums = jnp.dot(wave_hi, grid, preferred_element_type=F32)
-            sums = sums + jnp.dot(wave_lo, grid, preferred_element_type=F32)
-            total_ref[:, pl.ds(first, TILE), :] = sums.reshape(parts, TILE, sums.shape[1])
-        if sample is not core:
-            send_ref[...] = total_ref[...].reshape(send_ref.shape).astype(BF16)
     cut = first_ref.shape[0] // rows
-    first_ref[...] = total_ref[pl.ds(0, cut)].reshape(first_ref.shape)
-    second_ref[...] = total_ref[pl.ds(cut, parts - cut)].reshape(second_ref.shape)
+    kept = (parts - cut) * rows
+    for copy in copies[len(chunks) :]:
+        copy.wait()
+    cots = cots_ref[...].astype(F32)
+    real, imag = packed_tiles(wave_dev, index, cots, values_ref, table_ref)
+    second_ref[pl.ds(kept, real.shape[0]), :] = jnp.where(core == 0, real, imag)
+    send_ref[pl.ds(spec_rows, real.shape[0]), :] = jnp.where(core == 0, imag, real).astype(BF16)
+
+    for copy in copies[: len(chunks)]:
+        copy.wait()
+    for slot, (k, first) in enumerate(chunks):
+        grid = grid_ref[slot].astype(F32).reshape(width, channels).astype(BF16)
+        sums = jnp.dot(wave_hi, grid, preferred_element_type=F32)
+        sums = sums + jnp.dot(wave_lo, grid, preferred_element_type=F32)
+        total_ref[k, :, pl.ds(first, TILE), :] = sums.reshape(parts, TILE, channels)
+    send_ref[pl.ds(0, spec_rows), :] = total_ref[0].reshape(spec_rows, channels).astype(BF16)
+    kept_total = total_ref[1].reshape(spec_rows, channels)
+    first_ref[...] = kept_total[: cut * rows]
+    second_ref[pl.ds(0, kept), :] = kept_total[cut * rows :]
 
 
 def legendre_kernel(
@@ -145,36 +233,58 @@
 
 
 def mixing_kernel(
-    wave_dev, samples, where_ref, mine_ref, other_ref, mixing_ref, mixed_ref, grad_ref, coef_ref
+    wave_dev, samples, where_ref, mine_ref, other_ref, mixing_ref, mixed_ref, grad_ref, cot_ref, out_ref
 ):
     degrees, channels = mixing_ref.shape[:2]
     groups = degrees // 2 + 1
-    slots = 2 * groups * degrees
-    terms = slots * samples
+    slots = groups * degrees
+    terms = 2 * samples * slots
     index = where_ref[0]
     core = lax.rem(index, 2)
     mine, other = mine_ref[...].astype(F32), other_ref[...].astype(F32)
     held = [jnp.where(core == k, mine, other) for k in range(2)]
-    for sample in range(samples):
-        put_rows(coef_ref, sample, samples, held[sample][:slots])
-    coef = take_rows(coef_ref, 0, terms).astype(BF16)
-    cot = jnp.concatenate([held[0][slots:], held[1][slots:]], axis=0).astype(BF16)
-
-    block_rows = 2 * wave_dev * samples
-    shape = (degrees * block_rows, terms)
+    coef = [held[sample][part * slots : (part + 1) * slots] for part in range(2) for sample in range(2)]
+    coef = jnp.concatenate(coef, axis=0).astype(BF16)
+    cots = []
+    for part in range(2):
+        packed = held[part][2 * slots :]
+        for lane in range(2):
+            half = packed[:, lane * LANES : (lane + 1) * LANES]
+            cot_ref[part, pl.ds(lane * packed.shape[0], packed.shape[0]), :] = half
+        for sample in range(samples):
+            halves = [
+                cot_ref[part, pl.ds(2 * lane + sample, slots, stride=2 * samples), :]
+                for lane in range(2)
+            ]
+            cots.append(jnp.concatenate(halves, axis=1))
+    cot = jnp.concatenate(cots, axis=0).astype(BF16)
+
+    block = 2 * TILE
+    shape = (block, terms)
     row = lax.broadcasted_iota(jnp.int32, shape, 0)
-    degree = row // block_rows
-    wave = index * wave_dev + row % block_rows // (2 * samples)
-    group = jnp.where(wave < groups, wave, degrees - wave)
-    place = jnp.where(wave < groups, degree, degree - wave)
-    term = ((row // samples % 2 * groups + group) * degrees + place) * samples + row % samples
-    term = jnp.where(degree >= wave, term, -1)
-    chosen = jnp.where(lax.broadcasted_iota(jnp.int32, shape, 1) == term, 1.0, 0.0).astype(BF16)
-    lhs = jnp.dot(chosen, coef, preferred_element_type=F32)
+    term = lax.broadcasted_iota(jnp.int32, shape, 1)
+    wave = index * wave_dev + row // 2
+    tile = jnp.where(wave < groups, wave * degrees, (degrees - wave) * degrees - wave)
+    base = row % 2 * (samples * slots) + tile
+    chosen = []
     for degree in range(degrees):
-        block = lhs[degree * block_rows : (degree + 1) * block_rows].astype(BF16)
-        mixed = jnp.dot(block, mixing_ref[degree], preferred_element_type=F32)
-        mixed_ref[degree] = mixed.astype(BF16)
+        for sample in range(samples):
+            hit = jnp.where(wave <= degree, base + (sample * slots + degree), -1)
+            chosen.append(jnp.where(term == hit, 1.0, 0.0).astype(BF16))
+    chosen = jnp.concatenate(chosen, axis=0)
+    lhs = jnp.dot(chosen, coef, preferred_element_type=F32).astype(BF16)
+    count = 2 * wave_dev
+    for degree in range(degrees):
+        at = degree * samples * block
+        mixed = jnp.dot(
+            lhs[at : at + samples * block], mixing_ref[degree], preferred_element_type=F32
+        )
+        for sample in range(samples):
+            for lane in range(2):
+                part = mixed[sample * block : sample * block + count, lane * LANES : (lane + 1) * LANES]
+                at = degree * 2 * samples * count + 2 * lane + sample
+                out_ref[pl.ds(at, count, stride=2 * samples), :] = part
+    mixed_ref[...] = out_ref[...].astype(BF16)
 
     own = grad_ref.shape[0]
     channel = lax.broadcasted_iota(jnp.int32, (own, channels), 1)
@@ -183,55 +293,15 @@
     turned = lax.dot_general(
         pick, coef, (((1,), (1,)), ((), ())), preferred_element_type=F32
     )
-    spread = (own, degrees, terms)
-    slot = lax.broadcasted_iota(jnp.int32, spread, 2) // samples
-    place, group = slot % degrees, slot // degrees % groups
+    shape = (degrees, terms)
+    slot = lax.broadcasted_iota(jnp.int32, shape, 1) % slots
+    place, group = slot % degrees, slot // degrees
     degree = jnp.where(place >= group, place, place + degrees - group)
-    of_degree = degree == lax.broadcasted_iota(jnp.int32, spread, 1)
-    turned = jnp.where(of_degree, jnp.broadcast_to(turned[:, None, :], spread), 0.0)
-    turned = turned.reshape(own * degrees, terms).astype(BF16)
+    of_degree = degree == lax.broadcasted_iota(jnp.int32, shape, 0)
+    turned = [jnp.where(of_degree, turned[k : k + 1], 0.0) for k in range(own)]
+    turned = jnp.concatenate(turned, axis=0).astype(BF16)
     grad = jnp.dot(turned, cot, preferred_element_type=F32)
     grad_ref[...] = grad.reshape(own, degrees, channels)
-
-
-def pack_rows(legendre, cotangent, index, core):
-    wave_dev, degrees = legendre.shape[1:]
-    rows = legendre.shape[0]
-    channels = cotangent.shape[4]
-    half = degrees // 2
-
-    def of_wave(array, wave):
-        return jnp.where(index == wave // wave_dev, array[:, wave % wave_dev], 0)
-
-    tables = []
-    degree = jnp.arange(degrees, dtype=jnp.int32)[:, None]
-    for group in range(half + 1):
-        block = jnp.where(degree >= group, of_wave(legendre, group).T, 0)
-        rest = jnp.zeros_like(block)
-        if 0 < group < degrees - group:
-            rest = jnp.roll(of_wave(legendre, degrees - group).T, group, axis=0)
-            rest = jnp.where(degree < group, rest, 0)
-        tables.append(jnp.concatenate([block, rest], axis=1))
-    if len(tables) % 2:
-        tables.append(jnp.zeros_like(tables[0]))
-    table = jnp.stack(tables, axis=0).reshape(len(tables) // 2, 2, degrees, 2 * rows)
-    table = table.transpose(0, 2, 1, 3)
-    high = lax.reduce_precision(table, 8, 7)
-    table = jnp.concatenate([high, table - high], axis=3)
-    table = jnp.pad(table, ((0, 0), (0, 0), (0, 0), (0, LANES - 4 * rows)))
-    table = table.reshape(-1, channels).astype(BF16)
-
-    groups = []
-    for group in range(half + 1):
-        block = of_wave(cotangent, group)
-        if 0 < group < degrees - group:
-            rest = of_wave(cotangent, degrees - group)
-            block = jnp.concatenate([rest[degrees - group :], block[group:]], axis=0)
-        groups.append(block)
-    packed = jnp.stack(groups, axis=0)
-    mine = jnp.where(core == 0, packed[:, :, 0], packed[:, :, 1]).reshape(-1, channels)
-    other = jnp.where(core == 0, packed[:, :, 1], packed[:, :, 0]).reshape(-1, channels)
-    return jnp.concatenate([mine, table], axis=0), jnp.concatenate([other, table], axis=0)
 
 
 def sparse_shards(fields, legendre, mixing, cotangent):
@@ -242,35 +312,47 @@
     spec_rows = parts * rows
     packed_rows = (degrees // 2 + 1) * parts
     index = lax.axis_index("lon")
-    core = lax.rem(index, 2)
     where = index.reshape(1).astype(jnp.int32)
     whole = pl.BlockSpec(memory_space=pltpu.VMEM)
     scalar = pl.BlockSpec(memory_space=pltpu.SMEM)
     params = pltpu.CompilerParams(vmem_limit_bytes=VMEM_BYTES)
 
+    def in_hbm(array):
+        return pltpu.with_memory_space_constraint(array, pltpu.HBM)
+
     def exchange(array, even, odd):
         pairs = [(i, i ^ (odd if i % 2 else even)) for i in range(lon_count)]
         return lax.ppermute(array, "lon", pairs)
 
     cut = (parts // 2 + 2) * rows
-    keep_a, keep_b, send = pl.pallas_call(
+    rest = spec_rows - cut + packed_rows + (degrees // 4 + 1) * TILE
+    halves = cotangent.reshape(degrees, wave_dev, 2, samples, 2, LANES)
+    halves = halves.transpose(0, 1, 2, 4, 3, 5).reshape(-1, LANES)
+    chunks = samples * rows // TILE
+    far = pl.BlockSpec(memory_space=pltpu.HBM)
+    acc_a, acc_b, send = pl.pallas_call(
         functools.partial(fourier_kernel, cells * lon_count),
         out_shape=(
             jax.ShapeDtypeStruct((cut, channels), F32),
-            jax.ShapeDtypeStruct((spec_rows - cut, channels), F32),
-            jax.ShapeDtypeStruct((spec_rows, channels), BF16),
+            jax.ShapeDtypeStruct((rest, channels), F32),
+            jax.ShapeDtypeStruct((cut + rest, channels), BF16),
         ),
-        in_specs=[scalar, whole],
+        in_specs=[scalar, far, far, far],
         out_specs=(whole, whole, whole),
-        scratch_shapes=[pltpu.VMEM((parts, rows, channels), F32)],
+        scratch_shapes=[
+            pltpu.VMEM((chunks, TILE, cells, channels), BF16),
+            pltpu.VMEM((wave_dev, degrees, rows), F32),
+            pltpu.VMEM(halves.shape, BF16),
+            pltpu.VMEM((2, parts, rows, channels), F32),
+            pltpu.VMEM((wave_dev, degrees, LANES), F32),
+            pltpu.SemaphoreType.DMA((chunks + 2,)),
+        ],
         compiler_params=params,
-    )(where, fields)
+    )(where, in_hbm(fields), in_hbm(legendre.transpose(1, 2, 0)), in_hbm(halves))
 
     got = exchange(send, 1, 1)
-    extra, other = pack_rows(legendre, cotangent, index, core)
-    extra = extra + exchange(other, 1, 1)
-    acc_a = keep_a + got[:cut].astype(F32)
-    acc_b = jnp.concatenate([keep_b + got[cut:].astype(F32), extra.astype(F32)], axis=0)
+    acc_a = acc_a + got[:cut].astype(F32)
+    acc_b = acc_b + got[cut:].astype(F32)
     orders_a, orders_b = hop_orders(lon_count)
     for step, (hops_a, hops_b) in enumerate(zip(orders_a, orders_b)):
         got_a = exchange(acc_a.astype(BF16), *hops_a)
@@ -292,14 +374,18 @@
     mixed, grad = pl.pallas_call(
         functools.partial(mixing_kernel, wave_dev, samples),
         out_shape=(
-            jax.ShapeDtypeStruct((degrees, block_rows, channels), BF16),
+            jax.ShapeDtypeStruct((degrees * block_rows * 2, LANES), BF16),
             jax.ShapeDtypeStruct((channels // lon_count, degrees, channels), F32),
         ),
         in_specs=[scalar] + [whole] * 3,
         out_specs=(whole, whole),
-        scratch_shapes=[pltpu.VMEM((channels // LANES, packed_rows * samples, LANES), F32)],
+        scratch_shapes=[
+            pltpu.VMEM((2, packed_rows * 2, LANES), F32),
+            pltpu.VMEM((degrees * block_rows * 2, LANES), F32),
+        ],
         compiler_params=params,
     )(where, mine, other, mixing)
+    mixed = mixed.reshape(degrees, wave_dev, 2, 2, samples, LANES).transpose(0, 1, 2, 4, 3, 5)
     return mixed.reshape(degrees, wave_dev, 2, samples, channels), grad
 
 

time: 37.4 us -> 34.3 us (0.917)
  other arithmetic: 2.82 us -> 0.48 us
  local copies, waits for them, and re-layouts: 1.7 us -> 0.01 us
  Pallas kernels: 2.06 us -> 3.4 us
    pallas_call x1, Pallas kernels: 0.45 us -> 1.82 us  [sparse_shards(): pl.pallas_call(functools.partial(fourier_kernel, cells * lon_count), out_...]
    unnamed x7 -> x0, other arithmetic: 1.04 us -> none
    slice x4 -> x0, local copies, waits for them, and re-layouts: 0.92 us -> none  [the longest x1 0.91 us: of_wave(): return jnp.where(index == wave // wave_dev, array[:, wave % wave_dev], 0)]
    another operation x2 -> x0, other arithmetic: 0.76 us -> none  [the longest x1 0.75 us: pack_rows(): packed = jnp.stack(groups, axis=0)]
    reshape x1 -> x0, local copies, waits for them, and re-layouts: 0.68 us -> none  [sparse_shards(): return (mixed.reshape(degrees, wave_dev, 2, samples, channels), grad)]
    ppermute x11 -> x10, waiting for transfers between devices: 12.7 us -> 12.5 us  [exchange(): return lax.ppermute(array, 'lon', pairs)]
    ppermute x11 -> x10, starting transfers between devices: 17 us -> 17.1 us  [exchange(): return lax.ppermute(array, 'lon', pairs)]
  transfers between devices with their start and end apart: 11 -> 10, of which waited for: 8 -> 7; matrix products, arithmetic and copies ran while one was open for 1% -> 1% of each run, Pallas kernels for 1% -> 0%
where the time goes in v3:
time: 34.3 us; the launch traced here: 34.1 us
  starting transfers between devices  17.1 us (50%)
  waiting for transfers between devices  12.5 us (36%)
  Pallas kernels  3.4 us (10%)
  between operations  0.7 us (2%)
  other arithmetic  0.48 us (1%)
    ppermute x10, starting transfers between devices, exchange(): return lax.ppermute(array, 'lon', pairs)  17.1 us
    ppermute x10, waiting for transfers between devices, exchange(): return lax.ppermute(array, 'lon', pairs)  12.5 us
    pallas_call x1, Pallas kernels, sparse_shards(): pl.pallas_call(functools.partial(fourier_kernel, cells * lon_count), out_...  1.82 us
    pallas_call x1, Pallas kernels, sparse_shards(): pl.pallas_call(functools.partial(mixing_kernel, wave_dev, samples), out_s...  1.16 us
  transfers between devices with their start and end apart: 10, of which 7 were waited for; matrix products, arithmetic and copies ran while one was open for 1% of the time, Pallas kernels for 0%

profile of v3, /device:TPU:0, one launch (start us, length us, event | category | flops | bytes accessed | tf_op | source)
XLA Modules:
  0.0 34.1 jit_solution(15010516434506553350)
XLA Ops:
  0.6 1.8 %shard_map.59 = (f32[240,256]{1,0:T(8,128)S(1)}, f32[248,256]{1,0:T(8,128)S(1)}, bf16[488,256]{1,0:T(8,128)(2,1)S(1)}) custom-call(s32[1]{0:T(128)} %bitcast.where_ref, bf16[2,24,24,256]{3,2,1,0:T(8,128)(2,1)} %fields_ref.1, f32[6,8,24]{2,1,0:T(8,128)} %bitcast.13, bf16[384,128]{1,0:T(8,128)(2,1)} %bitcast.12), custom_call_target="tpu_custom_call" | custom-call | tf_op jit(solution)/shard_map/pallas_call | solution.py:333
  2.5 0.5 %collective-permute-start = (bf16[488,256]{1,0:T(8,128)(2,1)S(1)}, bf16[488,256]{1,0:T(8,128)(2,1)S(1)}, u32[]{:S(2)}, u32[]{:S(2)}) collective-permute-start(bf16[488,256]{1,0:T(8,128)(2,1)S(1)} %get-tuple-element.8), channel_id=1, source_target_pairs={{0,1},{1,0},{2,3},{3,2},{4,5},{5,4},{6,7},{7,6},{8,9},{9,8},{10,11... | collective-permute-start | bytes 749576 | tf_op jit(solution)/shard_map/ppermute | solution.py:325
  3.0 1.1 %collective-permute-done = bf16[488,256]{1,0:T(8,128)(2,1)S(1)} collective-permute-done((bf16[488,256]{1,0:T(8,128)(2,1)S(1)}, bf16[488,256]{1,0:T(8,128)(2,1)S(1)}, u32[]{:S(2)}, u32[]{:S(2)}) %collective-permute-start) | collective-permute-done | bytes 249888 | tf_op jit(solution)/shard_map/ppermute | solution.py:325
  4.2 2.9 %collective-permute-start.5 = (bf16[248,256]{1,0:T(8,128)(2,1)S(1)}, bf16[248,256]{1,0:T(8,128)(2,1)S(1)}, u32[]{:S(2)}, u32[]{:S(2)}) collective-permute-start(bf16[248,256]{1,0:T(8,128)(2,1)S(1)} %fusion), channel_id=1, source_target_pairs={{0,4},{1,25},{2,6},{3,27},{4,0},{5,29},{6,2},{7,31},{8,12},{9,17},... | collective-permute-start | bytes 380936 | tf_op jit(solution)/shard_map/ppermute | solution.py:325
  7.1 1.6 %collective-permute-start.1 = (bf16[240,256]{1,0:T(8,128)(2,1)S(1)}, bf16[240,256]{1,0:T(8,128)(2,1)S(1)}, u32[]{:S(2)}, u32[]{:S(2)}) collective-permute-start(bf16[240,256]{1,0:T(8,128)(2,1)S(1)} %fusion.2), channel_id=1, source_target_pairs={{0,2},{1,9},{2,0},{3,11},{4,6},{5,13},{6,4},{7,15},{8,10},{9,1},{1... | collective-permute-start | bytes 368648 | tf_op jit(solution)/shard_map/ppermute | solution.py:325
  8.7 1.3 %collective-permute-done.5 = bf16[248,256]{1,0:T(8,128)(2,1)S(1)} collective-permute-done((bf16[248,256]{1,0:T(8,128)(2,1)S(1)}, bf16[248,256]{1,0:T(8,128)(2,1)S(1)}, u32[]{:S(2)}, u32[]{:S(2)}) %collective-permute-start.5) | collective-permute-done | bytes 127008 | tf_op jit(solution)/shard_map/ppermute | solution.py:325
  10.0 0.1 fusion.5
  10.1 2.1 %collective-permute-start.6 = (bf16[248,256]{1,0:T(8,128)(2,1)S(1)}, bf16[248,256]{1,0:T(8,128)(2,1)S(1)}, u32[]{:S(2)}, u32[]{:S(2)}) collective-permute-start(bf16[248,256]{1,0:T(8,128)(2,1)S(1)} %fusion.5), channel_id=1, source_target_pairs={{0,2},{1,9},{2,0},{3,11},{4,6},{5,13},{6,4},{7,15},{8,10},{9,1},{1... | collective-permute-start | bytes 380936 | tf_op jit(solution)/shard_map/ppermute | solution.py:325
  12.1 0.0 collective-permute-done.1
  12.1 0.1 fusion.4
  12.2 1.6 %collective-permute-start.2 = (bf16[240,256]{1,0:T(8,128)(2,1)S(1)}, bf16[240,256]{1,0:T(8,128)(2,1)S(1)}, u32[]{:S(2)}, u32[]{:S(2)}) collective-permute-start(bf16[240,256]{1,0:T(8,128)(2,1)S(1)} %fusion.4), channel_id=1, source_target_pairs={{0,4},{1,25},{2,6},{3,27},{4,0},{5,29},{6,2},{7,31},{8,12},{9,17},... | collective-permute-start | bytes 368648 | tf_op jit(solution)/shard_map/ppermute | solution.py:325
  13.8 1.3 %collective-permute-done.6 = bf16[248,256]{1,0:T(8,128)(2,1)S(1)} collective-permute-done((bf16[248,256]{1,0:T(8,128)(2,1)S(1)}, bf16[248,256]{1,0:T(8,128)(2,1)S(1)}, u32[]{:S(2)}, u32[]{:S(2)}) %collective-permute-start.6) | collective-permute-done | bytes 127008 | tf_op jit(solution)/shard_map/ppermute | solution.py:325
  15.1 0.1 fusion.1
  15.1 4.2 %collective-permute-start.7 = (bf16[248,256]{1,0:T(8,128)(2,1)S(1)}, bf16[248,256]{1,0:T(8,128)(2,1)S(1)}, u32[]{:S(2)}, u32[]{:S(2)}) collective-permute-start(bf16[248,256]{1,0:T(8,128)(2,1)S(1)} %fusion.1), channel_id=1, source_target_pairs={{0,24},{1,5},{2,26},{3,7},{4,28},{5,1},{6,30},{7,3},{8,16},{9,13},... | collective-permute-start | bytes 380936 | tf_op jit(solution)/shard_map/ppermute | solution.py:325
  19.3 0.0 collective-permute-done.2
  19.3 0.1 fusion.3
  19.4 0.1 collective-permute-start.3
  19.5 2.9 %collective-permute-done.7 = bf16[248,256]{1,0:T(8,128)(2,1)S(1)} collective-permute-done((bf16[248,256]{1,0:T(8,128)(2,1)S(1)}, bf16[248,256]{1,0:T(8,128)(2,1)S(1)}, u32[]{:S(2)}, u32[]{:S(2)}) %collective-permute-start.7) | collective-permute-done | bytes 127008 | tf_op jit(solution)/shard_map/ppermute | solution.py:325
  22.3 0.1 fusion.6
  22.4 0.0 copy-start
  22.4 1.3 %collective-permute-start.8 = (bf16[248,256]{1,0:T(8,128)(2,1)S(1)}, bf16[248,256]{1,0:T(8,128)(2,1)S(1)}, u32[]{:S(2)}, u32[]{:S(2)}) collective-permute-start(bf16[248,256]{1,0:T(8,128)(2,1)S(1)} %get-tuple-element.12), channel_id=1, source_target_pairs={{0,8},{1,3},{2,10},{3,1},{4,12},{5,7},{6,14},{7,5},{8,0},{9,11},{1... | collective-permute-start | bytes 380936 | tf_op jit(solution)/shard_map/ppermute | solution.py:325
  23.7 0.6 %collective-permute-done.3 = bf16[240,256]{1,0:T(8,128)(2,1)S(1)} collective-permute-done((bf16[240,256]{1,0:T(8,128)(2,1)S(1)}, bf16[240,256]{1,0:T(8,128)(2,1)S(1)}, u32[]{:S(2)}, u32[]{:S(2)}) %collective-permute-start.3) | collective-permute-done | bytes 122912 | tf_op jit(solution)/shard_map/ppermute | solution.py:325
  24.3 0.1 fusion.7
  24.4 2.8 %collective-permute-start.4 = (bf16[240,256]{1,0:T(8,128)(2,1)S(1)}, bf16[240,256]{1,0:T(8,128)(2,1)S(1)}, u32[]{:S(2)}, u32[]{:S(2)}) collective-permute-start(bf16[240,256]{1,0:T(8,128)(2,1)S(1)} %get-tuple-element.14), channel_id=1, source_target_pairs={{0,24},{1,5},{2,26},{3,7},{4,28},{5,1},{6,30},{7,3},{8,16},{9,13},... | collective-permute-start | bytes 368648 | tf_op jit(solution)/shard_map/ppermute | solution.py:325
  27.3 4.0 %collective-permute-done.4.first_got_ref = bf16[240,256]{1,0:T(8,128)(2,1)S(1)} collective-permute-done((bf16[240,256]{1,0:T(8,128)(2,1)S(1)}, bf16[240,256]{1,0:T(8,128)(2,1)S(1)}, u32[]{:S(2)}, u32[]{:S(2)}) %collective-permute-start.4) | collective-permute-done | bytes 122912 | tf_op jit(solution)/shard_map/ppermute | solution.py:325
  31.3 0.0 collective-permute-done.8.second_got_ref
  31.3 0.4 %shard_map.60.mine_ref = bf16[160,256]{1,0:T(8,128)(2,1)S(1)} custom-call(f32[240,256]{1,0:T(8,128)S(1)} %get-tuple-element.15.first_ref, bf16[240,256]{1,0:T(8,128)(2,1)S(1)} %collective-permute-done.4.first_got_ref, f32[248,256]{1,0:T(8,128)S(1)} %get-tuple-element.13.second_ref, bf16[248,256]{1,0:T(8,128)(2,1)S(1)} %collective-permute-done.8.second_got_ref), custom_call_target="tpu_custom_call" | custom-call | tf_op jit(solution)/shard_map/pallas_call | solution.py:364
  31.7 0.0 collective-permute-start.9
  31.7 1.3 %collective-permute-done.9.other_ref = bf16[160,256]{1,0:T(8,128)(2,1)S(1)} collective-permute-done((bf16[160,256]{1,0:T(8,128)(2,1)S(1)}, bf16[160,256]{1,0:T(8,128)(2,1)S(1)}, u32[]{:S(2)}, u32[]{:S(2)}) %collective-permute-start.9) | collective-permute-done | bytes 81952 | tf_op jit(solution)/shard_map/ppermute | solution.py:325
  33.0 0.0 copy-done
  33.0 1.2 %shard_map.61 = (bf16[384,128]{1,0:T(8,128)(2,1)}, f32[8,8,256]{2,1,0:T(8,128)}) custom-call(s32[1]{0:T(128)} %bitcast.where_ref, bf16[160,256]{1,0:T(8,128)(2,1)S(1)} %shard_map.60.mine_ref, bf16[160,256]{1,0:T(8,128)(2,1)S(1)} %collective-permute-done.9.other_ref, bf16[8,256,256]{2,1,0:T(8,128)(2,1)S(1)} %copy-done), custom_call_target="tpu_custom_call" | custom-call | tf_op jit(solution)/shard_map/pallas_call | solution.py:374
  (2 shorter events, 0.1 us)
Async XLA Ops:
  2.5 1.7 %collective-permute-start = (bf16[488,256]{1,0:T(8,128)(2,1)S(1)}, bf16[488,256]{1,0:T(8,128)(2,1)S(1)}, u32[]{:S(2)}, u32[]{:S(2)}) collective-permute-start(bf16[488,256]{1,0:T(8,128)(2,1)S(1)} %get-tuple-element.8), channel_id=1, source_target_pairs={{0,1},{1,0},{2,3},{3,2},{4,5},{5,4},{6,7},{7,6},{8,9},{9,8},{10,11... | collective-permute-start | bytes 749576 | tf_op jit(solution)/shard_map/ppermute | solution.py:325
  4.2 5.8 %collective-permute-start.5 = (bf16[248,256]{1,0:T(8,128)(2,1)S(1)}, bf16[248,256]{1,0:T(8,128)(2,1)S(1)}, u32[]{:S(2)}, u32[]{:S(2)}) collective-permute-start(bf16[248,256]{1,0:T(8,128)(2,1)S(1)} %fusion), channel_id=1, source_target_pairs={{0,4},{1,25},{2,6},{3,27},{4,0},{5,29},{6,2},{7,31},{8,12},{9,17},... | collective-permute-start | bytes 380936 | tf_op jit(solution)/shard_map/ppermute | solution.py:325
  7.1 5.0 %collective-permute-start.1 = (bf16[240,256]{1,0:T(8,128)(2,1)S(1)}, bf16[240,256]{1,0:T(8,128)(2,1)S(1)}, u32[]{:S(2)}, u32[]{:S(2)}) collective-permute-start(bf16[240,256]{1,0:T(8,128)(2,1)S(1)} %fusion.2), channel_id=1, source_target_pairs={{0,2},{1,9},{2,0},{3,11},{4,6},{5,13},{6,4},{7,15},{8,10},{9,1},{1... | collective-permute-start | bytes 368648 | tf_op jit(solution)/shard_map/ppermute | solution.py:325
  10.1 5.0 %collective-permute-start.6 = (bf16[248,256]{1,0:T(8,128)(2,1)S(1)}, bf16[248,256]{1,0:T(8,128)(2,1)S(1)}, u32[]{:S(2)}, u32[]{:S(2)}) collective-permute-start(bf16[248,256]{1,0:T(8,128)(2,1)S(1)} %fusion.5), channel_id=1, source_target_pairs={{0,2},{1,9},{2,0},{3,11},{4,6},{5,13},{6,4},{7,15},{8,10},{9,1},{1... | collective-permute-start | bytes 380936 | tf_op jit(solution)/shard_map/ppermute | solution.py:325
  12.2 7.1 %collective-permute-start.2 = (bf16[240,256]{1,0:T(8,128)(2,1)S(1)}, bf16[240,256]{1,0:T(8,128)(2,1)S(1)}, u32[]{:S(2)}, u32[]{:S(2)}) collective-permute-start(bf16[240,256]{1,0:T(8,128)(2,1)S(1)} %fusion.4), channel_id=1, source_target_pairs={{0,4},{1,25},{2,6},{3,27},{4,0},{5,29},{6,2},{7,31},{8,12},{9,17},... | collective-permute-start | bytes 368648 | tf_op jit(solution)/shard_map/ppermute | solution.py:325
  15.1 7.2 %collective-permute-start.7 = (bf16[248,256]{1,0:T(8,128)(2,1)S(1)}, bf16[248,256]{1,0:T(8,128)(2,1)S(1)}, u32[]{:S(2)}, u32[]{:S(2)}) collective-permute-start(bf16[248,256]{1,0:T(8,128)(2,1)S(1)} %fusion.1), channel_id=1, source_target_pairs={{0,24},{1,5},{2,26},{3,7},{4,28},{5,1},{6,30},{7,3},{8,16},{9,13},... | collective-permute-start | bytes 380936 | tf_op jit(solution)/shard_map/ppermute | solution.py:325
  19.4 4.9 %collective-permute-start.3 = (bf16[240,256]{1,0:T(8,128)(2,1)S(1)}, bf16[240,256]{1,0:T(8,128)(2,1)S(1)}, u32[]{:S(2)}, u32[]{:S(2)}) collective-permute-start(bf16[240,256]{1,0:T(8,128)(2,1)S(1)} %fusion.3), channel_id=1, source_target_pairs={{0,8},{1,3},{2,10},{3,1},{4,12},{5,7},{6,14},{7,5},{8,0},{9,11},{1... | collective-permute-start | bytes 368648 | tf_op jit(solution)/shard_map/ppermute | solution.py:325
  22.4 10.6 %copy-start = (bf16[8,256,256]{2,1,0:T(8,128)(2,1)S(1)}, bf16[8,256,256]{2,1,0:T(8,128)(2,1)}, u32[]{:S(2)}) copy-start(bf16[8,256,256]{2,1,0:T(8,128)(2,1)} %mixing_ref.1) | copy-start | bytes 3145732
  22.4 8.8 %collective-permute-start.8 = (bf16[248,256]{1,0:T(8,128)(2,1)S(1)}, bf16[248,256]{1,0:T(8,128)(2,1)S(1)}, u32[]{:S(2)}, u32[]{:S(2)}) collective-permute-start(bf16[248,256]{1,0:T(8,128)(2,1)S(1)} %get-tuple-element.12), channel_id=1, source_target_pairs={{0,8},{1,3},{2,10},{3,1},{4,12},{5,7},{6,14},{7,5},{8,0},{9,11},{1... | collective-permute-start | bytes 380936 | tf_op jit(solution)/shard_map/ppermute | solution.py:325
  24.4 6.8 %collective-permute-start.4 = (bf16[240,256]{1,0:T(8,128)(2,1)S(1)}, bf16[240,256]{1,0:T(8,128)(2,1)S(1)}, u32[]{:S(2)}, u32[]{:S(2)}) collective-permute-start(bf16[240,256]{1,0:T(8,128)(2,1)S(1)} %get-tuple-element.14), channel_id=1, source_target_pairs={{0,24},{1,5},{2,26},{3,7},{4,28},{5,1},{6,30},{7,3},{8,16},{9,13},... | collective-permute-start | bytes 368648 | tf_op jit(solution)/shard_map/ppermute | solution.py:325
  31.7 1.3 %collective-permute-start.9 = (bf16[160,256]{1,0:T(8,128)(2,1)S(1)}, bf16[160,256]{1,0:T(8,128)(2,1)S(1)}, u32[]{:S(2)}, u32[]{:S(2)}) collective-permute-start(bf16[160,256]{1,0:T(8,128)(2,1)S(1)} %shard_map.60.mine_ref), channel_id=1, source_target_pairs={{0,1},{1,0},{2,3},{3,2},{4,5},{5,4},{6,7},{7,6},{8,9},{9,8},{10,11... | collective-permute-start | bytes 245768 | tf_op jit(solution)/shard_map/ppermute | solution.py:325

commit v4 on v3

--- a/solution.py
+++ b/solution.py
@@ -113,22 +113,22 @@
         block = jnp.where(owned[wave // wave_dev], table_ref[wave % wave_dev], 0.0)
         return jnp.where(row >= wave, block, 0.0)
 
-    groups = degrees // 2 + 1
-    tables = []
-    for group in range(groups):
+    table = jnp.zeros((degrees, 2 * LANES), F32)
+    for group in range(degrees // 2 + 1):
         block = basis(group)
         if 0 < group < degrees - group:
             rest = pltpu.roll(basis(degrees - group), group, 0)
             block = block + pltpu.roll(rest, rows, 1)
-        high = block.astype(BF16).astype(F32)
-        tables.append(high + pltpu.roll(block - high, 2 * rows, 1))
-    tables += [zeros] * (groups % 2)
+        block = jnp.concatenate([block, zeros], axis=1)
+        table = table + (pltpu.roll(block, 2 * rows * group, 1) if group else block)
+    high = table.astype(BF16).astype(F32)
 
     half = len(slots) // 4
     whole = []
     for tiles in parts:
-        lanes = [tiles[lane * half : (lane + 1) * half] + tables[lane::2] for lane in range(2)]
-        whole.append(jnp.concatenate([jnp.concatenate(lane, axis=0) for lane in lanes], axis=1))
+        lanes = [tiles[lane * half : (lane + 1) * half] for lane in range(2)]
+        cots = jnp.concatenate([jnp.concatenate(lane, axis=0) for lane in lanes], axis=1)
+        whole.append(jnp.concatenate([cots, high, table - high], axis=0))
     return whole
 
 
@@ -140,7 +140,8 @@
     cot_ref,
     first_ref,
     second_ref,
-    send_ref,
+    first_send_ref,
+    second_send_ref,
     grid_ref,
     values_ref,
     cots_ref,
@@ -189,7 +190,7 @@
     cots = cots_ref[...].astype(F32)
     real, imag = packed_tiles(wave_dev, index, cots, values_ref, table_ref)
     second_ref[pl.ds(kept, real.shape[0]), :] = jnp.where(core == 0, real, imag)
-    send_ref[pl.ds(spec_rows, real.shape[0]), :] = jnp.where(core == 0, imag, real).astype(BF16)
+    second_send_ref[pl.ds(kept, real.shape[0]), :] = jnp.where(core == 0, imag, real).astype(BF16)
 
     for copy in copies[: len(chunks)]:
         copy.wait()
@@ -197,11 +198,17 @@
         grid = grid_ref[slot].astype(F32).reshape(width, channels).astype(BF16)
         sums = jnp.dot(wave_hi, grid, preferred_element_type=F32)
         sums = sums + jnp.dot(wave_lo, grid, preferred_element_type=F32)
-        total_ref[k, :, pl.ds(first, TILE), :] = sums.reshape(parts, TILE, channels)
-    send_ref[pl.ds(0, spec_rows), :] = total_ref[0].reshape(spec_rows, channels).astype(BF16)
-    kept_total = total_ref[1].reshape(spec_rows, channels)
-    first_ref[...] = kept_total[: cut * rows]
-    second_ref[pl.ds(0, kept), :] = kept_total[cut * rows :]
+        for part in range(parts):
+            tile = sums[part * TILE : (part + 1) * TILE]
+            if k == 0:
+                total_ref[pl.ds(part * rows + first, TILE), :] = tile
+            elif part < cut:
+                first_ref[pl.ds(part * rows + first, TILE), :] = tile
+            else:
+                second_ref[pl.ds((part - cut) * rows + first, TILE), :] = tile
+        if k == 0 and first + TILE == rows:
+            first_send_ref[...] = total_ref[pl.ds(0, cut * rows), :].astype(BF16)
+            second_send_ref[pl.ds(0, kept), :] = total_ref[pl.ds(cut * rows, kept), :].astype(BF16)
 
 
 def legendre_kernel(
@@ -215,19 +222,22 @@
     spec = jnp.concatenate([first, second], axis=0)
     packed = groups * 2 * degrees
     table = spec[spec_rows + packed :]
+    spec_hi = spec[:spec_rows].astype(BF16).astype(F32)
+    spec_lo = spec[:spec_rows] - spec_hi
     coefs = []
     for part in range(2):
         for group in range(groups):
-            at, lane = group // 2 * degrees, group % 2 * LANES
-            basis = table[at : at + degrees, lane : lane + LANES]
-            basis = basis[:, : 2 * rows] + basis[:, 2 * rows : 4 * rows]
+            basis = table[:, 2 * rows * group : 2 * rows * (group + 1)].astype(BF16)
             partner = degrees - group if 0 < group < degrees - group else group
             low = (2 * group + part) * rows
             high = (2 * partner + part) * rows
-            block = jnp.concatenate([spec[low : low + rows], spec[high : high + rows]], axis=0)
-            coefs.append(
-                jnp.dot(basis, block, preferred_element_type=F32, precision=lax.Precision.HIGHEST)
+            block, rest = (
+                jnp.concatenate([half[low : low + rows], half[high : high + rows]], axis=0)
+                for half in (spec_hi, spec_lo)
             )
+            sums = jnp.dot(basis, block.astype(BF16), preferred_element_type=F32)
+            more = jnp.dot(basis[:degrees], rest.astype(BF16), preferred_element_type=F32)
+            coefs.append(sums[:degrees] + sums[degrees:] + more)
     coefs.append(spec[spec_rows : spec_rows + packed])
     out_ref[...] = jnp.concatenate(coefs, axis=0).astype(BF16)
 
@@ -325,34 +335,34 @@
         return lax.ppermute(array, "lon", pairs)
 
     cut = (parts // 2 + 2) * rows
-    rest = spec_rows - cut + packed_rows + (degrees // 4 + 1) * TILE
+    rest = spec_rows - cut + packed_rows + 2 * TILE
     halves = cotangent.reshape(degrees, wave_dev, 2, samples, 2, LANES)
     halves = halves.transpose(0, 1, 2, 4, 3, 5).reshape(-1, LANES)
     chunks = samples * rows // TILE
     far = pl.BlockSpec(memory_space=pltpu.HBM)
-    acc_a, acc_b, send = pl.pallas_call(
+    acc_a, acc_b, send_a, send_b = pl.pallas_call(
         functools.partial(fourier_kernel, cells * lon_count),
         out_shape=(
             jax.ShapeDtypeStruct((cut, channels), F32),
             jax.ShapeDtypeStruct((rest, channels), F32),
-            jax.ShapeDtypeStruct((cut + rest, channels), BF16),
+            jax.ShapeDtypeStruct((cut, channels), BF16),
+            jax.ShapeDtypeStruct((rest, channels), BF16),
         ),
         in_specs=[scalar, far, far, far],
-        out_specs=(whole, whole, whole),
+        out_specs=(whole, whole, whole, whole),
         scratch_shapes=[
             pltpu.VMEM((chunks, TILE, cells, channels), BF16),
             pltpu.VMEM((wave_dev, degrees, rows), F32),
             pltpu.VMEM(halves.shape, BF16),
-            pltpu.VMEM((2, parts, rows, channels), F32),
+            pltpu.VMEM((spec_rows, channels), F32),
             pltpu.VMEM((wave_dev, degrees, LANES), F32),
             pltpu.SemaphoreType.DMA((chunks + 2,)),
         ],
         compiler_params=params,
     )(where, in_hbm(fields), in_hbm(legendre.transpose(1, 2, 0)), in_hbm(halves))
 
-    got = exchange(send, 1, 1)
-    acc_a = acc_a + got[:cut].astype(F32)
-    acc_b = acc_b + got[cut:].astype(F32)
+    acc_a = acc_a + exchange(send_a, 1, 1).astype(F32)
+    acc_b = acc_b + exchange(send_b, 1, 1).astype(F32)
     orders_a, orders_b = hop_orders(lon_count)
     for step, (hops_a, hops_b) in enumerate(zip(orders_a, orders_b)):
         got_a = exchange(acc_a.astype(BF16), *hops_a)
@@ -411,7 +421,7 @@
         and degrees == TILE
         and degrees <= waves
         and rows % TILE == 0
-        and 4 * rows <= LANES
+        and 2 * rows * (degrees // 2 + 1) <= channels
         and channels == 2 * LANES
         and channels // count == TILE
         and longitudes % 4 == 0

time: 34.3 us -> 32 us (0.933)
  waiting for transfers between devices: 12.5 us -> 8.41 us
  starting transfers between devices: 17.1 us -> 19.1 us
    ppermute x10 -> x11, waiting for transfers between devices: 12.5 us -> 8.41 us  [exchange(): return lax.ppermute(array, 'lon', pairs)]
    ppermute x10 -> x11, starting transfers between devices: 17.1 us -> 19.1 us  [exchange(): return lax.ppermute(array, 'lon', pairs)]
  transfers between devices with their start and end apart: 10 -> 11, of which waited for: 7 -> 6; matrix products, arithmetic and copies ran while one was open for 1% -> 1% of each run, Pallas kernels for 0% -> 0%
where the time goes in v4:
time: 32 us; the launch traced here: 31.9 us
  starting transfers between devices  19.1 us (60%)
  waiting for transfers between devices  8.41 us (26%)
  Pallas kernels  3.23 us (10%)
  between operations  0.7 us (2%)
  other arithmetic  0.44 us (1%)
    ppermute x11, starting transfers between devices, exchange(): return lax.ppermute(array, 'lon', pairs)  19.1 us
    ppermute x11, waiting for transfers between devices, exchange(): return lax.ppermute(array, 'lon', pairs)  8.41 us
    pallas_call x1, Pallas kernels, sparse_shards(): pl.pallas_call(functools.partial(fourier_kernel, cells * lon_count), out_...  1.82 us
    pallas_call x1, Pallas kernels, sparse_shards(): pl.pallas_call(functools.partial(mixing_kernel, wave_dev, samples), out_s...  1.16 us
  transfers between devices with their start and end apart: 11, of which 6 were waited for; matrix products, arithmetic and copies ran while one was open for 1% of the time, Pallas kernels for 0%

profile of v4, /device:TPU:0, one launch (start us, length us, event | category | flops | bytes accessed | tf_op | source)
XLA Modules:
  0.0 31.9 jit_solution(14608252877726142089)
XLA Ops:
  0.6 1.8 %shard_map.59 = (f32[240,256]{1,0:T(8,128)S(1)}, f32[240,256]{1,0:T(8,128)S(1)}, bf16[240,256]{1,0:T(8,128)(2,1)S(1)}, bf16[240,256]{1,0:T(8,128)(2,1)S(1)}) custom-call(s32[1]{0:T(128)} %bitcast.where_ref, bf16[2,24,24,256]{3,2,1,0:T(8,128)(2,1)} %fields_ref.1, f32[6,8,24]{2,1,0:T(8,128)} %bitcast.13, bf16[384,128]{1,0:T(8,128)(2,1)} %bitcast.12), custom_call_target="tpu_custom_call" | custom-call | tf_op jit(solution)/shard_map/pallas_call | solution.py:343
  2.5 0.5 %collective-permute-start = (bf16[240,256]{1,0:T(8,128)(2,1)S(1)}, bf16[240,256]{1,0:T(8,128)(2,1)S(1)}, u32[]{:S(2)}, u32[]{:S(2)}) collective-permute-start(bf16[240,256]{1,0:T(8,128)(2,1)S(1)} %get-tuple-element.9), channel_id=1, source_target_pairs={{0,1},{1,0},{2,3},{3,2},{4,5},{5,4},{6,7},{7,6},{8,9},{9,8},{10,11... | collective-permute-start | bytes 368648 | tf_op jit(solution)/shard_map/ppermute | solution.py:335
  3.0 0.1 collective-permute-start.5
  3.1 0.9 %collective-permute-done = bf16[240,256]{1,0:T(8,128)(2,1)S(1)} collective-permute-done((bf16[240,256]{1,0:T(8,128)(2,1)S(1)}, bf16[240,256]{1,0:T(8,128)(2,1)S(1)}, u32[]{:S(2)}, u32[]{:S(2)}) %collective-permute-start) | collective-permute-done | bytes 122912 | tf_op jit(solution)/shard_map/ppermute | solution.py:335
  4.0 2.9 %collective-permute-start.1 = (bf16[240,256]{1,0:T(8,128)(2,1)S(1)}, bf16[240,256]{1,0:T(8,128)(2,1)S(1)}, u32[]{:S(2)}, u32[]{:S(2)}) collective-permute-start(bf16[240,256]{1,0:T(8,128)(2,1)S(1)} %fusion), channel_id=1, source_target_pairs={{0,2},{1,9},{2,0},{3,11},{4,6},{5,13},{6,4},{7,15},{8,10},{9,1},{1... | collective-permute-start | bytes 368648 | tf_op jit(solution)/shard_map/ppermute | solution.py:335
  6.9 0.0 collective-permute-done.5
  6.9 1.6 %collective-permute-start.6 = (bf16[240,256]{1,0:T(8,128)(2,1)S(1)}, bf16[240,256]{1,0:T(8,128)(2,1)S(1)}, u32[]{:S(2)}, u32[]{:S(2)}) collective-permute-start(bf16[240,256]{1,0:T(8,128)(2,1)S(1)} %fusion.2), channel_id=1, source_target_pairs={{0,4},{1,25},{2,6},{3,27},{4,0},{5,29},{6,2},{7,31},{8,12},{9,17},... | collective-permute-start | bytes 368648 | tf_op jit(solution)/shard_map/ppermute | solution.py:335
  8.5 1.2 %collective-permute-done.1 = bf16[240,256]{1,0:T(8,128)(2,1)S(1)} collective-permute-done((bf16[240,256]{1,0:T(8,128)(2,1)S(1)}, bf16[240,256]{1,0:T(8,128)(2,1)S(1)}, u32[]{:S(2)}, u32[]{:S(2)}) %collective-permute-start.1) | collective-permute-done | bytes 122912 | tf_op jit(solution)/shard_map/ppermute | solution.py:335
  9.8 2.1 %collective-permute-start.2 = (bf16[240,256]{1,0:T(8,128)(2,1)S(1)}, bf16[240,256]{1,0:T(8,128)(2,1)S(1)}, u32[]{:S(2)}, u32[]{:S(2)}) collective-permute-start(bf16[240,256]{1,0:T(8,128)(2,1)S(1)} %fusion.4), channel_id=1, source_target_pairs={{0,4},{1,25},{2,6},{3,27},{4,0},{5,29},{6,2},{7,31},{8,12},{9,17},... | collective-permute-start | bytes 368648 | tf_op jit(solution)/shard_map/ppermute | solution.py:335
  11.9 0.0 collective-permute-done.6
  12.0 1.6 %collective-permute-start.7 = (bf16[240,256]{1,0:T(8,128)(2,1)S(1)}, bf16[240,256]{1,0:T(8,128)(2,1)S(1)}, u32[]{:S(2)}, u32[]{:S(2)}) collective-permute-start(bf16[240,256]{1,0:T(8,128)(2,1)S(1)} %fusion.5), channel_id=1, source_target_pairs={{0,2},{1,9},{2,0},{3,11},{4,6},{5,13},{6,4},{7,15},{8,10},{9,1},{1... | collective-permute-start | bytes 368648 | tf_op jit(solution)/shard_map/ppermute | solution.py:335
  13.5 1.3 %collective-permute-done.2 = bf16[240,256]{1,0:T(8,128)(2,1)S(1)} collective-permute-done((bf16[240,256]{1,0:T(8,128)(2,1)S(1)}, bf16[240,256]{1,0:T(8,128)(2,1)S(1)}, u32[]{:S(2)}, u32[]{:S(2)}) %collective-permute-start.2) | collective-permute-done | bytes 122912 | tf_op jit(solution)/shard_map/ppermute | solution.py:335
  14.8 0.1 fusion.1
  14.8 2.1 %collective-permute-start.3 = (bf16[240,256]{1,0:T(8,128)(2,1)S(1)}, bf16[240,256]{1,0:T(8,128)(2,1)S(1)}, u32[]{:S(2)}, u32[]{:S(2)}) collective-permute-start(bf16[240,256]{1,0:T(8,128)(2,1)S(1)} %fusion.1), channel_id=1, source_target_pairs={{0,8},{1,3},{2,10},{3,1},{4,12},{5,7},{6,14},{7,5},{8,0},{9,11},{1... | collective-permute-start | bytes 368648 | tf_op jit(solution)/shard_map/ppermute | solution.py:335
  17.0 0.0 collective-permute-done.7
  17.0 0.1 fusion.3
  17.1 3.6 %collective-permute-start.8 = (bf16[240,256]{1,0:T(8,128)(2,1)S(1)}, bf16[240,256]{1,0:T(8,128)(2,1)S(1)}, u32[]{:S(2)}, u32[]{:S(2)}) collective-permute-start(bf16[240,256]{1,0:T(8,128)(2,1)S(1)} %fusion.3), channel_id=1, source_target_pairs={{0,24},{1,5},{2,26},{3,7},{4,28},{5,1},{6,30},{7,3},{8,16},{9,13},... | collective-permute-start | bytes 368648 | tf_op jit(solution)/shard_map/ppermute | solution.py:335
  20.6 0.0 collective-permute-done.3
  20.7 0.1 fusion.7
  20.7 0.0 copy-start
  20.8 3.3 %collective-permute-start.4 = (bf16[240,256]{1,0:T(8,128)(2,1)S(1)}, bf16[240,256]{1,0:T(8,128)(2,1)S(1)}, u32[]{:S(2)}, u32[]{:S(2)}) collective-permute-start(bf16[240,256]{1,0:T(8,128)(2,1)S(1)} %get-tuple-element.16), channel_id=1, source_target_pairs={{0,24},{1,5},{2,26},{3,7},{4,28},{5,1},{6,30},{7,3},{8,16},{9,13},... | collective-permute-start | bytes 368648 | tf_op jit(solution)/shard_map/ppermute | solution.py:335
  24.1 0.0 collective-permute-done.8
  24.1 0.1 fusion.6
  24.1 1.2 %collective-permute-start.9 = (bf16[240,256]{1,0:T(8,128)(2,1)S(1)}, bf16[240,256]{1,0:T(8,128)(2,1)S(1)}, u32[]{:S(2)}, u32[]{:S(2)}) collective-permute-start(bf16[240,256]{1,0:T(8,128)(2,1)S(1)} %get-tuple-element.14), channel_id=1, source_target_pairs={{0,8},{1,3},{2,10},{3,1},{4,12},{5,7},{6,14},{7,5},{8,0},{9,11},{1... | collective-permute-start | bytes 368648 | tf_op jit(solution)/shard_map/ppermute | solution.py:335
  25.4 2.2 %collective-permute-done.4.first_got_ref = bf16[240,256]{1,0:T(8,128)(2,1)S(1)} collective-permute-done((bf16[240,256]{1,0:T(8,128)(2,1)S(1)}, bf16[240,256]{1,0:T(8,128)(2,1)S(1)}, u32[]{:S(2)}, u32[]{:S(2)}) %collective-permute-start.4) | collective-permute-done | bytes 122912 | tf_op jit(solution)/shard_map/ppermute | solution.py:335
  27.6 1.5 %collective-permute-done.9.second_got_ref = bf16[240,256]{1,0:T(8,128)(2,1)S(1)} collective-permute-done((bf16[240,256]{1,0:T(8,128)(2,1)S(1)}, bf16[240,256]{1,0:T(8,128)(2,1)S(1)}, u32[]{:S(2)}, u32[]{:S(2)}) %collective-permute-start.9) | collective-permute-done | bytes 122912 | tf_op jit(solution)/shard_map/ppermute | solution.py:335
  29.1 0.2 shard_map.60.mine_ref
  29.3 0.1 collective-permute-start.10
  29.4 1.3 %collective-permute-done.10.other_ref = bf16[160,256]{1,0:T(8,128)(2,1)S(1)} collective-permute-done((bf16[160,256]{1,0:T(8,128)(2,1)S(1)}, bf16[160,256]{1,0:T(8,128)(2,1)S(1)}, u32[]{:S(2)}, u32[]{:S(2)}) %collective-permute-start.10) | collective-permute-done | bytes 81952 | tf_op jit(solution)/shard_map/ppermute | solution.py:335
  30.7 0.0 copy-done
  30.7 1.2 %shard_map.61 = (bf16[384,128]{1,0:T(8,128)(2,1)}, f32[8,8,256]{2,1,0:T(8,128)}) custom-call(s32[1]{0:T(128)} %bitcast.where_ref, bf16[160,256]{1,0:T(8,128)(2,1)S(1)} %shard_map.60.mine_ref, bf16[160,256]{1,0:T(8,128)(2,1)S(1)} %collective-permute-done.10.other_ref, bf16[8,256,256]{2,1,0:T(8,128)(2,1)S(1)} %copy-done), custom_call_target="tpu_custom_call" | custom-call | tf_op jit(solution)/shard_map/pallas_call | solution.py:384
  (4 shorter events, 0.1 us)
Async XLA Ops:
  2.5 1.5 %collective-permute-start = (bf16[240,256]{1,0:T(8,128)(2,1)S(1)}, bf16[240,256]{1,0:T(8,128)(2,1)S(1)}, u32[]{:S(2)}, u32[]{:S(2)}) collective-permute-start(bf16[240,256]{1,0:T(8,128)(2,1)S(1)} %get-tuple-element.9), channel_id=1, source_target_pairs={{0,1},{1,0},{2,3},{3,2},{4,5},{5,4},{6,7},{7,6},{8,9},{9,8},{10,11... | collective-permute-start | bytes 368648 | tf_op jit(solution)/shard_map/ppermute | solution.py:335
  3.0 3.9 %collective-permute-start.5 = (bf16[240,256]{1,0:T(8,128)(2,1)S(1)}, bf16[240,256]{1,0:T(8,128)(2,1)S(1)}, u32[]{:S(2)}, u32[]{:S(2)}) collective-permute-start(bf16[240,256]{1,0:T(8,128)(2,1)S(1)} %get-tuple-element.11), channel_id=1, source_target_pairs={{0,1},{1,0},{2,3},{3,2},{4,5},{5,4},{6,7},{7,6},{8,9},{9,8},{10,11... | collective-permute-start | bytes 368648 | tf_op jit(solution)/shard_map/ppermute | solution.py:335
  4.0 5.8 %collective-permute-start.1 = (bf16[240,256]{1,0:T(8,128)(2,1)S(1)}, bf16[240,256]{1,0:T(8,128)(2,1)S(1)}, u32[]{:S(2)}, u32[]{:S(2)}) collective-permute-start(bf16[240,256]{1,0:T(8,128)(2,1)S(1)} %fusion), channel_id=1, source_target_pairs={{0,2},{1,9},{2,0},{3,11},{4,6},{5,13},{6,4},{7,15},{8,10},{9,1},{1... | collective-permute-start | bytes 368648 | tf_op jit(solution)/shard_map/ppermute | solution.py:335
  6.9 5.0 %collective-permute-start.6 = (bf16[240,256]{1,0:T(8,128)(2,1)S(1)}, bf16[240,256]{1,0:T(8,128)(2,1)S(1)}, u32[]{:S(2)}, u32[]{:S(2)}) collective-permute-start(bf16[240,256]{1,0:T(8,128)(2,1)S(1)} %fusion.2), channel_id=1, source_target_pairs={{0,4},{1,25},{2,6},{3,27},{4,0},{5,29},{6,2},{7,31},{8,12},{9,17},... | collective-permute-start | bytes 368648 | tf_op jit(solution)/shard_map/ppermute | solution.py:335
  9.8 5.0 %collective-permute-start.2 = (bf16[240,256]{1,0:T(8,128)(2,1)S(1)}, bf16[240,256]{1,0:T(8,128)(2,1)S(1)}, u32[]{:S(2)}, u32[]{:S(2)}) collective-permute-start(bf16[240,256]{1,0:T(8,128)(2,1)S(1)} %fusion.4), channel_id=1, source_target_pairs={{0,4},{1,25},{2,6},{3,27},{4,0},{5,29},{6,2},{7,31},{8,12},{9,17},... | collective-permute-start | bytes 368648 | tf_op jit(solution)/shard_map/ppermute | solution.py:335
  12.0 5.0 %collective-permute-start.7 = (bf16[240,256]{1,0:T(8,128)(2,1)S(1)}, bf16[240,256]{1,0:T(8,128)(2,1)S(1)}, u32[]{:S(2)}, u32[]{:S(2)}) collective-permute-start(bf16[240,256]{1,0:T(8,128)(2,1)S(1)} %fusion.5), channel_id=1, source_target_pairs={{0,2},{1,9},{2,0},{3,11},{4,6},{5,13},{6,4},{7,15},{8,10},{9,1},{1... | collective-permute-start | bytes 368648 | tf_op jit(solution)/shard_map/ppermute | solution.py:335
  14.8 5.8 %collective-permute-start.3 = (bf16[240,256]{1,0:T(8,128)(2,1)S(1)}, bf16[240,256]{1,0:T(8,128)(2,1)S(1)}, u32[]{:S(2)}, u32[]{:S(2)}) collective-permute-start(bf16[240,256]{1,0:T(8,128)(2,1)S(1)} %fusion.1), channel_id=1, source_target_pairs={{0,8},{1,3},{2,10},{3,1},{4,12},{5,7},{6,14},{7,5},{8,0},{9,11},{1... | collective-permute-start | bytes 368648 | tf_op jit(solution)/shard_map/ppermute | solution.py:335
  17.1 7.0 %collective-permute-start.8 = (bf16[240,256]{1,0:T(8,128)(2,1)S(1)}, bf16[240,256]{1,0:T(8,128)(2,1)S(1)}, u32[]{:S(2)}, u32[]{:S(2)}) collective-permute-start(bf16[240,256]{1,0:T(8,128)(2,1)S(1)} %fusion.3), channel_id=1, source_target_pairs={{0,24},{1,5},{2,26},{3,7},{4,28},{5,1},{6,30},{7,3},{8,16},{9,13},... | collective-permute-start | bytes 368648 | tf_op jit(solution)/shard_map/ppermute | solution.py:335
  20.7 10.0 %copy-start = (bf16[8,256,256]{2,1,0:T(8,128)(2,1)S(1)}, bf16[8,256,256]{2,1,0:T(8,128)(2,1)}, u32[]{:S(2)}) copy-start(bf16[8,256,256]{2,1,0:T(8,128)(2,1)} %mixing_ref.1) | copy-start | bytes 3145732
  20.8 6.9 %collective-permute-start.4 = (bf16[240,256]{1,0:T(8,128)(2,1)S(1)}, bf16[240,256]{1,0:T(8,128)(2,1)S(1)}, u32[]{:S(2)}, u32[]{:S(2)}) collective-permute-start(bf16[240,256]{1,0:T(8,128)(2,1)S(1)} %get-tuple-element.16), channel_id=1, source_target_pairs={{0,24},{1,5},{2,26},{3,7},{4,28},{5,1},{6,30},{7,3},{8,16},{9,13},... | collective-permute-start | bytes 368648 | tf_op jit(solution)/shard_map/ppermute | solution.py:335
  24.1 4.9 %collective-permute-start.9 = (bf16[240,256]{1,0:T(8,128)(2,1)S(1)}, bf16[240,256]{1,0:T(8,128)(2,1)S(1)}, u32[]{:S(2)}, u32[]{:S(2)}) collective-permute-start(bf16[240,256]{1,0:T(8,128)(2,1)S(1)} %get-tuple-element.14), channel_id=1, source_target_pairs={{0,8},{1,3},{2,10},{3,1},{4,12},{5,7},{6,14},{7,5},{8,0},{9,11},{1... | collective-permute-start | bytes 368648 | tf_op jit(solution)/shard_map/ppermute | solution.py:335
  29.3 1.3 %collective-permute-start.10 = (bf16[160,256]{1,0:T(8,128)(2,1)S(1)}, bf16[160,256]{1,0:T(8,128)(2,1)S(1)}, u32[]{:S(2)}, u32[]{:S(2)}) collective-permute-start(bf16[160,256]{1,0:T(8,128)(2,1)S(1)} %shard_map.60.mine_ref), channel_id=1, source_target_pairs={{0,1},{1,0},{2,3},{3,2},{4,5},{5,4},{6,7},{7,6},{8,9},{9,8},{10,11... | collective-permute-start | bytes 245768 | tf_op jit(solution)/shard_map/ppermute | solution.py:335

commit v5 on v4

--- a/solution.py
+++ b/solution.py
@@ -132,8 +132,15 @@
     return whole
 
 
+def side_of(index, lon_count):
+    side = index
+    for bit in range(1, lon_count.bit_length() - 2):
+        side = side ^ (index >> bit)
+    return side & 1
+
+
 def fourier_kernel(
-    nlon_total,
+    lon_count,
     where_ref,
     fields_ref,
     legendre_ref,
@@ -153,21 +160,31 @@
     wave_dev, degrees = legendre_ref.shape[:2]
     parts = 2 * degrees
     spec_rows = parts * rows
+    nlon_total = cells * lon_count
     index = where_ref[0]
-    core = lax.rem(index, 2)
+    side = side_of(index, lon_count)
     chunks = [(k, first) for k in range(2) for first in range(0, rows, TILE)]
     copies = []
     for slot, (k, first) in enumerate(chunks):
-        sample = 1 - core if k == 0 else core
+        sample = 1 - side if k == 0 else side
         copies.append(
             pltpu.make_async_copy(
                 fields_ref.at[sample, pl.ds(first, TILE)], grid_ref.at[slot], sems.at[slot]
             )
         )
-    copies.append(pltpu.make_async_copy(legendre_ref, values_ref, sems.at[len(chunks)]))
-    copies.append(pltpu.make_async_copy(cot_ref, cots_ref, sems.at[len(chunks) + 1]))
     for copy in copies:
         copy.start()
+    owns = index < (degrees - 1) // wave_dev + 1
+    others = [
+        pltpu.make_async_copy(legendre_ref, values_ref, sems.at[len(chunks)]),
+        pltpu.make_async_copy(cot_ref, cots_ref, sems.at[len(chunks) + 1]),
+    ]
+
+    @pl.when(owns)
+    def _():
+        for copy in others:
+            copy.start()
+
     width = TILE * cells
     column = lax.broadcasted_iota(jnp.int32, (parts, width), 1)
     part = lax.broadcasted_iota(jnp.int32, (parts, width), 0)
@@ -185,14 +202,24 @@
     wave_lo = (wave - wave_hi.astype(F32)).astype(BF16)
     cut = first_ref.shape[0] // rows
     kept = (parts - cut) * rows
-    for copy in copies[len(chunks) :]:
-        copy.wait()
-    cots = cots_ref[...].astype(F32)
-    real, imag = packed_tiles(wave_dev, index, cots, values_ref, table_ref)
-    second_ref[pl.ds(kept, real.shape[0]), :] = jnp.where(core == 0, real, imag)
-    second_send_ref[pl.ds(kept, real.shape[0]), :] = jnp.where(core == 0, imag, real).astype(BF16)
-
-    for copy in copies[: len(chunks)]:
+    rest = pl.ds(kept, second_ref.shape[0] - kept)
+
+    @pl.when(owns)
+    def _():
+        for copy in others:
+            copy.wait()
+        cots = cots_ref[...].astype(F32)
+        real, imag = packed_tiles(wave_dev, index, cots, values_ref, table_ref)
+        second_ref[rest, :] = jnp.where(side == 0, real, imag)
+        second_send_ref[rest, :] = jnp.where(side == 0, imag, real).astype(BF16)
+
+    @pl.when(jnp.logical_not(owns))
+    def _():
+        second_ref[rest, :] = jnp.zeros((rest.size, channels), F32)
+        second_send_ref[rest, :] = jnp.zeros((rest.size, channels), BF16)
+
+
+    for copy in copies:
         copy.wait()
     for slot, (k, first) in enumerate(chunks):
         grid = grid_ref[slot].astype(F32).reshape(width, channels).astype(BF16)
@@ -243,16 +270,16 @@
 
 
 def mixing_kernel(
-    wave_dev, samples, where_ref, mine_ref, other_ref, mixing_ref, mixed_ref, grad_ref, cot_ref, out_ref
+    lon_count, wave_dev, samples, where_ref, mine_ref, other_ref, mixing_ref, mixed_ref, grad_ref, cot_ref, out_ref
 ):
     degrees, channels = mixing_ref.shape[:2]
     groups = degrees // 2 + 1
     slots = groups * degrees
     terms = 2 * samples * slots
     index = where_ref[0]
-    core = lax.rem(index, 2)
+    side = side_of(index, lon_count)
     mine, other = mine_ref[...].astype(F32), other_ref[...].astype(F32)
-    held = [jnp.where(core == k, mine, other) for k in range(2)]
+    held = [jnp.where(side == k, mine, other) for k in range(2)]
     coef = [held[sample][part * slots : (part + 1) * slots] for part in range(2) for sample in range(2)]
     coef = jnp.concatenate(coef, axis=0).astype(BF16)
     cots = []
@@ -330,8 +357,8 @@
     def in_hbm(array):
         return pltpu.with_memory_space_constraint(array, pltpu.HBM)
 
-    def exchange(array, even, odd):
-        pairs = [(i, i ^ (odd if i % 2 else even)) for i in range(lon_count)]
+    def exchange(array, *hops):
+        pairs = [(i, i ^ hops[side_of(i, lon_count)]) for i in range(lon_count)]
         return lax.ppermute(array, "lon", pairs)
 
     cut = (parts // 2 + 2) * rows
@@ -341,7 +368,7 @@
     chunks = samples * rows // TILE
     far = pl.BlockSpec(memory_space=pltpu.HBM)
     acc_a, acc_b, send_a, send_b = pl.pallas_call(
-        functools.partial(fourier_kernel, cells * lon_count),
+        functools.partial(fourier_kernel, lon_count),
         out_shape=(
             jax.ShapeDtypeStruct((cut, channels), F32),
             jax.ShapeDtypeStruct((rest, channels), F32),
@@ -382,7 +409,7 @@
 
     block_rows = 2 * wave_dev * samples
     mixed, grad = pl.pallas_call(
-        functools.partial(mixing_kernel, wave_dev, samples),
+        functools.partial(mixing_kernel, lon_count, wave_dev, samples),
         out_shape=(
             jax.ShapeDtypeStruct((degrees * block_rows * 2, LANES), BF16),
             jax.ShapeDtypeStruct((channels // lon_count, degrees, channels), F32),
@@ -402,6 +429,7 @@
 def hop_orders(lon_count):
     bits = [1 << k for k in range(1, lon_count.bit_length() - 1)]
     bits[-1] += bits[-2]
+    bits = [bit + 1 for bit in bits]
     half = len(bits) // 2
     near, far = bits[:half], bits[half:]
     chain_a = list(zip(near + far, far + near))

time: 32 us -> 30.2 us (0.944)
  starting transfers between devices: 19.1 us -> 17.2 us
    ppermute x11, starting transfers between devices: 19.1 us -> 17.2 us  [exchange(): return lax.ppermute(array, 'lon', pairs)]
  transfers between devices with their start and end apart: 11 -> 11, of which waited for: 6 -> 7; matrix products, arithmetic and copies ran while one was open for 1% -> 1% of each run, Pallas kernels for 0% -> 0%
where the time goes in v5:
time: 30.2 us; the launch traced here: 30.1 us
  starting transfers between devices  17.2 us (57%)
  waiting for transfers between devices  8.45 us (28%)
  Pallas kernels  3.23 us (11%)
  between operations  0.69 us (2%)
  other arithmetic  0.44 us (1%)
    ppermute x11, starting transfers between devices, exchange(): return lax.ppermute(array, 'lon', pairs)  17.2 us
    ppermute x11, waiting for transfers between devices, exchange(): return lax.ppermute(array, 'lon', pairs)  8.45 us
    pallas_call x1, Pallas kernels, sparse_shards(): pl.pallas_call(functools.partial(fourier_kernel, lon_count), out_shape=(j...  1.82 us
    pallas_call x1, Pallas kernels, sparse_shards(): pl.pallas_call(functools.partial(mixing_kernel, lon_count, wave_dev, samp...  1.16 us
  transfers between devices with their start and end apart: 11, of which 7 were waited for; matrix products, arithmetic and copies ran while one was open for 1% of the time, Pallas kernels for 0%

profile of v5, /device:TPU:0, one launch (start us, length us, event | category | flops | bytes accessed | tf_op | source)
XLA Modules:
  0.0 30.1 jit_solution(3295893014155908046)
XLA Ops:
  0.6 1.8 %shard_map.59 = (f32[240,256]{1,0:T(8,128)S(1)}, f32[240,256]{1,0:T(8,128)S(1)}, bf16[240,256]{1,0:T(8,128)(2,1)S(1)}, bf16[240,256]{1,0:T(8,128)(2,1)S(1)}) custom-call(s32[1]{0:T(128)} %bitcast.where_ref, bf16[2,24,24,256]{3,2,1,0:T(8,128)(2,1)} %fields_ref.1, f32[6,8,24]{2,1,0:T(8,128)} %bitcast.13, bf16[384,128]{1,0:T(8,128)(2,1)} %bitcast.12), custom_call_target="tpu_custom_call" | custom-call | tf_op jit(solution)/shard_map/pallas_call | solution.py:370
  2.5 0.5 %collective-permute-start = (bf16[240,256]{1,0:T(8,128)(2,1)S(1)}, bf16[240,256]{1,0:T(8,128)(2,1)S(1)}, u32[]{:S(2)}, u32[]{:S(2)}) collective-permute-start(bf16[240,256]{1,0:T(8,128)(2,1)S(1)} %get-tuple-element.9), channel_id=1, source_target_pairs={{0,1},{1,0},{2,3},{3,2},{4,5},{5,4},{6,7},{7,6},{8,9},{9,8},{10,11... | collective-permute-start | bytes 368648 | tf_op jit(solution)/shard_map/ppermute | solution.py:362
  3.0 0.1 collective-permute-start.5
  3.1 0.9 %collective-permute-done = bf16[240,256]{1,0:T(8,128)(2,1)S(1)} collective-permute-done((bf16[240,256]{1,0:T(8,128)(2,1)S(1)}, bf16[240,256]{1,0:T(8,128)(2,1)S(1)}, u32[]{:S(2)}, u32[]{:S(2)}) %collective-permute-start) | collective-permute-done | bytes 122912 | tf_op jit(solution)/shard_map/ppermute | solution.py:362
  4.0 2.4 %collective-permute-start.1 = (bf16[240,256]{1,0:T(8,128)(2,1)S(1)}, bf16[240,256]{1,0:T(8,128)(2,1)S(1)}, u32[]{:S(2)}, u32[]{:S(2)}) collective-permute-start(bf16[240,256]{1,0:T(8,128)(2,1)S(1)} %fusion), channel_id=1, source_target_pairs={{0,3},{1,8},{2,11},{3,0},{4,13},{5,6},{6,5},{7,14},{8,1},{9,10},{1... | collective-permute-start | bytes 368648 | tf_op jit(solution)/shard_map/ppermute | solution.py:362
  6.4 0.0 collective-permute-done.5
  6.4 1.5 %collective-permute-start.6 = (bf16[240,256]{1,0:T(8,128)(2,1)S(1)}, bf16[240,256]{1,0:T(8,128)(2,1)S(1)}, u32[]{:S(2)}, u32[]{:S(2)}) collective-permute-start(bf16[240,256]{1,0:T(8,128)(2,1)S(1)} %fusion.2), channel_id=1, source_target_pairs={{0,5},{1,24},{2,27},{3,6},{4,29},{5,0},{6,3},{7,30},{8,17},{9,12},... | collective-permute-start | bytes 368648 | tf_op jit(solution)/shard_map/ppermute | solution.py:362
  8.0 1.0 %collective-permute-done.1 = bf16[240,256]{1,0:T(8,128)(2,1)S(1)} collective-permute-done((bf16[240,256]{1,0:T(8,128)(2,1)S(1)}, bf16[240,256]{1,0:T(8,128)(2,1)S(1)}, u32[]{:S(2)}, u32[]{:S(2)}) %collective-permute-start.1) | collective-permute-done | bytes 122912 | tf_op jit(solution)/shard_map/ppermute | solution.py:362
  9.0 1.8 %collective-permute-start.2 = (bf16[240,256]{1,0:T(8,128)(2,1)S(1)}, bf16[240,256]{1,0:T(8,128)(2,1)S(1)}, u32[]{:S(2)}, u32[]{:S(2)}) collective-permute-start(bf16[240,256]{1,0:T(8,128)(2,1)S(1)} %fusion.4), channel_id=1, source_target_pairs={{0,5},{1,24},{2,27},{3,6},{4,29},{5,0},{6,3},{7,30},{8,17},{9,12},... | collective-permute-start | bytes 368648 | tf_op jit(solution)/shard_map/ppermute | solution.py:362
  10.9 0.0 collective-permute-done.6
  10.9 1.5 %collective-permute-start.7 = (bf16[240,256]{1,0:T(8,128)(2,1)S(1)}, bf16[240,256]{1,0:T(8,128)(2,1)S(1)}, u32[]{:S(2)}, u32[]{:S(2)}) collective-permute-start(bf16[240,256]{1,0:T(8,128)(2,1)S(1)} %fusion.5), channel_id=1, source_target_pairs={{0,3},{1,8},{2,11},{3,0},{4,13},{5,6},{6,5},{7,14},{8,1},{9,10},{1... | collective-permute-start | bytes 368648 | tf_op jit(solution)/shard_map/ppermute | solution.py:362
  12.4 1.0 %collective-permute-done.2 = bf16[240,256]{1,0:T(8,128)(2,1)S(1)} collective-permute-done((bf16[240,256]{1,0:T(8,128)(2,1)S(1)}, bf16[240,256]{1,0:T(8,128)(2,1)S(1)}, u32[]{:S(2)}, u32[]{:S(2)}) %collective-permute-start.2) | collective-permute-done | bytes 122912 | tf_op jit(solution)/shard_map/ppermute | solution.py:362
  13.4 0.1 fusion.1
  13.5 2.4 %collective-permute-start.3 = (bf16[240,256]{1,0:T(8,128)(2,1)S(1)}, bf16[240,256]{1,0:T(8,128)(2,1)S(1)}, u32[]{:S(2)}, u32[]{:S(2)}) collective-permute-start(bf16[240,256]{1,0:T(8,128)(2,1)S(1)} %fusion.1), channel_id=1, source_target_pairs={{0,9},{1,2},{2,1},{3,10},{4,7},{5,12},{6,15},{7,4},{8,11},{9,0},{1... | collective-permute-start | bytes 368648 | tf_op jit(solution)/shard_map/ppermute | solution.py:362
  15.9 0.0 collective-permute-done.7
  15.9 0.1 fusion.3
  16.0 3.5 %collective-permute-start.8 = (bf16[240,256]{1,0:T(8,128)(2,1)S(1)}, bf16[240,256]{1,0:T(8,128)(2,1)S(1)}, u32[]{:S(2)}, u32[]{:S(2)}) collective-permute-start(bf16[240,256]{1,0:T(8,128)(2,1)S(1)} %fusion.3), channel_id=1, source_target_pairs={{0,25},{1,4},{2,7},{3,26},{4,1},{5,28},{6,31},{7,2},{8,13},{9,16},... | collective-permute-start | bytes 368648 | tf_op jit(solution)/shard_map/ppermute | solution.py:362
  19.5 0.0 collective-permute-done.3
  19.5 0.1 fusion.7
  19.6 0.0 copy-start
  19.6 2.2 %collective-permute-start.4 = (bf16[240,256]{1,0:T(8,128)(2,1)S(1)}, bf16[240,256]{1,0:T(8,128)(2,1)S(1)}, u32[]{:S(2)}, u32[]{:S(2)}) collective-permute-start(bf16[240,256]{1,0:T(8,128)(2,1)S(1)} %get-tuple-element.16), channel_id=1, source_target_pairs={{0,25},{1,4},{2,7},{3,26},{4,1},{5,28},{6,31},{7,2},{8,13},{9,16},... | collective-permute-start | bytes 368648 | tf_op jit(solution)/shard_map/ppermute | solution.py:362
  21.8 0.4 %collective-permute-done.8 = bf16[240,256]{1,0:T(8,128)(2,1)S(1)} collective-permute-done((bf16[240,256]{1,0:T(8,128)(2,1)S(1)}, bf16[240,256]{1,0:T(8,128)(2,1)S(1)}, u32[]{:S(2)}, u32[]{:S(2)}) %collective-permute-start.8) | collective-permute-done | bytes 122912 | tf_op jit(solution)/shard_map/ppermute | solution.py:362
  22.3 0.1 fusion.6
  22.4 0.7 %collective-permute-start.9 = (bf16[240,256]{1,0:T(8,128)(2,1)S(1)}, bf16[240,256]{1,0:T(8,128)(2,1)S(1)}, u32[]{:S(2)}, u32[]{:S(2)}) collective-permute-start(bf16[240,256]{1,0:T(8,128)(2,1)S(1)} %get-tuple-element.14), channel_id=1, source_target_pairs={{0,9},{1,2},{2,1},{3,10},{4,7},{5,12},{6,15},{7,4},{8,11},{9,0},{1... | collective-permute-start | bytes 368648 | tf_op jit(solution)/shard_map/ppermute | solution.py:362
  23.0 2.9 %collective-permute-done.4.first_got_ref = bf16[240,256]{1,0:T(8,128)(2,1)S(1)} collective-permute-done((bf16[240,256]{1,0:T(8,128)(2,1)S(1)}, bf16[240,256]{1,0:T(8,128)(2,1)S(1)}, u32[]{:S(2)}, u32[]{:S(2)}) %collective-permute-start.4) | collective-permute-done | bytes 122912 | tf_op jit(solution)/shard_map/ppermute | solution.py:362
  25.9 1.3 %collective-permute-done.9.second_got_ref = bf16[240,256]{1,0:T(8,128)(2,1)S(1)} collective-permute-done((bf16[240,256]{1,0:T(8,128)(2,1)S(1)}, bf16[240,256]{1,0:T(8,128)(2,1)S(1)}, u32[]{:S(2)}, u32[]{:S(2)}) %collective-permute-start.9) | collective-permute-done | bytes 122912 | tf_op jit(solution)/shard_map/ppermute | solution.py:362
  27.2 0.2 shard_map.60.mine_ref
  27.5 0.5 %collective-permute-start.10 = (bf16[160,256]{1,0:T(8,128)(2,1)S(1)}, bf16[160,256]{1,0:T(8,128)(2,1)S(1)}, u32[]{:S(2)}, u32[]{:S(2)}) collective-permute-start(bf16[160,256]{1,0:T(8,128)(2,1)S(1)} %shard_map.60.mine_ref), channel_id=1, source_target_pairs={{0,1},{1,0},{2,3},{3,2},{4,5},{5,4},{6,7},{7,6},{8,9},{9,8},{10,11... | collective-permute-start | bytes 245768 | tf_op jit(solution)/shard_map/ppermute | solution.py:362
  28.0 0.9 %collective-permute-done.10.other_ref = bf16[160,256]{1,0:T(8,128)(2,1)S(1)} collective-permute-done((bf16[160,256]{1,0:T(8,128)(2,1)S(1)}, bf16[160,256]{1,0:T(8,128)(2,1)S(1)}, u32[]{:S(2)}, u32[]{:S(2)}) %collective-permute-start.10) | collective-permute-done | bytes 81952 | tf_op jit(solution)/shard_map/ppermute | solution.py:362
  28.9 0.0 copy-done
  28.9 1.2 %shard_map.61 = (bf16[384,128]{1,0:T(8,128)(2,1)}, f32[8,8,256]{2,1,0:T(8,128)}) custom-call(s32[1]{0:T(128)} %bitcast.where_ref, bf16[160,256]{1,0:T(8,128)(2,1)S(1)} %shard_map.60.mine_ref, bf16[160,256]{1,0:T(8,128)(2,1)S(1)} %collective-permute-done.10.other_ref, bf16[8,256,256]{2,1,0:T(8,128)(2,1)S(1)} %copy-done), custom_call_target="tpu_custom_call" | custom-call | tf_op jit(solution)/shard_map/pallas_call | solution.py:411
  (4 shorter events, 0.1 us)
Async XLA Ops:
  2.5 1.5 %collective-permute-start = (bf16[240,256]{1,0:T(8,128)(2,1)S(1)}, bf16[240,256]{1,0:T(8,128)(2,1)S(1)}, u32[]{:S(2)}, u32[]{:S(2)}) collective-permute-start(bf16[240,256]{1,0:T(8,128)(2,1)S(1)} %get-tuple-element.9), channel_id=1, source_target_pairs={{0,1},{1,0},{2,3},{3,2},{4,5},{5,4},{6,7},{7,6},{8,9},{9,8},{10,11... | collective-permute-start | bytes 368648 | tf_op jit(solution)/shard_map/ppermute | solution.py:362
  3.0 3.4 %collective-permute-start.5 = (bf16[240,256]{1,0:T(8,128)(2,1)S(1)}, bf16[240,256]{1,0:T(8,128)(2,1)S(1)}, u32[]{:S(2)}, u32[]{:S(2)}) collective-permute-start(bf16[240,256]{1,0:T(8,128)(2,1)S(1)} %get-tuple-element.11), channel_id=1, source_target_pairs={{0,1},{1,0},{2,3},{3,2},{4,5},{5,4},{6,7},{7,6},{8,9},{9,8},{10,11... | collective-permute-start | bytes 368648 | tf_op jit(solution)/shard_map/ppermute | solution.py:362
  4.0 5.0 %collective-permute-start.1 = (bf16[240,256]{1,0:T(8,128)(2,1)S(1)}, bf16[240,256]{1,0:T(8,128)(2,1)S(1)}, u32[]{:S(2)}, u32[]{:S(2)}) collective-permute-start(bf16[240,256]{1,0:T(8,128)(2,1)S(1)} %fusion), channel_id=1, source_target_pairs={{0,3},{1,8},{2,11},{3,0},{4,13},{5,6},{6,5},{7,14},{8,1},{9,10},{1... | collective-permute-start | bytes 368648 | tf_op jit(solution)/shard_map/ppermute | solution.py:362
  6.4 4.4 %collective-permute-start.6 = (bf16[240,256]{1,0:T(8,128)(2,1)S(1)}, bf16[240,256]{1,0:T(8,128)(2,1)S(1)}, u32[]{:S(2)}, u32[]{:S(2)}) collective-permute-start(bf16[240,256]{1,0:T(8,128)(2,1)S(1)} %fusion.2), channel_id=1, source_target_pairs={{0,5},{1,24},{2,27},{3,6},{4,29},{5,0},{6,3},{7,30},{8,17},{9,12},... | collective-permute-start | bytes 368648 | tf_op jit(solution)/shard_map/ppermute | solution.py:362
  9.0 4.4 %collective-permute-start.2 = (bf16[240,256]{1,0:T(8,128)(2,1)S(1)}, bf16[240,256]{1,0:T(8,128)(2,1)S(1)}, u32[]{:S(2)}, u32[]{:S(2)}) collective-permute-start(bf16[240,256]{1,0:T(8,128)(2,1)S(1)} %fusion.4), channel_id=1, source_target_pairs={{0,5},{1,24},{2,27},{3,6},{4,29},{5,0},{6,3},{7,30},{8,17},{9,12},... | collective-permute-start | bytes 368648 | tf_op jit(solution)/shard_map/ppermute | solution.py:362
  10.9 5.0 %collective-permute-start.7 = (bf16[240,256]{1,0:T(8,128)(2,1)S(1)}, bf16[240,256]{1,0:T(8,128)(2,1)S(1)}, u32[]{:S(2)}, u32[]{:S(2)}) collective-permute-start(bf16[240,256]{1,0:T(8,128)(2,1)S(1)} %fusion.5), channel_id=1, source_target_pairs={{0,3},{1,8},{2,11},{3,0},{4,13},{5,6},{6,5},{7,14},{8,1},{9,10},{1... | collective-permute-start | bytes 368648 | tf_op jit(solution)/shard_map/ppermute | solution.py:362
  13.5 6.0 %collective-permute-start.3 = (bf16[240,256]{1,0:T(8,128)(2,1)S(1)}, bf16[240,256]{1,0:T(8,128)(2,1)S(1)}, u32[]{:S(2)}, u32[]{:S(2)}) collective-permute-start(bf16[240,256]{1,0:T(8,128)(2,1)S(1)} %fusion.1), channel_id=1, source_target_pairs={{0,9},{1,2},{2,1},{3,10},{4,7},{5,12},{6,15},{7,4},{8,11},{9,0},{1... | collective-permute-start | bytes 368648 | tf_op jit(solution)/shard_map/ppermute | solution.py:362
  16.0 6.3 %collective-permute-start.8 = (bf16[240,256]{1,0:T(8,128)(2,1)S(1)}, bf16[240,256]{1,0:T(8,128)(2,1)S(1)}, u32[]{:S(2)}, u32[]{:S(2)}) collective-permute-start(bf16[240,256]{1,0:T(8,128)(2,1)S(1)} %fusion.3), channel_id=1, source_target_pairs={{0,25},{1,4},{2,7},{3,26},{4,1},{5,28},{6,31},{7,2},{8,13},{9,16},... | collective-permute-start | bytes 368648 | tf_op jit(solution)/shard_map/ppermute | solution.py:362
  19.6 9.3 %copy-start = (bf16[8,256,256]{2,1,0:T(8,128)(2,1)S(1)}, bf16[8,256,256]{2,1,0:T(8,128)(2,1)}, u32[]{:S(2)}) copy-start(bf16[8,256,256]{2,1,0:T(8,128)(2,1)} %mixing_ref.1) | copy-start | bytes 3145732
  19.6 6.3 %collective-permute-start.4 = (bf16[240,256]{1,0:T(8,128)(2,1)S(1)}, bf16[240,256]{1,0:T(8,128)(2,1)S(1)}, u32[]{:S(2)}, u32[]{:S(2)}) collective-permute-start(bf16[240,256]{1,0:T(8,128)(2,1)S(1)} %get-tuple-element.16), channel_id=1, source_target_pairs={{0,25},{1,4},{2,7},{3,26},{4,1},{5,28},{6,31},{7,2},{8,13},{9,16},... | collective-permute-start | bytes 368648 | tf_op jit(solution)/shard_map/ppermute | solution.py:362
  22.4 4.8 %collective-permute-start.9 = (bf16[240,256]{1,0:T(8,128)(2,1)S(1)}, bf16[240,256]{1,0:T(8,128)(2,1)S(1)}, u32[]{:S(2)}, u32[]{:S(2)}) collective-permute-start(bf16[240,256]{1,0:T(8,128)(2,1)S(1)} %get-tuple-element.14), channel_id=1, source_target_pairs={{0,9},{1,2},{2,1},{3,10},{4,7},{5,12},{6,15},{7,4},{8,11},{9,0},{1... | collective-permute-start | bytes 368648 | tf_op jit(solution)/shard_map/ppermute | solution.py:362
  27.5 1.4 %collective-permute-start.10 = (bf16[160,256]{1,0:T(8,128)(2,1)S(1)}, bf16[160,256]{1,0:T(8,128)(2,1)S(1)}, u32[]{:S(2)}, u32[]{:S(2)}) collective-permute-start(bf16[160,256]{1,0:T(8,128)(2,1)S(1)} %shard_map.60.mine_ref), channel_id=1, source_target_pairs={{0,1},{1,0},{2,3},{3,2},{4,5},{5,4},{6,7},{7,6},{8,9},{9,8},{10,11... | collective-permute-start | bytes 245768 | tf_op jit(solution)/shard_map/ppermute | solution.py:362

commit v6 on v5

--- a/solution.py
+++ b/solution.py
@@ -163,21 +163,16 @@
     nlon_total = cells * lon_count
     index = where_ref[0]
     side = side_of(index, lon_count)
-    chunks = [(k, first) for k in range(2) for first in range(0, rows, TILE)]
-    copies = []
-    for slot, (k, first) in enumerate(chunks):
-        sample = 1 - side if k == 0 else side
-        copies.append(
-            pltpu.make_async_copy(
-                fields_ref.at[sample, pl.ds(first, TILE)], grid_ref.at[slot], sems.at[slot]
-            )
-        )
+    copies = [
+        pltpu.make_async_copy(fields_ref.at[sample], grid_ref.at[k], sems.at[k])
+        for k, sample in enumerate((1 - side, side))
+    ]
     for copy in copies:
         copy.start()
     owns = index < (degrees - 1) // wave_dev + 1
     others = [
-        pltpu.make_async_copy(legendre_ref, values_ref, sems.at[len(chunks)]),
-        pltpu.make_async_copy(cot_ref, cots_ref, sems.at[len(chunks) + 1]),
+        pltpu.make_async_copy(legendre_ref, values_ref, sems.at[2]),
+        pltpu.make_async_copy(cot_ref, cots_ref, sems.at[3]),
     ]
 
     @pl.when(owns)
@@ -221,8 +216,8 @@
 
     for copy in copies:
         copy.wait()
-    for slot, (k, first) in enumerate(chunks):
-        grid = grid_ref[slot].astype(F32).reshape(width, channels).astype(BF16)
+    for k, first in [(k, first) for k in range(2) for first in range(0, rows, TILE)]:
+        grid = grid_ref[k, pl.ds(first, TILE)].astype(F32).reshape(width, channels).astype(BF16)
         sums = jnp.dot(wave_hi, grid, preferred_element_type=F32)
         sums = sums + jnp.dot(wave_lo, grid, preferred_element_type=F32)
         for part in range(parts):
@@ -361,11 +356,10 @@
         pairs = [(i, i ^ hops[side_of(i, lon_count)]) for i in range(lon_count)]
         return lax.ppermute(array, "lon", pairs)
 
-    cut = (parts // 2 + 2) * rows
+    cut = (parts // 2 + 3) * rows
     rest = spec_rows - cut + packed_rows + 2 * TILE
     halves = cotangent.reshape(degrees, wave_dev, 2, samples, 2, LANES)
     halves = halves.transpose(0, 1, 2, 4, 3, 5).reshape(-1, LANES)
-    chunks = samples * rows // TILE
     far = pl.BlockSpec(memory_space=pltpu.HBM)
     acc_a, acc_b, send_a, send_b = pl.pallas_call(
         functools.partial(fourier_kernel, lon_count),
@@ -378,12 +372,12 @@
         in_specs=[scalar, far, far, far],
         out_specs=(whole, whole, whole, whole),
         scratch_shapes=[
-            pltpu.VMEM((chunks, TILE, cells, channels), BF16),
+            pltpu.VMEM(fields.shape, BF16),
             pltpu.VMEM((wave_dev, degrees, rows), F32),
             pltpu.VMEM(halves.shape, BF16),
             pltpu.VMEM((spec_rows, channels), F32),
             pltpu.VMEM((wave_dev, degrees, LANES), F32),
-            pltpu.SemaphoreType.DMA((chunks + 2,)),
+            pltpu.SemaphoreType.DMA((4,)),
         ],
         compiler_params=params,
     )(where, in_hbm(fields), in_hbm(legendre.transpose(1, 2, 0)), in_hbm(halves))
@@ -432,8 +426,10 @@
     bits = [bit + 1 for bit in bits]
     half = len(bits) // 2
     near, far = bits[:half], bits[half:]
-    chain_a = list(zip(near + far, far + near))
-    chain_b = list(zip(near[::-1] + far[::-1], far[::-1] + near[::-1]))
+    one = [hop for pair in zip(near, far) for hop in pair]
+    two = [hop for pair in zip(far, near) for hop in pair]
+    chain_a = list(zip(one, two))
+    chain_b = list(zip(one[half:] + one[:half][::-1], two[half:] + two[:half][::-1]))
     return chain_a, chain_b
 
 
@@ -446,6 +442,7 @@
         and samples == 2
         and count >= 8
         and count & (count - 1) == 0
+        and count.bit_length() % 2 == 0
         and degrees == TILE
         and degrees <= waves
         and rows % TILE == 0

time: 30.2 us -> 29.7 us (0.983)
  starting transfers between devices: 17.2 us -> 16 us
  waiting for transfers between devices: 8.45 us -> 9.27 us
    ppermute x11, starting transfers between devices: 17.2 us -> 16 us  [exchange(): return lax.ppermute(array, 'lon', pairs)]
    ppermute x11, waiting for transfers between devices: 8.45 us -> 9.27 us  [exchange(): return lax.ppermute(array, 'lon', pairs)]
  transfers between devices with their start and end apart: 11 -> 11, of which waited for: 7 -> 6; matrix products, arithmetic and copies ran while one was open for 1% -> 1% of each run, Pallas kernels for 0% -> 0%
where the time goes in v6:
time: 29.7 us; the launch traced here: 29.5 us
  starting transfers between devices  16 us (54%)
  waiting for transfers between devices  9.27 us (31%)
  Pallas kernels  3.08 us (10%)
  between operations  0.69 us (2%)
  other arithmetic  0.42 us (1%)
    ppermute x11, starting transfers between devices, exchange(): return lax.ppermute(array, 'lon', pairs)  16 us
    ppermute x11, waiting for transfers between devices, exchange(): return lax.ppermute(array, 'lon', pairs)  9.27 us
    pallas_call x1, Pallas kernels, sparse_shards(): pl.pallas_call(functools.partial(fourier_kernel, lon_count), out_shape=(j...  1.67 us
    pallas_call x1, Pallas kernels, sparse_shards(): pl.pallas_call(functools.partial(mixing_kernel, lon_count, wave_dev, samp...  1.16 us
  transfers between devices with their start and end apart: 11, of which 6 were waited for; matrix products, arithmetic and copies ran while one was open for 1% of the time, Pallas kernels for 0%

profile of v6, /device:TPU:0, one launch (start us, length us, event | category | flops | bytes accessed | tf_op | source)
XLA Modules:
  0.0 29.5 jit_solution(13583342124702602716)
XLA Ops:
  0.6 1.7 %shard_map.59 = (f32[264,256]{1,0:T(8,128)S(1)}, f32[216,256]{1,0:T(8,128)S(1)}, bf16[264,256]{1,0:T(8,128)(2,1)S(1)}, bf16[216,256]{1,0:T(8,128)(2,1)S(1)}) custom-call(s32[1]{0:T(128)} %bitcast.where_ref, bf16[2,24,24,256]{3,2,1,0:T(8,128)(2,1)} %fields_ref.1, f32[6,8,24]{2,1,0:T(8,128)} %bitcast.13, bf16[384,128]{1,0:T(8,128)(2,1)} %bitcast.12), custom_call_target="tpu_custom_call" | custom-call | tf_op jit(solution)/shard_map/pallas_call | solution.py:364
  2.3 0.5 %collective-permute-start = (bf16[264,256]{1,0:T(8,128)(2,1)S(1)}, bf16[264,256]{1,0:T(8,128)(2,1)S(1)}, u32[]{:S(2)}, u32[]{:S(2)}) collective-permute-start(bf16[264,256]{1,0:T(8,128)(2,1)S(1)} %get-tuple-element.9), channel_id=1, source_target_pairs={{0,1},{1,0},{2,3},{3,2},{4,5},{5,4},{6,7},{7,6},{8,9},{9,8},{10,11... | collective-permute-start | bytes 405512 | tf_op jit(solution)/shard_map/ppermute | solution.py:357
  2.8 0.1 collective-permute-start.5
  2.9 0.9 %collective-permute-done = bf16[264,256]{1,0:T(8,128)(2,1)S(1)} collective-permute-done((bf16[264,256]{1,0:T(8,128)(2,1)S(1)}, bf16[264,256]{1,0:T(8,128)(2,1)S(1)}, u32[]{:S(2)}, u32[]{:S(2)}) %collective-permute-start) | collective-permute-done | bytes 135200 | tf_op jit(solution)/shard_map/ppermute | solution.py:357
  3.8 2.5 %collective-permute-start.1 = (bf16[264,256]{1,0:T(8,128)(2,1)S(1)}, bf16[264,256]{1,0:T(8,128)(2,1)S(1)}, u32[]{:S(2)}, u32[]{:S(2)}) collective-permute-start(bf16[264,256]{1,0:T(8,128)(2,1)S(1)} %fusion), channel_id=1, source_target_pairs={{0,3},{1,8},{2,11},{3,0},{4,13},{5,6},{6,5},{7,14},{8,1},{9,10},{1... | collective-permute-start | bytes 405512 | tf_op jit(solution)/shard_map/ppermute | solution.py:357
  6.3 0.0 collective-permute-done.5
  6.3 1.6 %collective-permute-start.6 = (bf16[216,256]{1,0:T(8,128)(2,1)S(1)}, bf16[216,256]{1,0:T(8,128)(2,1)S(1)}, u32[]{:S(2)}, u32[]{:S(2)}) collective-permute-start(bf16[216,256]{1,0:T(8,128)(2,1)S(1)} %fusion.2), channel_id=1, source_target_pairs={{0,5},{1,24},{2,27},{3,6},{4,29},{5,0},{6,3},{7,30},{8,17},{9,12},... | collective-permute-start | bytes 331784 | tf_op jit(solution)/shard_map/ppermute | solution.py:357
  7.9 1.1 %collective-permute-done.1 = bf16[264,256]{1,0:T(8,128)(2,1)S(1)} collective-permute-done((bf16[264,256]{1,0:T(8,128)(2,1)S(1)}, bf16[264,256]{1,0:T(8,128)(2,1)S(1)}, u32[]{:S(2)}, u32[]{:S(2)}) %collective-permute-start.1) | collective-permute-done | bytes 135200 | tf_op jit(solution)/shard_map/ppermute | solution.py:357
  9.1 2.2 %collective-permute-start.2 = (bf16[264,256]{1,0:T(8,128)(2,1)S(1)}, bf16[264,256]{1,0:T(8,128)(2,1)S(1)}, u32[]{:S(2)}, u32[]{:S(2)}) collective-permute-start(bf16[264,256]{1,0:T(8,128)(2,1)S(1)} %fusion.5), channel_id=1, source_target_pairs={{0,9},{1,2},{2,1},{3,10},{4,7},{5,12},{6,15},{7,4},{8,11},{9,0},{1... | collective-permute-start | bytes 405512 | tf_op jit(solution)/shard_map/ppermute | solution.py:357
  11.2 0.0 collective-permute-done.6
  11.3 3.3 %collective-permute-start.7 = (bf16[216,256]{1,0:T(8,128)(2,1)S(1)}, bf16[216,256]{1,0:T(8,128)(2,1)S(1)}, u32[]{:S(2)}, u32[]{:S(2)}) collective-permute-start(bf16[216,256]{1,0:T(8,128)(2,1)S(1)} %fusion.4), channel_id=1, source_target_pairs={{0,25},{1,4},{2,7},{3,26},{4,1},{5,28},{6,31},{7,2},{8,13},{9,16},... | collective-permute-start | bytes 331784 | tf_op jit(solution)/shard_map/ppermute | solution.py:357
  14.6 0.0 collective-permute-done.2
  14.6 0.1 fusion.1
  14.6 1.0 %collective-permute-start.3 = (bf16[264,256]{1,0:T(8,128)(2,1)S(1)}, bf16[264,256]{1,0:T(8,128)(2,1)S(1)}, u32[]{:S(2)}, u32[]{:S(2)}) collective-permute-start(bf16[264,256]{1,0:T(8,128)(2,1)S(1)} %fusion.1), channel_id=1, source_target_pairs={{0,5},{1,24},{2,27},{3,6},{4,29},{5,0},{6,3},{7,30},{8,17},{9,12},... | collective-permute-start | bytes 405512 | tf_op jit(solution)/shard_map/ppermute | solution.py:357
  15.7 1.8 %collective-permute-done.7 = bf16[216,256]{1,0:T(8,128)(2,1)S(1)} collective-permute-done((bf16[216,256]{1,0:T(8,128)(2,1)S(1)}, bf16[216,256]{1,0:T(8,128)(2,1)S(1)}, u32[]{:S(2)}, u32[]{:S(2)}) %collective-permute-start.7) | collective-permute-done | bytes 110624 | tf_op jit(solution)/shard_map/ppermute | solution.py:357
  17.4 0.1 fusion.3
  17.5 0.2 collective-permute-start.8
  17.7 1.4 %collective-permute-done.3 = bf16[264,256]{1,0:T(8,128)(2,1)S(1)} collective-permute-done((bf16[264,256]{1,0:T(8,128)(2,1)S(1)}, bf16[264,256]{1,0:T(8,128)(2,1)S(1)}, u32[]{:S(2)}, u32[]{:S(2)}) %collective-permute-start.3) | collective-permute-done | bytes 135200 | tf_op jit(solution)/shard_map/ppermute | solution.py:357
  19.1 0.1 fusion.7
  19.2 0.0 copy-start
  19.2 3.2 %collective-permute-start.4 = (bf16[264,256]{1,0:T(8,128)(2,1)S(1)}, bf16[264,256]{1,0:T(8,128)(2,1)S(1)}, u32[]{:S(2)}, u32[]{:S(2)}) collective-permute-start(bf16[264,256]{1,0:T(8,128)(2,1)S(1)} %get-tuple-element.16), channel_id=1, source_target_pairs={{0,25},{1,4},{2,7},{3,26},{4,1},{5,28},{6,31},{7,2},{8,13},{9,16},... | collective-permute-start | bytes 405512 | tf_op jit(solution)/shard_map/ppermute | solution.py:357
  22.4 0.0 collective-permute-done.8
  22.4 0.1 fusion.6
  22.5 1.2 %collective-permute-start.9 = (bf16[216,256]{1,0:T(8,128)(2,1)S(1)}, bf16[216,256]{1,0:T(8,128)(2,1)S(1)}, u32[]{:S(2)}, u32[]{:S(2)}) collective-permute-start(bf16[216,256]{1,0:T(8,128)(2,1)S(1)} %get-tuple-element.14), channel_id=1, source_target_pairs={{0,3},{1,8},{2,11},{3,0},{4,13},{5,6},{6,5},{7,14},{8,1},{9,10},{1... | collective-permute-start | bytes 331784 | tf_op jit(solution)/shard_map/ppermute | solution.py:357
  23.7 3.0 %collective-permute-done.9.second_got_ref = bf16[216,256]{1,0:T(8,128)(2,1)S(1)} collective-permute-done((bf16[216,256]{1,0:T(8,128)(2,1)S(1)}, bf16[216,256]{1,0:T(8,128)(2,1)S(1)}, u32[]{:S(2)}, u32[]{:S(2)}) %collective-permute-start.9) | collective-permute-done | bytes 110624 | tf_op jit(solution)/shard_map/ppermute | solution.py:357
  26.7 0.0 collective-permute-done.4.first_got_ref
  26.8 0.2 shard_map.60.mine_ref
  27.0 0.3 collective-permute-start.10
  27.3 1.1 %collective-permute-done.10.other_ref = bf16[160,256]{1,0:T(8,128)(2,1)S(1)} collective-permute-done((bf16[160,256]{1,0:T(8,128)(2,1)S(1)}, bf16[160,256]{1,0:T(8,128)(2,1)S(1)}, u32[]{:S(2)}, u32[]{:S(2)}) %collective-permute-start.10) | collective-permute-done | bytes 81952 | tf_op jit(solution)/shard_map/ppermute | solution.py:357
  28.4 0.0 copy-done
  28.4 1.2 %shard_map.61 = (bf16[384,128]{1,0:T(8,128)(2,1)}, f32[8,8,256]{2,1,0:T(8,128)}) custom-call(s32[1]{0:T(128)} %bitcast.where_ref, bf16[160,256]{1,0:T(8,128)(2,1)S(1)} %shard_map.60.mine_ref, bf16[160,256]{1,0:T(8,128)(2,1)S(1)} %collective-permute-done.10.other_ref, bf16[8,256,256]{2,1,0:T(8,128)(2,1)S(1)} %copy-done), custom_call_target="tpu_custom_call" | custom-call | tf_op jit(solution)/shard_map/pallas_call | solution.py:405
  (4 shorter events, 0.1 us)
Async XLA Ops:
  2.3 1.5 %collective-permute-start = (bf16[264,256]{1,0:T(8,128)(2,1)S(1)}, bf16[264,256]{1,0:T(8,128)(2,1)S(1)}, u32[]{:S(2)}, u32[]{:S(2)}) collective-permute-start(bf16[264,256]{1,0:T(8,128)(2,1)S(1)} %get-tuple-element.9), channel_id=1, source_target_pairs={{0,1},{1,0},{2,3},{3,2},{4,5},{5,4},{6,7},{7,6},{8,9},{9,8},{10,11... | collective-permute-start | bytes 405512 | tf_op jit(solution)/shard_map/ppermute | solution.py:357
  2.8 3.5 %collective-permute-start.5 = (bf16[216,256]{1,0:T(8,128)(2,1)S(1)}, bf16[216,256]{1,0:T(8,128)(2,1)S(1)}, u32[]{:S(2)}, u32[]{:S(2)}) collective-permute-start(bf16[216,256]{1,0:T(8,128)(2,1)S(1)} %get-tuple-element.11), channel_id=1, source_target_pairs={{0,1},{1,0},{2,3},{3,2},{4,5},{5,4},{6,7},{7,6},{8,9},{9,8},{10,11... | collective-permute-start | bytes 331784 | tf_op jit(solution)/shard_map/ppermute | solution.py:357
  3.8 5.2 %collective-permute-start.1 = (bf16[264,256]{1,0:T(8,128)(2,1)S(1)}, bf16[264,256]{1,0:T(8,128)(2,1)S(1)}, u32[]{:S(2)}, u32[]{:S(2)}) collective-permute-start(bf16[264,256]{1,0:T(8,128)(2,1)S(1)} %fusion), channel_id=1, source_target_pairs={{0,3},{1,8},{2,11},{3,0},{4,13},{5,6},{6,5},{7,14},{8,1},{9,10},{1... | collective-permute-start | bytes 405512 | tf_op jit(solution)/shard_map/ppermute | solution.py:357
  6.3 4.9 %collective-permute-start.6 = (bf16[216,256]{1,0:T(8,128)(2,1)S(1)}, bf16[216,256]{1,0:T(8,128)(2,1)S(1)}, u32[]{:S(2)}, u32[]{:S(2)}) collective-permute-start(bf16[216,256]{1,0:T(8,128)(2,1)S(1)} %fusion.2), channel_id=1, source_target_pairs={{0,5},{1,24},{2,27},{3,6},{4,29},{5,0},{6,3},{7,30},{8,17},{9,12},... | collective-permute-start | bytes 331784 | tf_op jit(solution)/shard_map/ppermute | solution.py:357
  9.1 5.5 %collective-permute-start.2 = (bf16[264,256]{1,0:T(8,128)(2,1)S(1)}, bf16[264,256]{1,0:T(8,128)(2,1)S(1)}, u32[]{:S(2)}, u32[]{:S(2)}) collective-permute-start(bf16[264,256]{1,0:T(8,128)(2,1)S(1)} %fusion.5), channel_id=1, source_target_pairs={{0,9},{1,2},{2,1},{3,10},{4,7},{5,12},{6,15},{7,4},{8,11},{9,0},{1... | collective-permute-start | bytes 405512 | tf_op jit(solution)/shard_map/ppermute | solution.py:357
  11.3 6.1 %collective-permute-start.7 = (bf16[216,256]{1,0:T(8,128)(2,1)S(1)}, bf16[216,256]{1,0:T(8,128)(2,1)S(1)}, u32[]{:S(2)}, u32[]{:S(2)}) collective-permute-start(bf16[216,256]{1,0:T(8,128)(2,1)S(1)} %fusion.4), channel_id=1, source_target_pairs={{0,25},{1,4},{2,7},{3,26},{4,1},{5,28},{6,31},{7,2},{8,13},{9,16},... | collective-permute-start | bytes 331784 | tf_op jit(solution)/shard_map/ppermute | solution.py:357
  14.6 4.5 %collective-permute-start.3 = (bf16[264,256]{1,0:T(8,128)(2,1)S(1)}, bf16[264,256]{1,0:T(8,128)(2,1)S(1)}, u32[]{:S(2)}, u32[]{:S(2)}) collective-permute-start(bf16[264,256]{1,0:T(8,128)(2,1)S(1)} %fusion.1), channel_id=1, source_target_pairs={{0,5},{1,24},{2,27},{3,6},{4,29},{5,0},{6,3},{7,30},{8,17},{9,12},... | collective-permute-start | bytes 405512 | tf_op jit(solution)/shard_map/ppermute | solution.py:357
  17.5 4.9 %collective-permute-start.8 = (bf16[216,256]{1,0:T(8,128)(2,1)S(1)}, bf16[216,256]{1,0:T(8,128)(2,1)S(1)}, u32[]{:S(2)}, u32[]{:S(2)}) collective-permute-start(bf16[216,256]{1,0:T(8,128)(2,1)S(1)} %fusion.3), channel_id=1, source_target_pairs={{0,9},{1,2},{2,1},{3,10},{4,7},{5,12},{6,15},{7,4},{8,11},{9,0},{1... | collective-permute-start | bytes 331784 | tf_op jit(solution)/shard_map/ppermute | solution.py:357
  19.2 9.1 %copy-start = (bf16[8,256,256]{2,1,0:T(8,128)(2,1)S(1)}, bf16[8,256,256]{2,1,0:T(8,128)(2,1)}, u32[]{:S(2)}) copy-start(bf16[8,256,256]{2,1,0:T(8,128)(2,1)} %mixing_ref.1) | copy-start | bytes 3145732
  19.2 7.5 %collective-permute-start.4 = (bf16[264,256]{1,0:T(8,128)(2,1)S(1)}, bf16[264,256]{1,0:T(8,128)(2,1)S(1)}, u32[]{:S(2)}, u32[]{:S(2)}) collective-permute-start(bf16[264,256]{1,0:T(8,128)(2,1)S(1)} %get-tuple-element.16), channel_id=1, source_target_pairs={{0,25},{1,4},{2,7},{3,26},{4,1},{5,28},{6,31},{7,2},{8,13},{9,16},... | collective-permute-start | bytes 405512 | tf_op jit(solution)/shard_map/ppermute | solution.py:357
  22.5 4.2 %collective-permute-start.9 = (bf16[216,256]{1,0:T(8,128)(2,1)S(1)}, bf16[216,256]{1,0:T(8,128)(2,1)S(1)}, u32[]{:S(2)}, u32[]{:S(2)}) collective-permute-start(bf16[216,256]{1,0:T(8,128)(2,1)S(1)} %get-tuple-element.14), channel_id=1, source_target_pairs={{0,3},{1,8},{2,11},{3,0},{4,13},{5,6},{6,5},{7,14},{8,1},{9,10},{1... | collective-permute-start | bytes 331784 | tf_op jit(solution)/shard_map/ppermute | solution.py:357
  27.0 1.3 %collective-permute-start.10 = (bf16[160,256]{1,0:T(8,128)(2,1)S(1)}, bf16[160,256]{1,0:T(8,128)(2,1)S(1)}, u32[]{:S(2)}, u32[]{:S(2)}) collective-permute-start(bf16[160,256]{1,0:T(8,128)(2,1)S(1)} %shard_map.60.mine_ref), channel_id=1, source_target_pairs={{0,1},{1,0},{2,3},{3,2},{4,5},{5,4},{6,7},{7,6},{8,9},{9,8},{10,11... | collective-permute-start | bytes 245768 | tf_op jit(solution)/shard_map/ppermute | solution.py:357

commit v7 on v6

--- a/solution.py
+++ b/solution.py
@@ -156,8 +156,9 @@
     table_ref,
     sems,
 ):
-    rows, cells, channels = fields_ref.shape[1:]
-    wave_dev, degrees = legendre_ref.shape[:2]
+    channels = fields_ref.shape[2]
+    wave_dev, degrees, rows = legendre_ref.shape
+    cells = fields_ref.shape[1] // rows
     parts = 2 * degrees
     spec_rows = parts * rows
     nlon_total = cells * lon_count
@@ -206,18 +207,17 @@
         cots = cots_ref[...].astype(F32)
         real, imag = packed_tiles(wave_dev, index, cots, values_ref, table_ref)
         second_ref[rest, :] = jnp.where(side == 0, real, imag)
-        second_send_ref[rest, :] = jnp.where(side == 0, imag, real).astype(BF16)
+        total_ref[pl.ds(spec_rows, rest.size), :] = jnp.where(side == 0, imag, real)
 
     @pl.when(jnp.logical_not(owns))
     def _():
         second_ref[rest, :] = jnp.zeros((rest.size, channels), F32)
-        second_send_ref[rest, :] = jnp.zeros((rest.size, channels), BF16)
-
+        total_ref[pl.ds(spec_rows, rest.size), :] = jnp.zeros((rest.size, channels), F32)
 
     for copy in copies:
         copy.wait()
     for k, first in [(k, first) for k in range(2) for first in range(0, rows, TILE)]:
-        grid = grid_ref[k, pl.ds(first, TILE)].astype(F32).reshape(width, channels).astype(BF16)
+        grid = grid_ref[k, pl.ds(first * cells, width), :]
         sums = jnp.dot(wave_hi, grid, preferred_element_type=F32)
         sums = sums + jnp.dot(wave_lo, grid, preferred_element_type=F32)
         for part in range(parts):
@@ -230,7 +230,8 @@
                 second_ref[pl.ds((part - cut) * rows + first, TILE), :] = tile
         if k == 0 and first + TILE == rows:
             first_send_ref[...] = total_ref[pl.ds(0, cut * rows), :].astype(BF16)
-            second_send_ref[pl.ds(0, kept), :] = total_ref[pl.ds(cut * rows, kept), :].astype(BF16)
+            after = pl.ds(cut * rows, second_send_ref.shape[0])
+            second_send_ref[...] = total_ref[after, :].astype(BF16)
 
 
 def legendre_kernel(
@@ -360,6 +361,7 @@
     rest = spec_rows - cut + packed_rows + 2 * TILE
     halves = cotangent.reshape(degrees, wave_dev, 2, samples, 2, LANES)
     halves = halves.transpose(0, 1, 2, 4, 3, 5).reshape(-1, LANES)
+    grid = fields.reshape(samples, rows * cells, channels)
     far = pl.BlockSpec(memory_space=pltpu.HBM)
     acc_a, acc_b, send_a, send_b = pl.pallas_call(
         functools.partial(fourier_kernel, lon_count),
@@ -372,15 +374,15 @@
         in_specs=[scalar, far, far, far],
         out_specs=(whole, whole, whole, whole),
         scratch_shapes=[
-            pltpu.VMEM(fields.shape, BF16),
+            pltpu.VMEM((samples, rows * cells, channels), BF16),
             pltpu.VMEM((wave_dev, degrees, rows), F32),
             pltpu.VMEM(halves.shape, BF16),
-            pltpu.VMEM((spec_rows, channels), F32),
+            pltpu.VMEM((cut + rest, channels), F32),
             pltpu.VMEM((wave_dev, degrees, LANES), F32),
             pltpu.SemaphoreType.DMA((4,)),
         ],
         compiler_params=params,
-    )(where, in_hbm(fields), in_hbm(legendre.transpose(1, 2, 0)), in_hbm(halves))
+    )(where, in_hbm(grid), in_hbm(legendre.transpose(1, 2, 0)), in_hbm(halves))
 
     acc_a = acc_a + exchange(send_a, 1, 1).astype(F32)
     acc_b = acc_b + exchange(send_b, 1, 1).astype(F32)
@@ -446,6 +448,7 @@
         and degrees == TILE
         and degrees <= waves
         and rows % TILE == 0
+        and longitudes // count % 2 == 0
         and 2 * rows * (degrees // 2 + 1) <= channels
         and channels == 2 * LANES
         and channels // count == TILE

time: 29.7 us -> 29.7 us (level)
  no operation moved by 1% of the time
where the time goes in v7:
time: 29.7 us; the launch traced here: 29.5 us
  starting transfers between devices  16 us (54%)
  waiting for transfers between devices  9.27 us (31%)
  Pallas kernels  3.08 us (10%)
  between operations  0.69 us (2%)
  other arithmetic  0.42 us (1%)
    ppermute x11, starting transfers between devices, exchange(): return lax.ppermute(array, 'lon', pairs)  16 us
    ppermute x11, waiting for transfers between devices, exchange(): return lax.ppermute(array, 'lon', pairs)  9.27 us
    pallas_call x1, Pallas kernels, sparse_shards(): pl.pallas_call(functools.partial(fourier_kernel, lon_count), out_shape=(j...  1.67 us
    pallas_call x1, Pallas kernels, sparse_shards(): pl.pallas_call(functools.partial(mixing_kernel, lon_count, wave_dev, samp...  1.16 us
  transfers between devices with their start and end apart: 11, of which 6 were waited for; matrix products, arithmetic and copies ran while one was open for 1% of the time, Pallas kernels for 0%

profile of v7, /device:TPU:0, one launch (start us, length us, event | category | flops | bytes accessed | tf_op | source)
XLA Modules:
  0.0 29.5 jit_solution(15766750230645062209)
XLA Ops:
  0.6 1.7 %shard_map.59 = (f32[264,256]{1,0:T(8,128)S(1)}, f32[216,256]{1,0:T(8,128)S(1)}, bf16[264,256]{1,0:T(8,128)(2,1)S(1)}, bf16[216,256]{1,0:T(8,128)(2,1)S(1)}) custom-call(s32[1]{0:T(128)} %bitcast.where_ref, bf16[2,576,256]{2,1,0:T(8,128)(2,1)} %bitcast.13, f32[6,8,24]{2,1,0:T(8,128)} %bitcast.15, bf16[384,128]{1,0:T(8,128)(2,1)} %bitcast.14), custom_call_target="tpu_custom_call" | custom-call | tf_op jit(solution)/shard_map/pallas_call | solution.py:366
  2.3 0.5 %collective-permute-start = (bf16[264,256]{1,0:T(8,128)(2,1)S(1)}, bf16[264,256]{1,0:T(8,128)(2,1)S(1)}, u32[]{:S(2)}, u32[]{:S(2)}) collective-permute-start(bf16[264,256]{1,0:T(8,128)(2,1)S(1)} %get-tuple-element.9), channel_id=1, source_target_pairs={{0,1},{1,0},{2,3},{3,2},{4,5},{5,4},{6,7},{7,6},{8,9},{9,8},{10,11... | collective-permute-start | bytes 405512 | tf_op jit(solution)/shard_map/ppermute | solution.py:358
  2.8 0.1 collective-permute-start.5
  2.9 0.9 %collective-permute-done = bf16[264,256]{1,0:T(8,128)(2,1)S(1)} collective-permute-done((bf16[264,256]{1,0:T(8,128)(2,1)S(1)}, bf16[264,256]{1,0:T(8,128)(2,1)S(1)}, u32[]{:S(2)}, u32[]{:S(2)}) %collective-permute-start) | collective-permute-done | bytes 135200 | tf_op jit(solution)/shard_map/ppermute | solution.py:358
  3.9 2.5 %collective-permute-start.1 = (bf16[264,256]{1,0:T(8,128)(2,1)S(1)}, bf16[264,256]{1,0:T(8,128)(2,1)S(1)}, u32[]{:S(2)}, u32[]{:S(2)}) collective-permute-start(bf16[264,256]{1,0:T(8,128)(2,1)S(1)} %fusion), channel_id=1, source_target_pairs={{0,3},{1,8},{2,11},{3,0},{4,13},{5,6},{6,5},{7,14},{8,1},{9,10},{1... | collective-permute-start | bytes 405512 | tf_op jit(solution)/shard_map/ppermute | solution.py:358
  6.3 0.0 collective-permute-done.5
  6.3 1.6 %collective-permute-start.6 = (bf16[216,256]{1,0:T(8,128)(2,1)S(1)}, bf16[216,256]{1,0:T(8,128)(2,1)S(1)}, u32[]{:S(2)}, u32[]{:S(2)}) collective-permute-start(bf16[216,256]{1,0:T(8,128)(2,1)S(1)} %fusion.2), channel_id=1, source_target_pairs={{0,5},{1,24},{2,27},{3,6},{4,29},{5,0},{6,3},{7,30},{8,17},{9,12},... | collective-permute-start | bytes 331784 | tf_op jit(solution)/shard_map/ppermute | solution.py:358
  7.9 1.1 %collective-permute-done.1 = bf16[264,256]{1,0:T(8,128)(2,1)S(1)} collective-permute-done((bf16[264,256]{1,0:T(8,128)(2,1)S(1)}, bf16[264,256]{1,0:T(8,128)(2,1)S(1)}, u32[]{:S(2)}, u32[]{:S(2)}) %collective-permute-start.1) | collective-permute-done | bytes 135200 | tf_op jit(solution)/shard_map/ppermute | solution.py:358
  9.1 2.2 %collective-permute-start.2 = (bf16[264,256]{1,0:T(8,128)(2,1)S(1)}, bf16[264,256]{1,0:T(8,128)(2,1)S(1)}, u32[]{:S(2)}, u32[]{:S(2)}) collective-permute-start(bf16[264,256]{1,0:T(8,128)(2,1)S(1)} %fusion.5), channel_id=1, source_target_pairs={{0,9},{1,2},{2,1},{3,10},{4,7},{5,12},{6,15},{7,4},{8,11},{9,0},{1... | collective-permute-start | bytes 405512 | tf_op jit(solution)/shard_map/ppermute | solution.py:358
  11.2 0.0 collective-permute-done.6
  11.3 3.3 %collective-permute-start.7 = (bf16[216,256]{1,0:T(8,128)(2,1)S(1)}, bf16[216,256]{1,0:T(8,128)(2,1)S(1)}, u32[]{:S(2)}, u32[]{:S(2)}) collective-permute-start(bf16[216,256]{1,0:T(8,128)(2,1)S(1)} %fusion.4), channel_id=1, source_target_pairs={{0,25},{1,4},{2,7},{3,26},{4,1},{5,28},{6,31},{7,2},{8,13},{9,16},... | collective-permute-start | bytes 331784 | tf_op jit(solution)/shard_map/ppermute | solution.py:358
  14.6 0.0 collective-permute-done.2
  14.6 0.1 fusion.1
  14.6 1.0 %collective-permute-start.3 = (bf16[264,256]{1,0:T(8,128)(2,1)S(1)}, bf16[264,256]{1,0:T(8,128)(2,1)S(1)}, u32[]{:S(2)}, u32[]{:S(2)}) collective-permute-start(bf16[264,256]{1,0:T(8,128)(2,1)S(1)} %fusion.1), channel_id=1, source_target_pairs={{0,5},{1,24},{2,27},{3,6},{4,29},{5,0},{6,3},{7,30},{8,17},{9,12},... | collective-permute-start | bytes 405512 | tf_op jit(solution)/shard_map/ppermute | solution.py:358
  15.7 1.8 %collective-permute-done.7 = bf16[216,256]{1,0:T(8,128)(2,1)S(1)} collective-permute-done((bf16[216,256]{1,0:T(8,128)(2,1)S(1)}, bf16[216,256]{1,0:T(8,128)(2,1)S(1)}, u32[]{:S(2)}, u32[]{:S(2)}) %collective-permute-start.7) | collective-permute-done | bytes 110624 | tf_op jit(solution)/shard_map/ppermute | solution.py:358
  17.4 0.1 fusion.3
  17.5 0.2 collective-permute-start.8
  17.7 1.4 %collective-permute-done.3 = bf16[264,256]{1,0:T(8,128)(2,1)S(1)} collective-permute-done((bf16[264,256]{1,0:T(8,128)(2,1)S(1)}, bf16[264,256]{1,0:T(8,128)(2,1)S(1)}, u32[]{:S(2)}, u32[]{:S(2)}) %collective-permute-start.3) | collective-permute-done | bytes 135200 | tf_op jit(solution)/shard_map/ppermute | solution.py:358
  19.1 0.1 fusion.7
  19.2 0.0 copy-start
  19.2 3.2 %collective-permute-start.4 = (bf16[264,256]{1,0:T(8,128)(2,1)S(1)}, bf16[264,256]{1,0:T(8,128)(2,1)S(1)}, u32[]{:S(2)}, u32[]{:S(2)}) collective-permute-start(bf16[264,256]{1,0:T(8,128)(2,1)S(1)} %get-tuple-element.16), channel_id=1, source_target_pairs={{0,25},{1,4},{2,7},{3,26},{4,1},{5,28},{6,31},{7,2},{8,13},{9,16},... | collective-permute-start | bytes 405512 | tf_op jit(solution)/shard_map/ppermute | solution.py:358
  22.4 0.0 collective-permute-done.8
  22.4 0.1 fusion.6
  22.5 1.2 %collective-permute-start.9 = (bf16[216,256]{1,0:T(8,128)(2,1)S(1)}, bf16[216,256]{1,0:T(8,128)(2,1)S(1)}, u32[]{:S(2)}, u32[]{:S(2)}) collective-permute-start(bf16[216,256]{1,0:T(8,128)(2,1)S(1)} %get-tuple-element.14), channel_id=1, source_target_pairs={{0,3},{1,8},{2,11},{3,0},{4,13},{5,6},{6,5},{7,14},{8,1},{9,10},{1... | collective-permute-start | bytes 331784 | tf_op jit(solution)/shard_map/ppermute | solution.py:358
  23.7 3.0 %collective-permute-done.9.second_got_ref = bf16[216,256]{1,0:T(8,128)(2,1)S(1)} collective-permute-done((bf16[216,256]{1,0:T(8,128)(2,1)S(1)}, bf16[216,256]{1,0:T(8,128)(2,1)S(1)}, u32[]{:S(2)}, u32[]{:S(2)}) %collective-permute-start.9) | collective-permute-done | bytes 110624 | tf_op jit(solution)/shard_map/ppermute | solution.py:358
  26.8 0.0 collective-permute-done.4.first_got_ref
  26.8 0.2 shard_map.60.mine_ref
  27.0 0.3 collective-permute-start.10
  27.3 1.1 %collective-permute-done.10.other_ref = bf16[160,256]{1,0:T(8,128)(2,1)S(1)} collective-permute-done((bf16[160,256]{1,0:T(8,128)(2,1)S(1)}, bf16[160,256]{1,0:T(8,128)(2,1)S(1)}, u32[]{:S(2)}, u32[]{:S(2)}) %collective-permute-start.10) | collective-permute-done | bytes 81952 | tf_op jit(solution)/shard_map/ppermute | solution.py:358
  28.4 0.0 copy-done
  28.4 1.2 %shard_map.61 = (bf16[384,128]{1,0:T(8,128)(2,1)}, f32[8,8,256]{2,1,0:T(8,128)}) custom-call(s32[1]{0:T(128)} %bitcast.where_ref, bf16[160,256]{1,0:T(8,128)(2,1)S(1)} %shard_map.60.mine_ref, bf16[160,256]{1,0:T(8,128)(2,1)S(1)} %collective-permute-done.10.other_ref, bf16[8,256,256]{2,1,0:T(8,128)(2,1)S(1)} %copy-done), custom_call_target="tpu_custom_call" | custom-call | tf_op jit(solution)/shard_map/pallas_call | solution.py:407
  (4 shorter events, 0.1 us)
Async XLA Ops:
  2.3 1.5 %collective-permute-start = (bf16[264,256]{1,0:T(8,128)(2,1)S(1)}, bf16[264,256]{1,0:T(8,128)(2,1)S(1)}, u32[]{:S(2)}, u32[]{:S(2)}) collective-permute-start(bf16[264,256]{1,0:T(8,128)(2,1)S(1)} %get-tuple-element.9), channel_id=1, source_target_pairs={{0,1},{1,0},{2,3},{3,2},{4,5},{5,4},{6,7},{7,6},{8,9},{9,8},{10,11... | collective-permute-start | bytes 405512 | tf_op jit(solution)/shard_map/ppermute | solution.py:358
  2.8 3.5 %collective-permute-start.5 = (bf16[216,256]{1,0:T(8,128)(2,1)S(1)}, bf16[216,256]{1,0:T(8,128)(2,1)S(1)}, u32[]{:S(2)}, u32[]{:S(2)}) collective-permute-start(bf16[216,256]{1,0:T(8,128)(2,1)S(1)} %get-tuple-element.11), channel_id=1, source_target_pairs={{0,1},{1,0},{2,3},{3,2},{4,5},{5,4},{6,7},{7,6},{8,9},{9,8},{10,11... | collective-permute-start | bytes 331784 | tf_op jit(solution)/shard_map/ppermute | solution.py:358
  3.9 5.1 %collective-permute-start.1 = (bf16[264,256]{1,0:T(8,128)(2,1)S(1)}, bf16[264,256]{1,0:T(8,128)(2,1)S(1)}, u32[]{:S(2)}, u32[]{:S(2)}) collective-permute-start(bf16[264,256]{1,0:T(8,128)(2,1)S(1)} %fusion), channel_id=1, source_target_pairs={{0,3},{1,8},{2,11},{3,0},{4,13},{5,6},{6,5},{7,14},{8,1},{9,10},{1... | collective-permute-start | bytes 405512 | tf_op jit(solution)/shard_map/ppermute | solution.py:358
  6.3 4.9 %collective-permute-start.6 = (bf16[216,256]{1,0:T(8,128)(2,1)S(1)}, bf16[216,256]{1,0:T(8,128)(2,1)S(1)}, u32[]{:S(2)}, u32[]{:S(2)}) collective-permute-start(bf16[216,256]{1,0:T(8,128)(2,1)S(1)} %fusion.2), channel_id=1, source_target_pairs={{0,5},{1,24},{2,27},{3,6},{4,29},{5,0},{6,3},{7,30},{8,17},{9,12},... | collective-permute-start | bytes 331784 | tf_op jit(solution)/shard_map/ppermute | solution.py:358
  9.1 5.5 %collective-permute-start.2 = (bf16[264,256]{1,0:T(8,128)(2,1)S(1)}, bf16[264,256]{1,0:T(8,128)(2,1)S(1)}, u32[]{:S(2)}, u32[]{:S(2)}) collective-permute-start(bf16[264,256]{1,0:T(8,128)(2,1)S(1)} %fusion.5), channel_id=1, source_target_pairs={{0,9},{1,2},{2,1},{3,10},{4,7},{5,12},{6,15},{7,4},{8,11},{9,0},{1... | collective-permute-start | bytes 405512 | tf_op jit(solution)/shard_map/ppermute | solution.py:358
  11.3 6.1 %collective-permute-start.7 = (bf16[216,256]{1,0:T(8,128)(2,1)S(1)}, bf16[216,256]{1,0:T(8,128)(2,1)S(1)}, u32[]{:S(2)}, u32[]{:S(2)}) collective-permute-start(bf16[216,256]{1,0:T(8,128)(2,1)S(1)} %fusion.4), channel_id=1, source_target_pairs={{0,25},{1,4},{2,7},{3,26},{4,1},{5,28},{6,31},{7,2},{8,13},{9,16},... | collective-permute-start | bytes 331784 | tf_op jit(solution)/shard_map/ppermute | solution.py:358
  14.6 4.5 %collective-permute-start.3 = (bf16[264,256]{1,0:T(8,128)(2,1)S(1)}, bf16[264,256]{1,0:T(8,128)(2,1)S(1)}, u32[]{:S(2)}, u32[]{:S(2)}) collective-permute-start(bf16[264,256]{1,0:T(8,128)(2,1)S(1)} %fusion.1), channel_id=1, source_target_pairs={{0,5},{1,24},{2,27},{3,6},{4,29},{5,0},{6,3},{7,30},{8,17},{9,12},... | collective-permute-start | bytes 405512 | tf_op jit(solution)/shard_map/ppermute | solution.py:358
  17.5 4.9 %collective-permute-start.8 = (bf16[216,256]{1,0:T(8,128)(2,1)S(1)}, bf16[216,256]{1,0:T(8,128)(2,1)S(1)}, u32[]{:S(2)}, u32[]{:S(2)}) collective-permute-start(bf16[216,256]{1,0:T(8,128)(2,1)S(1)} %fusion.3), channel_id=1, source_target_pairs={{0,9},{1,2},{2,1},{3,10},{4,7},{5,12},{6,15},{7,4},{8,11},{9,0},{1... | collective-permute-start | bytes 331784 | tf_op jit(solution)/shard_map/ppermute | solution.py:358
  19.2 9.1 %copy-start = (bf16[8,256,256]{2,1,0:T(8,128)(2,1)S(1)}, bf16[8,256,256]{2,1,0:T(8,128)(2,1)}, u32[]{:S(2)}) copy-start(bf16[8,256,256]{2,1,0:T(8,128)(2,1)} %mixing_ref.1) | copy-start | bytes 3145732
  19.2 7.5 %collective-permute-start.4 = (bf16[264,256]{1,0:T(8,128)(2,1)S(1)}, bf16[264,256]{1,0:T(8,128)(2,1)S(1)}, u32[]{:S(2)}, u32[]{:S(2)}) collective-permute-start(bf16[264,256]{1,0:T(8,128)(2,1)S(1)} %get-tuple-element.16), channel_id=1, source_target_pairs={{0,25},{1,4},{2,7},{3,26},{4,1},{5,28},{6,31},{7,2},{8,13},{9,16},... | collective-permute-start | bytes 405512 | tf_op jit(solution)/shard_map/ppermute | solution.py:358
  22.5 4.2 %collective-permute-start.9 = (bf16[216,256]{1,0:T(8,128)(2,1)S(1)}, bf16[216,256]{1,0:T(8,128)(2,1)S(1)}, u32[]{:S(2)}, u32[]{:S(2)}) collective-permute-start(bf16[216,256]{1,0:T(8,128)(2,1)S(1)} %get-tuple-element.14), channel_id=1, source_target_pairs={{0,3},{1,8},{2,11},{3,0},{4,13},{5,6},{6,5},{7,14},{8,1},{9,10},{1... | collective-permute-start | bytes 331784 | tf_op jit(solution)/shard_map/ppermute | solution.py:358
  27.0 1.3 %collective-permute-start.10 = (bf16[160,256]{1,0:T(8,128)(2,1)S(1)}, bf16[160,256]{1,0:T(8,128)(2,1)S(1)}, u32[]{:S(2)}, u32[]{:S(2)}) collective-permute-start(bf16[160,256]{1,0:T(8,128)(2,1)S(1)} %shard_map.60.mine_ref), channel_id=1, source_target_pairs={{0,1},{1,0},{2,3},{3,2},{4,5},{5,4},{6,7},{7,6},{8,9},{9,8},{10,11... | collective-permute-start | bytes 245768 | tf_op jit(solution)/shard_map/ppermute | solution.py:358

commit v8 on v7

--- a/solution.py
+++ b/solution.py
@@ -13,6 +13,7 @@
 TILE = 8
 LANES = 128
 VMEM_BYTES = 32 * 1024 * 1024
+CHAINS = 3
 
 
 def dense_shards(fields, legendre, mixing, cotangent):
@@ -145,17 +146,10 @@
     fields_ref,
     legendre_ref,
     cot_ref,
-    first_ref,
-    second_ref,
-    first_send_ref,
-    second_send_ref,
-    grid_ref,
-    values_ref,
-    cots_ref,
-    total_ref,
-    table_ref,
-    sems,
+    *refs,
 ):
+    keep_refs, send_refs = refs[:CHAINS], refs[CHAINS : 2 * CHAINS]
+    grid_ref, values_ref, cots_ref, total_ref, table_ref, sems = refs[2 * CHAINS :]
     channels = fields_ref.shape[2]
     wave_dev, degrees, rows = legendre_ref.shape
     cells = fields_ref.shape[1] // rows
@@ -196,9 +190,9 @@
     wave = wave.reshape(parts * TILE, width)
     wave_hi = wave.astype(BF16)
     wave_lo = (wave - wave_hi.astype(F32)).astype(BF16)
-    cut = first_ref.shape[0] // rows
-    kept = (parts - cut) * rows
-    rest = pl.ds(kept, second_ref.shape[0] - kept)
+    size = total_ref.shape[0] // CHAINS
+    packed = total_ref.shape[0] - spec_rows
+    rest = pl.ds(size - packed, packed)
 
     @pl.when(owns)
     def _():
@@ -206,13 +200,13 @@
             copy.wait()
         cots = cots_ref[...].astype(F32)
         real, imag = packed_tiles(wave_dev, index, cots, values_ref, table_ref)
-        second_ref[rest, :] = jnp.where(side == 0, real, imag)
-        total_ref[pl.ds(spec_rows, rest.size), :] = jnp.where(side == 0, imag, real)
+        keep_refs[-1][rest, :] = jnp.where(side == 0, real, imag)
+        total_ref[pl.ds(spec_rows, packed), :] = jnp.where(side == 0, imag, real)
 
     @pl.when(jnp.logical_not(owns))
     def _():
-        second_ref[rest, :] = jnp.zeros((rest.size, channels), F32)
-        total_ref[pl.ds(spec_rows, rest.size), :] = jnp.zeros((rest.size, channels), F32)
+        keep_refs[-1][rest, :] = jnp.zeros((packed, channels), F32)
+        total_ref[pl.ds(spec_rows, packed), :] = jnp.zeros((packed, channels), F32)
 
     for copy in copies:
         copy.wait()
@@ -222,27 +216,25 @@
         sums = sums + jnp.dot(wave_lo, grid, preferred_element_type=F32)
         for part in range(parts):
             tile = sums[part * TILE : (part + 1) * TILE]
+            at = part * rows + first
             if k == 0:
-                total_ref[pl.ds(part * rows + first, TILE), :] = tile
-            elif part < cut:
-                first_ref[pl.ds(part * rows + first, TILE), :] = tile
+                total_ref[pl.ds(at, TILE), :] = tile
             else:
-                second_ref[pl.ds((part - cut) * rows + first, TILE), :] = tile
+                keep_refs[at // size][pl.ds(at % size, TILE), :] = tile
         if k == 0 and first + TILE == rows:
-            first_send_ref[...] = total_ref[pl.ds(0, cut * rows), :].astype(BF16)
-            after = pl.ds(cut * rows, second_send_ref.shape[0])
-            second_send_ref[...] = total_ref[after, :].astype(BF16)
-
-
-def legendre_kernel(
-    rows, first_ref, first_got_ref, second_ref, second_got_ref, out_ref
-):
+            for chain, send_ref in enumerate(send_refs):
+                send_ref[...] = total_ref[pl.ds(chain * size, size), :].astype(BF16)
+
+
+def legendre_kernel(rows, *refs):
     degrees = TILE
     groups = degrees // 2 + 1
-    first = first_ref[...] + first_got_ref[...].astype(F32)
-    second = second_ref[...] + second_got_ref[...].astype(F32)
+    out_ref = refs[-1]
+    sums = [
+        refs[2 * chain][...] + refs[2 * chain + 1][...].astype(F32) for chain in range(CHAINS)
+    ]
     spec_rows = 2 * degrees * rows
-    spec = jnp.concatenate([first, second], axis=0)
+    spec = jnp.concatenate(sums, axis=0)
     packed = groups * 2 * degrees
     table = spec[spec_rows + packed :]
     spec_hi = spec[:spec_rows].astype(BF16).astype(F32)
@@ -357,50 +349,45 @@
         pairs = [(i, i ^ hops[side_of(i, lon_count)]) for i in range(lon_count)]
         return lax.ppermute(array, "lon", pairs)
 
-    cut = (parts // 2 + 3) * rows
-    rest = spec_rows - cut + packed_rows + 2 * TILE
+    size = (spec_rows + packed_rows + 2 * TILE) // CHAINS
     halves = cotangent.reshape(degrees, wave_dev, 2, samples, 2, LANES)
     halves = halves.transpose(0, 1, 2, 4, 3, 5).reshape(-1, LANES)
     grid = fields.reshape(samples, rows * cells, channels)
     far = pl.BlockSpec(memory_space=pltpu.HBM)
-    acc_a, acc_b, send_a, send_b = pl.pallas_call(
+    outs = pl.pallas_call(
         functools.partial(fourier_kernel, lon_count),
-        out_shape=(
-            jax.ShapeDtypeStruct((cut, channels), F32),
-            jax.ShapeDtypeStruct((rest, channels), F32),
-            jax.ShapeDtypeStruct((cut, channels), BF16),
-            jax.ShapeDtypeStruct((rest, channels), BF16),
-        ),
+        out_shape=(jax.ShapeDtypeStruct((size, channels), F32),) * CHAINS
+        + (jax.ShapeDtypeStruct((size, channels), BF16),) * CHAINS,
         in_specs=[scalar, far, far, far],
-        out_specs=(whole, whole, whole, whole),
+        out_specs=(whole,) * (2 * CHAINS),
         scratch_shapes=[
             pltpu.VMEM((samples, rows * cells, channels), BF16),
             pltpu.VMEM((wave_dev, degrees, rows), F32),
             pltpu.VMEM(halves.shape, BF16),
-            pltpu.VMEM((cut + rest, channels), F32),
+            pltpu.VMEM((CHAINS * size, channels), F32),
             pltpu.VMEM((wave_dev, degrees, LANES), F32),
             pltpu.SemaphoreType.DMA((4,)),
         ],
         compiler_params=params,
     )(where, in_hbm(grid), in_hbm(legendre.transpose(1, 2, 0)), in_hbm(halves))
 
-    acc_a = acc_a + exchange(send_a, 1, 1).astype(F32)
-    acc_b = acc_b + exchange(send_b, 1, 1).astype(F32)
-    orders_a, orders_b = hop_orders(lon_count)
-    for step, (hops_a, hops_b) in enumerate(zip(orders_a, orders_b)):
-        got_a = exchange(acc_a.astype(BF16), *hops_a)
-        got_b = exchange(acc_b.astype(BF16), *hops_b)
-        if step < len(orders_a) - 1:
-            acc_a = acc_a + got_a.astype(F32)
-            acc_b = acc_b + got_b.astype(F32)
+    accs = [
+        keep + exchange(send, 1, 1).astype(F32)
+        for keep, send in zip(outs[:CHAINS], outs[CHAINS:])
+    ]
+    for step, hops in enumerate(zip(*hop_orders(lon_count))):
+        gots = [exchange(acc.astype(BF16), *hop) for acc, hop in zip(accs, hops)]
+        if step < len(hop_orders(lon_count)[0]) - 1:
+            accs = [acc + got.astype(F32) for acc, got in zip(accs, gots)]
+    pairs = [array for pair in zip(accs, gots) for array in pair]
 
     mine = pl.pallas_call(
         functools.partial(legendre_kernel, rows),
         out_shape=jax.ShapeDtypeStruct((2 * packed_rows, channels), BF16),
-        in_specs=[whole] * 4,
+        in_specs=[whole] * (2 * CHAINS),
         out_specs=whole,
         compiler_params=params,
-    )(acc_a, got_a, acc_b, got_b)
+    )(*pairs)
     other = exchange(mine, 1, 1)
 
     block_rows = 2 * wave_dev * samples
@@ -432,7 +419,7 @@
     two = [hop for pair in zip(far, near) for hop in pair]
     chain_a = list(zip(one, two))
     chain_b = list(zip(one[half:] + one[:half][::-1], two[half:] + two[:half][::-1]))
-    return chain_a, chain_b
+    return chain_a, chain_b, list(zip(two, one))
 
 
 def few_waves(mesh, fields, legendre):
@@ -448,6 +435,7 @@
         and degrees == TILE
         and degrees <= waves
         and rows % TILE == 0
+        and (2 * degrees * (rows + degrees // 2 + 1) + 2 * TILE) % (2 * TILE * CHAINS) == 0
         and longitudes // count % 2 == 0
         and 2 * rows * (degrees // 2 + 1) <= channels
         and channels == 2 * LANES

time: 29.7 us -> 30.9 us (1.040)
  starting transfers between devices: 16 us -> 19 us
  waiting for transfers between devices: 9.27 us -> 7.52 us
    ppermute x11 -> x16, starting transfers between devices: 16 us -> 19 us  [exchange(): return lax.ppermute(array, 'lon', pairs)]
    ppermute x11 -> x16, waiting for transfers between devices: 9.27 us -> 7.52 us  [exchange(): return lax.ppermute(array, 'lon', pairs)]
  transfers between devices with their start and end apart: 11 -> 16, of which waited for: 6 -> 7; matrix products, arithmetic and copies ran while one was open for 1% -> 1% of each run, Pallas kernels for 0% -> 0%
where the time goes in v8:
time: 30.9 us; the launch traced here: 30.7 us
  starting transfers between devices  19 us (61%)
  waiting for transfers between devices  7.52 us (24%)
  Pallas kernels  3.08 us (10%)
  between operations  0.74 us (2%)
  other arithmetic  0.4 us (1%)
    ppermute x16, starting transfers between devices, exchange(): return lax.ppermute(array, 'lon', pairs)  19 us
    ppermute x16, waiting for transfers between devices, exchange(): return lax.ppermute(array, 'lon', pairs)  7.52 us
    pallas_call x1, Pallas kernels, sparse_shards(): pl.pallas_call(functools.partial(fourier_kernel, lon_count), out_shape=(j...  1.67 us
    pallas_call x1, Pallas kernels, sparse_shards(): pl.pallas_call(functools.partial(mixing_kernel, lon_count, wave_dev, samp...  1.16 us
  transfers between devices with their start and end apart: 16, of which 7 were waited for; matrix products, arithmetic and copies ran while one was open for 1% of the time, Pallas kernels for 0%

profile of v8, /device:TPU:0, one launch (start us, length us, event | category | flops | bytes accessed | tf_op | source)
XLA Modules:
  0.0 30.7 jit_solution(11229271649766117234)
XLA Ops:
  0.6 1.7 %shard_map.59 = (f32[160,256]{1,0:T(8,128)S(1)}, f32[160,256]{1,0:T(8,128)S(1)}, f32[160,256]{1,0:T(8,128)S(1)}, bf16[160,256]{1,0:T(8,128)(2,1)S(1)}, bf16[160,...) custom-call(s32[1]{0:T(128)} %bitcast.where_ref, bf16[2,576,256]{2,1,0:T(8,128)(2,1)} %bitcast.13, ...), custom_call_target="tpu_custom_call" | custom-call | tf_op jit(solution)/shard_map/pallas_call | solution.py:357
  2.3 0.5 %collective-permute-start = (bf16[160,256]{1,0:T(8,128)(2,1)S(1)}, bf16[160,256]{1,0:T(8,128)(2,1)S(1)}, u32[]{:S(2)}, u32[]{:S(2)}) collective-permute-start(bf16[160,256]{1,0:T(8,128)(2,1)S(1)} %get-tuple-element.11), channel_id=1, source_target_pairs={{0,1},{1,0},{2,3},{3,2},{4,5},{5,4},{6,7},{7,6},{8,9},{9,8},{10,11... | collective-permute-start | bytes 245768 | tf_op jit(solution)/shard_map/ppermute | solution.py:350
  2.8 0.1 collective-permute-start.5
  2.9 0.4 %collective-permute-start.10 = (bf16[160,256]{1,0:T(8,128)(2,1)S(1)}, bf16[160,256]{1,0:T(8,128)(2,1)S(1)}, u32[]{:S(2)}, u32[]{:S(2)}) collective-permute-start(bf16[160,256]{1,0:T(8,128)(2,1)S(1)} %get-tuple-element.15), channel_id=1, source_target_pairs={{0,1},{1,0},{2,3},{3,2},{4,5},{5,4},{6,7},{7,6},{8,9},{9,8},{10,11... | collective-permute-start | bytes 245768 | tf_op jit(solution)/shard_map/ppermute | solution.py:350
  3.3 0.4 %collective-permute-done = bf16[160,256]{1,0:T(8,128)(2,1)S(1)} collective-permute-done((bf16[160,256]{1,0:T(8,128)(2,1)S(1)}, bf16[160,256]{1,0:T(8,128)(2,1)S(1)}, u32[]{:S(2)}, u32[]{:S(2)}) %collective-permute-start) | collective-permute-done | bytes 81952 | tf_op jit(solution)/shard_map/ppermute | solution.py:350
  3.8 2.4 %collective-permute-start.1 = (bf16[160,256]{1,0:T(8,128)(2,1)S(1)}, bf16[160,256]{1,0:T(8,128)(2,1)S(1)}, u32[]{:S(2)}, u32[]{:S(2)}) collective-permute-start(bf16[160,256]{1,0:T(8,128)(2,1)S(1)} %fusion), channel_id=1, source_target_pairs={{0,3},{1,8},{2,11},{3,0},{4,13},{5,6},{6,5},{7,14},{8,1},{9,10},{1... | collective-permute-start | bytes 245768 | tf_op jit(solution)/shard_map/ppermute | solution.py:350
  6.2 0.0 collective-permute-done.5
  6.3 1.5 %collective-permute-start.6 = (bf16[160,256]{1,0:T(8,128)(2,1)S(1)}, bf16[160,256]{1,0:T(8,128)(2,1)S(1)}, u32[]{:S(2)}, u32[]{:S(2)}) collective-permute-start(bf16[160,256]{1,0:T(8,128)(2,1)S(1)} %fusion.2), channel_id=1, source_target_pairs={{0,5},{1,24},{2,27},{3,6},{4,29},{5,0},{6,3},{7,30},{8,17},{9,12},... | collective-permute-start | bytes 245768 | tf_op jit(solution)/shard_map/ppermute | solution.py:350
  7.8 0.0 collective-permute-done.10
  7.8 1.4 %collective-permute-start.11 = (bf16[160,256]{1,0:T(8,128)(2,1)S(1)}, bf16[160,256]{1,0:T(8,128)(2,1)S(1)}, u32[]{:S(2)}, u32[]{:S(2)}) collective-permute-start(bf16[160,256]{1,0:T(8,128)(2,1)S(1)} %fusion.4), channel_id=1, source_target_pairs={{0,9},{1,2},{2,1},{3,10},{4,7},{5,12},{6,15},{7,4},{8,11},{9,0},{1... | collective-permute-start | bytes 245768 | tf_op jit(solution)/shard_map/ppermute | solution.py:350
  9.3 1.0 %collective-permute-start.2 = (bf16[160,256]{1,0:T(8,128)(2,1)S(1)}, bf16[160,256]{1,0:T(8,128)(2,1)S(1)}, u32[]{:S(2)}, u32[]{:S(2)}) collective-permute-start(bf16[160,256]{1,0:T(8,128)(2,1)S(1)} %fusion.6), channel_id=1, source_target_pairs={{0,9},{1,2},{2,1},{3,10},{4,7},{5,12},{6,15},{7,4},{8,11},{9,0},{1... | collective-permute-start | bytes 245768 | tf_op jit(solution)/shard_map/ppermute | solution.py:350
  10.3 3.8 %collective-permute-start.7 = (bf16[160,256]{1,0:T(8,128)(2,1)S(1)}, bf16[160,256]{1,0:T(8,128)(2,1)S(1)}, u32[]{:S(2)}, u32[]{:S(2)}) collective-permute-start(bf16[160,256]{1,0:T(8,128)(2,1)S(1)} %fusion.7), channel_id=1, source_target_pairs={{0,25},{1,4},{2,7},{3,26},{4,1},{5,28},{6,31},{7,2},{8,13},{9,16},... | collective-permute-start | bytes 245768 | tf_op jit(solution)/shard_map/ppermute | solution.py:350
  14.2 0.1 collective-permute-start.12
  14.3 1.8 %collective-permute-start.3 = (bf16[160,256]{1,0:T(8,128)(2,1)S(1)}, bf16[160,256]{1,0:T(8,128)(2,1)S(1)}, u32[]{:S(2)}, u32[]{:S(2)}) collective-permute-start(bf16[160,256]{1,0:T(8,128)(2,1)S(1)} %fusion.1), channel_id=1, source_target_pairs={{0,5},{1,24},{2,27},{3,6},{4,29},{5,0},{6,3},{7,30},{8,17},{9,12},... | collective-permute-start | bytes 245768 | tf_op jit(solution)/shard_map/ppermute | solution.py:350
  16.1 0.3 collective-permute-done.7
  16.4 0.5 %collective-permute-start.8 = (bf16[160,256]{1,0:T(8,128)(2,1)S(1)}, bf16[160,256]{1,0:T(8,128)(2,1)S(1)}, u32[]{:S(2)}, u32[]{:S(2)}) collective-permute-start(bf16[160,256]{1,0:T(8,128)(2,1)S(1)} %fusion.3), channel_id=1, source_target_pairs={{0,9},{1,2},{2,1},{3,10},{4,7},{5,12},{6,15},{7,4},{8,11},{9,0},{1... | collective-permute-start | bytes 245768 | tf_op jit(solution)/shard_map/ppermute | solution.py:350
  17.0 1.1 %collective-permute-done.12 = bf16[160,256]{1,0:T(8,128)(2,1)S(1)} collective-permute-done((bf16[160,256]{1,0:T(8,128)(2,1)S(1)}, bf16[160,256]{1,0:T(8,128)(2,1)S(1)}, u32[]{:S(2)}, u32[]{:S(2)}) %collective-permute-start.12) | collective-permute-done | bytes 81952 | tf_op jit(solution)/shard_map/ppermute | solution.py:350
  18.1 2.1 %collective-permute-start.13 = (bf16[160,256]{1,0:T(8,128)(2,1)S(1)}, bf16[160,256]{1,0:T(8,128)(2,1)S(1)}, u32[]{:S(2)}, u32[]{:S(2)}) collective-permute-start(bf16[160,256]{1,0:T(8,128)(2,1)S(1)} %fusion.5), channel_id=1, source_target_pairs={{0,25},{1,4},{2,7},{3,26},{4,1},{5,28},{6,31},{7,2},{8,13},{9,16},... | collective-permute-start | bytes 245768 | tf_op jit(solution)/shard_map/ppermute | solution.py:350
  20.3 0.1 fusion.11
  20.3 0.0 copy-start
  20.3 1.6 %collective-permute-start.4 = (bf16[160,256]{1,0:T(8,128)(2,1)S(1)}, bf16[160,256]{1,0:T(8,128)(2,1)S(1)}, u32[]{:S(2)}, u32[]{:S(2)}) collective-permute-start(bf16[160,256]{1,0:T(8,128)(2,1)S(1)} %get-tuple-element.22), channel_id=1, source_target_pairs={{0,25},{1,4},{2,7},{3,26},{4,1},{5,28},{6,31},{7,2},{8,13},{9,16},... | collective-permute-start | bytes 245768 | tf_op jit(solution)/shard_map/ppermute | solution.py:350
  21.9 0.1 fusion.10
  22.0 0.4 %collective-permute-start.9 = (bf16[160,256]{1,0:T(8,128)(2,1)S(1)}, bf16[160,256]{1,0:T(8,128)(2,1)S(1)}, u32[]{:S(2)}, u32[]{:S(2)}) collective-permute-start(bf16[160,256]{1,0:T(8,128)(2,1)S(1)} %get-tuple-element.20), channel_id=1, source_target_pairs={{0,3},{1,8},{2,11},{3,0},{4,13},{5,6},{6,5},{7,14},{8,1},{9,10},{1... | collective-permute-start | bytes 245768 | tf_op jit(solution)/shard_map/ppermute | solution.py:350
  22.3 1.7 %collective-permute-done.13 = bf16[160,256]{1,0:T(8,128)(2,1)S(1)} collective-permute-done((bf16[160,256]{1,0:T(8,128)(2,1)S(1)}, bf16[160,256]{1,0:T(8,128)(2,1)S(1)}, u32[]{:S(2)}, u32[]{:S(2)}) %collective-permute-start.13) | collective-permute-done | bytes 81952 | tf_op jit(solution)/shard_map/ppermute | solution.py:350
  24.0 0.1 fusion.9
  24.0 1.0 %collective-permute-start.14 = (bf16[160,256]{1,0:T(8,128)(2,1)S(1)}, bf16[160,256]{1,0:T(8,128)(2,1)S(1)}, u32[]{:S(2)}, u32[]{:S(2)}) collective-permute-start(bf16[160,256]{1,0:T(8,128)(2,1)S(1)} %get-tuple-element.18), channel_id=1, source_target_pairs={{0,5},{1,24},{2,27},{3,6},{4,29},{5,0},{6,3},{7,30},{8,17},{9,12},... | collective-permute-start | bytes 245768 | tf_op jit(solution)/shard_map/ppermute | solution.py:350
  25.0 1.4 %collective-permute-done.4.refs_1_ = bf16[160,256]{1,0:T(8,128)(2,1)S(1)} collective-permute-done((bf16[160,256]{1,0:T(8,128)(2,1)S(1)}, bf16[160,256]{1,0:T(8,128)(2,1)S(1)}, u32[]{:S(2)}, u32[]{:S(2)}) %collective-permute-start.4) | collective-permute-done | bytes 81952 | tf_op jit(solution)/shard_map/ppermute | solution.py:350
  26.5 1.5 %collective-permute-done.14.refs_5_ = bf16[160,256]{1,0:T(8,128)(2,1)S(1)} collective-permute-done((bf16[160,256]{1,0:T(8,128)(2,1)S(1)}, bf16[160,256]{1,0:T(8,128)(2,1)S(1)}, u32[]{:S(2)}, u32[]{:S(2)}) %collective-permute-start.14) | collective-permute-done | bytes 81952 | tf_op jit(solution)/shard_map/ppermute | solution.py:350
  28.0 0.2 shard_map.60.mine_ref
  28.2 0.3 collective-permute-start.15
  28.5 1.1 %collective-permute-done.15.other_ref = bf16[160,256]{1,0:T(8,128)(2,1)S(1)} collective-permute-done((bf16[160,256]{1,0:T(8,128)(2,1)S(1)}, bf16[160,256]{1,0:T(8,128)(2,1)S(1)}, u32[]{:S(2)}, u32[]{:S(2)}) %collective-permute-start.15) | collective-permute-done | bytes 81952 | tf_op jit(solution)/shard_map/ppermute | solution.py:350
  29.6 1.2 %shard_map.61 = (bf16[384,128]{1,0:T(8,128)(2,1)}, f32[8,8,256]{2,1,0:T(8,128)}) custom-call(s32[1]{0:T(128)} %bitcast.where_ref, bf16[160,256]{1,0:T(8,128)(2,1)S(1)} %shard_map.60.mine_ref, bf16[160,256]{1,0:T(8,128)(2,1)S(1)} %collective-permute-done.15.other_ref, bf16[8,256,256]{2,1,0:T(8,128)(2,1)S(1)} %copy-done), custom_call_target="tpu_custom_call" | custom-call | tf_op jit(solution)/shard_map/pallas_call | solution.py:394
  (17 shorter events, 0.3 us)
Async XLA Ops:
  2.3 1.4 %collective-permute-start = (bf16[160,256]{1,0:T(8,128)(2,1)S(1)}, bf16[160,256]{1,0:T(8,128)(2,1)S(1)}, u32[]{:S(2)}, u32[]{:S(2)}) collective-permute-start(bf16[160,256]{1,0:T(8,128)(2,1)S(1)} %get-tuple-element.11), channel_id=1, source_target_pairs={{0,1},{1,0},{2,3},{3,2},{4,5},{5,4},{6,7},{7,6},{8,9},{9,8},{10,11... | collective-permute-start | bytes 245768 | tf_op jit(solution)/shard_map/ppermute | solution.py:350
  2.8 3.4 %collective-permute-start.5 = (bf16[160,256]{1,0:T(8,128)(2,1)S(1)}, bf16[160,256]{1,0:T(8,128)(2,1)S(1)}, u32[]{:S(2)}, u32[]{:S(2)}) collective-permute-start(bf16[160,256]{1,0:T(8,128)(2,1)S(1)} %get-tuple-element.13), channel_id=1, source_target_pairs={{0,1},{1,0},{2,3},{3,2},{4,5},{5,4},{6,7},{7,6},{8,9},{9,8},{10,11... | collective-permute-start | bytes 245768 | tf_op jit(solution)/shard_map/ppermute | solution.py:350
  2.9 4.9 %collective-permute-start.10 = (bf16[160,256]{1,0:T(8,128)(2,1)S(1)}, bf16[160,256]{1,0:T(8,128)(2,1)S(1)}, u32[]{:S(2)}, u32[]{:S(2)}) collective-permute-start(bf16[160,256]{1,0:T(8,128)(2,1)S(1)} %get-tuple-element.15), channel_id=1, source_target_pairs={{0,1},{1,0},{2,3},{3,2},{4,5},{5,4},{6,7},{7,6},{8,9},{9,8},{10,11... | collective-permute-start | bytes 245768 | tf_op jit(solution)/shard_map/ppermute | solution.py:350
  3.8 5.4 %collective-permute-start.1 = (bf16[160,256]{1,0:T(8,128)(2,1)S(1)}, bf16[160,256]{1,0:T(8,128)(2,1)S(1)}, u32[]{:S(2)}, u32[]{:S(2)}) collective-permute-start(bf16[160,256]{1,0:T(8,128)(2,1)S(1)} %fusion), channel_id=1, source_target_pairs={{0,3},{1,8},{2,11},{3,0},{4,13},{5,6},{6,5},{7,14},{8,1},{9,10},{1... | collective-permute-start | bytes 245768 | tf_op jit(solution)/shard_map/ppermute | solution.py:350
  6.3 4.0 %collective-permute-start.6 = (bf16[160,256]{1,0:T(8,128)(2,1)S(1)}, bf16[160,256]{1,0:T(8,128)(2,1)S(1)}, u32[]{:S(2)}, u32[]{:S(2)}) collective-permute-start(bf16[160,256]{1,0:T(8,128)(2,1)S(1)} %fusion.2), channel_id=1, source_target_pairs={{0,5},{1,24},{2,27},{3,6},{4,29},{5,0},{6,3},{7,30},{8,17},{9,12},... | collective-permute-start | bytes 245768 | tf_op jit(solution)/shard_map/ppermute | solution.py:350
  7.8 6.3 %collective-permute-start.11 = (bf16[160,256]{1,0:T(8,128)(2,1)S(1)}, bf16[160,256]{1,0:T(8,128)(2,1)S(1)}, u32[]{:S(2)}, u32[]{:S(2)}) collective-permute-start(bf16[160,256]{1,0:T(8,128)(2,1)S(1)} %fusion.4), channel_id=1, source_target_pairs={{0,9},{1,2},{2,1},{3,10},{4,7},{5,12},{6,15},{7,4},{8,11},{9,0},{1... | collective-permute-start | bytes 245768 | tf_op jit(solution)/shard_map/ppermute | solution.py:350
  9.3 5.0 %collective-permute-start.2 = (bf16[160,256]{1,0:T(8,128)(2,1)S(1)}, bf16[160,256]{1,0:T(8,128)(2,1)S(1)}, u32[]{:S(2)}, u32[]{:S(2)}) collective-permute-start(bf16[160,256]{1,0:T(8,128)(2,1)S(1)} %fusion.6), channel_id=1, source_target_pairs={{0,9},{1,2},{2,1},{3,10},{4,7},{5,12},{6,15},{7,4},{8,11},{9,0},{1... | collective-permute-start | bytes 245768 | tf_op jit(solution)/shard_map/ppermute | solution.py:350
  10.3 6.1 %collective-permute-start.7 = (bf16[160,256]{1,0:T(8,128)(2,1)S(1)}, bf16[160,256]{1,0:T(8,128)(2,1)S(1)}, u32[]{:S(2)}, u32[]{:S(2)}) collective-permute-start(bf16[160,256]{1,0:T(8,128)(2,1)S(1)} %fusion.7), channel_id=1, source_target_pairs={{0,25},{1,4},{2,7},{3,26},{4,1},{5,28},{6,31},{7,2},{8,13},{9,16},... | collective-permute-start | bytes 245768 | tf_op jit(solution)/shard_map/ppermute | solution.py:350
  14.2 3.9 %collective-permute-start.12 = (bf16[160,256]{1,0:T(8,128)(2,1)S(1)}, bf16[160,256]{1,0:T(8,128)(2,1)S(1)}, u32[]{:S(2)}, u32[]{:S(2)}) collective-permute-start(bf16[160,256]{1,0:T(8,128)(2,1)S(1)} %fusion.8), channel_id=1, source_target_pairs={{0,3},{1,8},{2,11},{3,0},{4,13},{5,6},{6,5},{7,14},{8,1},{9,10},{1... | collective-permute-start | bytes 245768 | tf_op jit(solution)/shard_map/ppermute | solution.py:350
  14.3 6.0 %collective-permute-start.3 = (bf16[160,256]{1,0:T(8,128)(2,1)S(1)}, bf16[160,256]{1,0:T(8,128)(2,1)S(1)}, u32[]{:S(2)}, u32[]{:S(2)}) collective-permute-start(bf16[160,256]{1,0:T(8,128)(2,1)S(1)} %fusion.1), channel_id=1, source_target_pairs={{0,5},{1,24},{2,27},{3,6},{4,29},{5,0},{6,3},{7,30},{8,17},{9,12},... | collective-permute-start | bytes 245768 | tf_op jit(solution)/shard_map/ppermute | solution.py:350
  16.4 5.5 %collective-permute-start.8 = (bf16[160,256]{1,0:T(8,128)(2,1)S(1)}, bf16[160,256]{1,0:T(8,128)(2,1)S(1)}, u32[]{:S(2)}, u32[]{:S(2)}) collective-permute-start(bf16[160,256]{1,0:T(8,128)(2,1)S(1)} %fusion.3), channel_id=1, source_target_pairs={{0,9},{1,2},{2,1},{3,10},{4,7},{5,12},{6,15},{7,4},{8,11},{9,0},{1... | collective-permute-start | bytes 245768 | tf_op jit(solution)/shard_map/ppermute | solution.py:350
  18.1 5.8 %collective-permute-start.13 = (bf16[160,256]{1,0:T(8,128)(2,1)S(1)}, bf16[160,256]{1,0:T(8,128)(2,1)S(1)}, u32[]{:S(2)}, u32[]{:S(2)}) collective-permute-start(bf16[160,256]{1,0:T(8,128)(2,1)S(1)} %fusion.5), channel_id=1, source_target_pairs={{0,25},{1,4},{2,7},{3,26},{4,1},{5,28},{6,31},{7,2},{8,13},{9,16},... | collective-permute-start | bytes 245768 | tf_op jit(solution)/shard_map/ppermute | solution.py:350
  20.3 9.2 %copy-start = (bf16[8,256,256]{2,1,0:T(8,128)(2,1)S(1)}, bf16[8,256,256]{2,1,0:T(8,128)(2,1)}, u32[]{:S(2)}) copy-start(bf16[8,256,256]{2,1,0:T(8,128)(2,1)} %mixing_ref.1) | copy-start | bytes 3145732
  20.3 6.1 %collective-permute-start.4 = (bf16[160,256]{1,0:T(8,128)(2,1)S(1)}, bf16[160,256]{1,0:T(8,128)(2,1)S(1)}, u32[]{:S(2)}, u32[]{:S(2)}) collective-permute-start(bf16[160,256]{1,0:T(8,128)(2,1)S(1)} %get-tuple-element.22), channel_id=1, source_target_pairs={{0,25},{1,4},{2,7},{3,26},{4,1},{5,28},{6,31},{7,2},{8,13},{9,16},... | collective-permute-start | bytes 245768 | tf_op jit(solution)/shard_map/ppermute | solution.py:350
  22.0 4.5 %collective-permute-start.9 = (bf16[160,256]{1,0:T(8,128)(2,1)S(1)}, bf16[160,256]{1,0:T(8,128)(2,1)S(1)}, u32[]{:S(2)}, u32[]{:S(2)}) collective-permute-start(bf16[160,256]{1,0:T(8,128)(2,1)S(1)} %get-tuple-element.20), channel_id=1, source_target_pairs={{0,3},{1,8},{2,11},{3,0},{4,13},{5,6},{6,5},{7,14},{8,1},{9,10},{1... | collective-permute-start | bytes 245768 | tf_op jit(solution)/shard_map/ppermute | solution.py:350
  24.0 3.9 %collective-permute-start.14 = (bf16[160,256]{1,0:T(8,128)(2,1)S(1)}, bf16[160,256]{1,0:T(8,128)(2,1)S(1)}, u32[]{:S(2)}, u32[]{:S(2)}) collective-permute-start(bf16[160,256]{1,0:T(8,128)(2,1)S(1)} %get-tuple-element.18), channel_id=1, source_target_pairs={{0,5},{1,24},{2,27},{3,6},{4,29},{5,0},{6,3},{7,30},{8,17},{9,12},... | collective-permute-start | bytes 245768 | tf_op jit(solution)/shard_map/ppermute | solution.py:350
  28.2 1.3 %collective-permute-start.15 = (bf16[160,256]{1,0:T(8,128)(2,1)S(1)}, bf16[160,256]{1,0:T(8,128)(2,1)S(1)}, u32[]{:S(2)}, u32[]{:S(2)}) collective-permute-start(bf16[160,256]{1,0:T(8,128)(2,1)S(1)} %shard_map.60.mine_ref), channel_id=1, source_target_pairs={{0,1},{1,0},{2,3},{3,2},{4,5},{5,4},{6,7},{7,6},{8,9},{9,8},{10,11... | collective-permute-start | bytes 245768 | tf_op jit(solution)/shard_map/ppermute | solution.py:350

commit v9 on v7

--- a/solution.py
+++ b/solution.py
@@ -250,7 +250,7 @@
     coefs = []
     for part in range(2):
         for group in range(groups):
-            basis = table[:, 2 * rows * group : 2 * rows * (group + 1)].astype(BF16)
+            basis = table[:, 2 * rows * group : 2 * rows * (group + 1)]
             partner = degrees - group if 0 < group < degrees - group else group
             low = (2 * group + part) * rows
             high = (2 * partner + part) * rows
@@ -258,9 +258,11 @@
                 jnp.concatenate([half[low : low + rows], half[high : high + rows]], axis=0)
                 for half in (spec_hi, spec_lo)
             )
-            sums = jnp.dot(basis, block.astype(BF16), preferred_element_type=F32)
-            more = jnp.dot(basis[:degrees], rest.astype(BF16), preferred_element_type=F32)
-            coefs.append(sums[:degrees] + sums[degrees:] + more)
+            last = jnp.concatenate([basis[:degrees], jnp.zeros_like(basis[:degrees])], axis=0)
+            both = jnp.concatenate([basis, last], axis=1).astype(BF16)
+            block = jnp.concatenate([block, rest], axis=0).astype(BF16)
+            sums = jnp.dot(both, block, preferred_element_type=F32)
+            coefs.append(sums[:degrees] + sums[degrees:])
     coefs.append(spec[spec_rows : spec_rows + packed])
     out_ref[...] = jnp.concatenate(coefs, axis=0).astype(BF16)
 

time: 29.7 us -> 29.7 us (level)
  no operation moved by 1% of the time
where the time goes in v9:
time: 29.7 us; the launch traced here: 29.5 us
  starting transfers between devices  16 us (54%)
  waiting for transfers between devices  9.27 us (31%)
  Pallas kernels  3.08 us (10%)
  between operations  0.69 us (2%)
  other arithmetic  0.42 us (1%)
    ppermute x11, starting transfers between devices, exchange(): return lax.ppermute(array, 'lon', pairs)  16 us
    ppermute x11, waiting for transfers between devices, exchange(): return lax.ppermute(array, 'lon', pairs)  9.27 us
    pallas_call x1, Pallas kernels, sparse_shards(): pl.pallas_call(functools.partial(fourier_kernel, lon_count), out_shape=(j...  1.67 us
    pallas_call x1, Pallas kernels, sparse_shards(): pl.pallas_call(functools.partial(mixing_kernel, lon_count, wave_dev, samp...  1.16 us
  transfers between devices with their start and end apart: 11, of which 6 were waited for; matrix products, arithmetic and copies ran while one was open for 1% of the time, Pallas kernels for 0%

profile of v9, /device:TPU:0, one launch (start us, length us, event | category | flops | bytes accessed | tf_op | source)
XLA Modules:
  0.0 29.5 jit_solution(1527160980385766021)
XLA Ops:
  0.6 1.7 %shard_map.59 = (f32[264,256]{1,0:T(8,128)S(1)}, f32[216,256]{1,0:T(8,128)S(1)}, bf16[264,256]{1,0:T(8,128)(2,1)S(1)}, bf16[216,256]{1,0:T(8,128)(2,1)S(1)}) custom-call(s32[1]{0:T(128)} %bitcast.where_ref, bf16[2,576,256]{2,1,0:T(8,128)(2,1)} %bitcast.13, f32[6,8,24]{2,1,0:T(8,128)} %bitcast.15, bf16[384,128]{1,0:T(8,128)(2,1)} %bitcast.14), custom_call_target="tpu_custom_call" | custom-call | tf_op jit(solution)/shard_map/pallas_call | solution.py:368
  2.3 0.5 %collective-permute-start = (bf16[264,256]{1,0:T(8,128)(2,1)S(1)}, bf16[264,256]{1,0:T(8,128)(2,1)S(1)}, u32[]{:S(2)}, u32[]{:S(2)}) collective-permute-start(bf16[264,256]{1,0:T(8,128)(2,1)S(1)} %get-tuple-element.9), channel_id=1, source_target_pairs={{0,1},{1,0},{2,3},{3,2},{4,5},{5,4},{6,7},{7,6},{8,9},{9,8},{10,11... | collective-permute-start | bytes 405512 | tf_op jit(solution)/shard_map/ppermute | solution.py:360
  2.8 0.1 collective-permute-start.5
  2.9 0.9 %collective-permute-done = bf16[264,256]{1,0:T(8,128)(2,1)S(1)} collective-permute-done((bf16[264,256]{1,0:T(8,128)(2,1)S(1)}, bf16[264,256]{1,0:T(8,128)(2,1)S(1)}, u32[]{:S(2)}, u32[]{:S(2)}) %collective-permute-start) | collective-permute-done | bytes 135200 | tf_op jit(solution)/shard_map/ppermute | solution.py:360
  3.9 2.5 %collective-permute-start.1 = (bf16[264,256]{1,0:T(8,128)(2,1)S(1)}, bf16[264,256]{1,0:T(8,128)(2,1)S(1)}, u32[]{:S(2)}, u32[]{:S(2)}) collective-permute-start(bf16[264,256]{1,0:T(8,128)(2,1)S(1)} %fusion), channel_id=1, source_target_pairs={{0,3},{1,8},{2,11},{3,0},{4,13},{5,6},{6,5},{7,14},{8,1},{9,10},{1... | collective-permute-start | bytes 405512 | tf_op jit(solution)/shard_map/ppermute | solution.py:360
  6.3 0.0 collective-permute-done.5
  6.3 1.6 %collective-permute-start.6 = (bf16[216,256]{1,0:T(8,128)(2,1)S(1)}, bf16[216,256]{1,0:T(8,128)(2,1)S(1)}, u32[]{:S(2)}, u32[]{:S(2)}) collective-permute-start(bf16[216,256]{1,0:T(8,128)(2,1)S(1)} %fusion.2), channel_id=1, source_target_pairs={{0,5},{1,24},{2,27},{3,6},{4,29},{5,0},{6,3},{7,30},{8,17},{9,12},... | collective-permute-start | bytes 331784 | tf_op jit(solution)/shard_map/ppermute | solution.py:360
  7.9 1.1 %collective-permute-done.1 = bf16[264,256]{1,0:T(8,128)(2,1)S(1)} collective-permute-done((bf16[264,256]{1,0:T(8,128)(2,1)S(1)}, bf16[264,256]{1,0:T(8,128)(2,1)S(1)}, u32[]{:S(2)}, u32[]{:S(2)}) %collective-permute-start.1) | collective-permute-done | bytes 135200 | tf_op jit(solution)/shard_map/ppermute | solution.py:360
  9.1 2.2 %collective-permute-start.2 = (bf16[264,256]{1,0:T(8,128)(2,1)S(1)}, bf16[264,256]{1,0:T(8,128)(2,1)S(1)}, u32[]{:S(2)}, u32[]{:S(2)}) collective-permute-start(bf16[264,256]{1,0:T(8,128)(2,1)S(1)} %fusion.5), channel_id=1, source_target_pairs={{0,9},{1,2},{2,1},{3,10},{4,7},{5,12},{6,15},{7,4},{8,11},{9,0},{1... | collective-permute-start | bytes 405512 | tf_op jit(solution)/shard_map/ppermute | solution.py:360
  11.2 0.0 collective-permute-done.6
  11.3 3.3 %collective-permute-start.7 = (bf16[216,256]{1,0:T(8,128)(2,1)S(1)}, bf16[216,256]{1,0:T(8,128)(2,1)S(1)}, u32[]{:S(2)}, u32[]{:S(2)}) collective-permute-start(bf16[216,256]{1,0:T(8,128)(2,1)S(1)} %fusion.4), channel_id=1, source_target_pairs={{0,25},{1,4},{2,7},{3,26},{4,1},{5,28},{6,31},{7,2},{8,13},{9,16},... | collective-permute-start | bytes 331784 | tf_op jit(solution)/shard_map/ppermute | solution.py:360
  14.6 0.0 collective-permute-done.2
  14.6 0.1 fusion.1
  14.6 1.0 %collective-permute-start.3 = (bf16[264,256]{1,0:T(8,128)(2,1)S(1)}, bf16[264,256]{1,0:T(8,128)(2,1)S(1)}, u32[]{:S(2)}, u32[]{:S(2)}) collective-permute-start(bf16[264,256]{1,0:T(8,128)(2,1)S(1)} %fusion.1), channel_id=1, source_target_pairs={{0,5},{1,24},{2,27},{3,6},{4,29},{5,0},{6,3},{7,30},{8,17},{9,12},... | collective-permute-start | bytes 405512 | tf_op jit(solution)/shard_map/ppermute | solution.py:360
  15.7 1.8 %collective-permute-done.7 = bf16[216,256]{1,0:T(8,128)(2,1)S(1)} collective-permute-done((bf16[216,256]{1,0:T(8,128)(2,1)S(1)}, bf16[216,256]{1,0:T(8,128)(2,1)S(1)}, u32[]{:S(2)}, u32[]{:S(2)}) %collective-permute-start.7) | collective-permute-done | bytes 110624 | tf_op jit(solution)/shard_map/ppermute | solution.py:360
  17.4 0.1 fusion.3
  17.5 0.2 collective-permute-start.8
  17.7 1.4 %collective-permute-done.3 = bf16[264,256]{1,0:T(8,128)(2,1)S(1)} collective-permute-done((bf16[264,256]{1,0:T(8,128)(2,1)S(1)}, bf16[264,256]{1,0:T(8,128)(2,1)S(1)}, u32[]{:S(2)}, u32[]{:S(2)}) %collective-permute-start.3) | collective-permute-done | bytes 135200 | tf_op jit(solution)/shard_map/ppermute | solution.py:360
  19.1 0.1 fusion.7
  19.2 0.0 copy-start
  19.2 3.2 %collective-permute-start.4 = (bf16[264,256]{1,0:T(8,128)(2,1)S(1)}, bf16[264,256]{1,0:T(8,128)(2,1)S(1)}, u32[]{:S(2)}, u32[]{:S(2)}) collective-permute-start(bf16[264,256]{1,0:T(8,128)(2,1)S(1)} %get-tuple-element.16), channel_id=1, source_target_pairs={{0,25},{1,4},{2,7},{3,26},{4,1},{5,28},{6,31},{7,2},{8,13},{9,16},... | collective-permute-start | bytes 405512 | tf_op jit(solution)/shard_map/ppermute | solution.py:360
  22.4 0.0 collective-permute-done.8
  22.4 0.1 fusion.6
  22.5 1.2 %collective-permute-start.9 = (bf16[216,256]{1,0:T(8,128)(2,1)S(1)}, bf16[216,256]{1,0:T(8,128)(2,1)S(1)}, u32[]{:S(2)}, u32[]{:S(2)}) collective-permute-start(bf16[216,256]{1,0:T(8,128)(2,1)S(1)} %get-tuple-element.14), channel_id=1, source_target_pairs={{0,3},{1,8},{2,11},{3,0},{4,13},{5,6},{6,5},{7,14},{8,1},{9,10},{1... | collective-permute-start | bytes 331784 | tf_op jit(solution)/shard_map/ppermute | solution.py:360
  23.7 3.0 %collective-permute-done.9.second_got_ref = bf16[216,256]{1,0:T(8,128)(2,1)S(1)} collective-permute-done((bf16[216,256]{1,0:T(8,128)(2,1)S(1)}, bf16[216,256]{1,0:T(8,128)(2,1)S(1)}, u32[]{:S(2)}, u32[]{:S(2)}) %collective-permute-start.9) | collective-permute-done | bytes 110624 | tf_op jit(solution)/shard_map/ppermute | solution.py:360
  26.8 0.0 collective-permute-done.4.first_got_ref
  26.8 0.2 shard_map.60.mine_ref
  27.0 0.3 collective-permute-start.10
  27.3 1.1 %collective-permute-done.10.other_ref = bf16[160,256]{1,0:T(8,128)(2,1)S(1)} collective-permute-done((bf16[160,256]{1,0:T(8,128)(2,1)S(1)}, bf16[160,256]{1,0:T(8,128)(2,1)S(1)}, u32[]{:S(2)}, u32[]{:S(2)}) %collective-permute-start.10) | collective-permute-done | bytes 81952 | tf_op jit(solution)/shard_map/ppermute | solution.py:360
  28.3 0.0 copy-done
  28.3 1.2 %shard_map.61 = (bf16[384,128]{1,0:T(8,128)(2,1)}, f32[8,8,256]{2,1,0:T(8,128)}) custom-call(s32[1]{0:T(128)} %bitcast.where_ref, bf16[160,256]{1,0:T(8,128)(2,1)S(1)} %shard_map.60.mine_ref, bf16[160,256]{1,0:T(8,128)(2,1)S(1)} %collective-permute-done.10.other_ref, bf16[8,256,256]{2,1,0:T(8,128)(2,1)S(1)} %copy-done), custom_call_target="tpu_custom_call" | custom-call | tf_op jit(solution)/shard_map/pallas_call | solution.py:409
  (4 shorter events, 0.1 us)
Async XLA Ops:
  2.3 1.5 %collective-permute-start = (bf16[264,256]{1,0:T(8,128)(2,1)S(1)}, bf16[264,256]{1,0:T(8,128)(2,1)S(1)}, u32[]{:S(2)}, u32[]{:S(2)}) collective-permute-start(bf16[264,256]{1,0:T(8,128)(2,1)S(1)} %get-tuple-element.9), channel_id=1, source_target_pairs={{0,1},{1,0},{2,3},{3,2},{4,5},{5,4},{6,7},{7,6},{8,9},{9,8},{10,11... | collective-permute-start | bytes 405512 | tf_op jit(solution)/shard_map/ppermute | solution.py:360
  2.8 3.5 %collective-permute-start.5 = (bf16[216,256]{1,0:T(8,128)(2,1)S(1)}, bf16[216,256]{1,0:T(8,128)(2,1)S(1)}, u32[]{:S(2)}, u32[]{:S(2)}) collective-permute-start(bf16[216,256]{1,0:T(8,128)(2,1)S(1)} %get-tuple-element.11), channel_id=1, source_target_pairs={{0,1},{1,0},{2,3},{3,2},{4,5},{5,4},{6,7},{7,6},{8,9},{9,8},{10,11... | collective-permute-start | bytes 331784 | tf_op jit(solution)/shard_map/ppermute | solution.py:360
  3.9 5.1 %collective-permute-start.1 = (bf16[264,256]{1,0:T(8,128)(2,1)S(1)}, bf16[264,256]{1,0:T(8,128)(2,1)S(1)}, u32[]{:S(2)}, u32[]{:S(2)}) collective-permute-start(bf16[264,256]{1,0:T(8,128)(2,1)S(1)} %fusion), channel_id=1, source_target_pairs={{0,3},{1,8},{2,11},{3,0},{4,13},{5,6},{6,5},{7,14},{8,1},{9,10},{1... | collective-permute-start | bytes 405512 | tf_op jit(solution)/shard_map/ppermute | solution.py:360
  6.3 4.9 %collective-permute-start.6 = (bf16[216,256]{1,0:T(8,128)(2,1)S(1)}, bf16[216,256]{1,0:T(8,128)(2,1)S(1)}, u32[]{:S(2)}, u32[]{:S(2)}) collective-permute-start(bf16[216,256]{1,0:T(8,128)(2,1)S(1)} %fusion.2), channel_id=1, source_target_pairs={{0,5},{1,24},{2,27},{3,6},{4,29},{5,0},{6,3},{7,30},{8,17},{9,12},... | collective-permute-start | bytes 331784 | tf_op jit(solution)/shard_map/ppermute | solution.py:360
  9.1 5.5 %collective-permute-start.2 = (bf16[264,256]{1,0:T(8,128)(2,1)S(1)}, bf16[264,256]{1,0:T(8,128)(2,1)S(1)}, u32[]{:S(2)}, u32[]{:S(2)}) collective-permute-start(bf16[264,256]{1,0:T(8,128)(2,1)S(1)} %fusion.5), channel_id=1, source_target_pairs={{0,9},{1,2},{2,1},{3,10},{4,7},{5,12},{6,15},{7,4},{8,11},{9,0},{1... | collective-permute-start | bytes 405512 | tf_op jit(solution)/shard_map/ppermute | solution.py:360
  11.3 6.1 %collective-permute-start.7 = (bf16[216,256]{1,0:T(8,128)(2,1)S(1)}, bf16[216,256]{1,0:T(8,128)(2,1)S(1)}, u32[]{:S(2)}, u32[]{:S(2)}) collective-permute-start(bf16[216,256]{1,0:T(8,128)(2,1)S(1)} %fusion.4), channel_id=1, source_target_pairs={{0,25},{1,4},{2,7},{3,26},{4,1},{5,28},{6,31},{7,2},{8,13},{9,16},... | collective-permute-start | bytes 331784 | tf_op jit(solution)/shard_map/ppermute | solution.py:360
  14.6 4.5 %collective-permute-start.3 = (bf16[264,256]{1,0:T(8,128)(2,1)S(1)}, bf16[264,256]{1,0:T(8,128)(2,1)S(1)}, u32[]{:S(2)}, u32[]{:S(2)}) collective-permute-start(bf16[264,256]{1,0:T(8,128)(2,1)S(1)} %fusion.1), channel_id=1, source_target_pairs={{0,5},{1,24},{2,27},{3,6},{4,29},{5,0},{6,3},{7,30},{8,17},{9,12},... | collective-permute-start | bytes 405512 | tf_op jit(solution)/shard_map/ppermute | solution.py:360
  17.5 4.9 %collective-permute-start.8 = (bf16[216,256]{1,0:T(8,128)(2,1)S(1)}, bf16[216,256]{1,0:T(8,128)(2,1)S(1)}, u32[]{:S(2)}, u32[]{:S(2)}) collective-permute-start(bf16[216,256]{1,0:T(8,128)(2,1)S(1)} %fusion.3), channel_id=1, source_target_pairs={{0,9},{1,2},{2,1},{3,10},{4,7},{5,12},{6,15},{7,4},{8,11},{9,0},{1... | collective-permute-start | bytes 331784 | tf_op jit(solution)/shard_map/ppermute | solution.py:360
  19.2 9.1 %copy-start = (bf16[8,256,256]{2,1,0:T(8,128)(2,1)S(1)}, bf16[8,256,256]{2,1,0:T(8,128)(2,1)}, u32[]{:S(2)}) copy-start(bf16[8,256,256]{2,1,0:T(8,128)(2,1)} %mixing_ref.1) | copy-start | bytes 3145732
  19.2 7.5 %collective-permute-start.4 = (bf16[264,256]{1,0:T(8,128)(2,1)S(1)}, bf16[264,256]{1,0:T(8,128)(2,1)S(1)}, u32[]{:S(2)}, u32[]{:S(2)}) collective-permute-start(bf16[264,256]{1,0:T(8,128)(2,1)S(1)} %get-tuple-element.16), channel_id=1, source_target_pairs={{0,25},{1,4},{2,7},{3,26},{4,1},{5,28},{6,31},{7,2},{8,13},{9,16},... | collective-permute-start | bytes 405512 | tf_op jit(solution)/shard_map/ppermute | solution.py:360
  22.5 4.2 %collective-permute-start.9 = (bf16[216,256]{1,0:T(8,128)(2,1)S(1)}, bf16[216,256]{1,0:T(8,128)(2,1)S(1)}, u32[]{:S(2)}, u32[]{:S(2)}) collective-permute-start(bf16[216,256]{1,0:T(8,128)(2,1)S(1)} %get-tuple-element.14), channel_id=1, source_target_pairs={{0,3},{1,8},{2,11},{3,0},{4,13},{5,6},{6,5},{7,14},{8,1},{9,10},{1... | collective-permute-start | bytes 331784 | tf_op jit(solution)/shard_map/ppermute | solution.py:360
  27.0 1.3 %collective-permute-start.10 = (bf16[160,256]{1,0:T(8,128)(2,1)S(1)}, bf16[160,256]{1,0:T(8,128)(2,1)S(1)}, u32[]{:S(2)}, u32[]{:S(2)}) collective-permute-start(bf16[160,256]{1,0:T(8,128)(2,1)S(1)} %shard_map.60.mine_ref), channel_id=1, source_target_pairs={{0,1},{1,0},{2,3},{3,2},{4,5},{5,4},{6,7},{7,6},{8,9},{9,8},{10,11... | collective-permute-start | bytes 245768 | tf_op jit(solution)/shard_map/ppermute | solution.py:360
